TPU v7x, 256 devices: a whole 4x4x8 slice. The times are simulated.
256 devices in a mesh: inp: 16 (over y, z_lo, core), hid: 16 (over z_hi, x).
Axes of the slice: x: 4, y: 4, z: 8 (z_hi: 4, z_lo: 2; z = z_hi * 2 + z_lo), core: 2. Of those that a mesh axis runs over, the one named last changes fastest.
Arguments:
- inputs: bfloat16 [128, 16384], P(None, 'inp'), may hold values from -6 to 6
- out_grad: bfloat16 [128, 16384], P(None, 'inp'), may hold values from -6 to 6
- gate_index: int32 [8192, 26624], P('inp', 'hid'), may hold values from 0 to 255, as said below
- up_index: int32 [8192, 26624], P('inp', 'hid'), may hold values from 0 to 255, as said below
- down_index: int32 [13312, 16384], P('hid', 'inp'), may hold values from 0 to 255, as said below
- gate_table: float32 [16, 26624], P(None, 'hid'), may hold values from -0.046875 to 0.046875
- up_table: float32 [16, 26624], P(None, 'hid'), may hold values from -0.046875 to 0.046875
- down_table: float32 [16, 16384], P(None, 'inp'), may hold values from -0.0390625 to 0.0390625
Outputs:
- input_grad: bfloat16 [128, 16384], P('hid', 'inp')
- gate_table_grad: float32 [16, 26624], P(None, 'hid')
- up_table_grad: float32 [16, 26624], P(None, 'hid')
- down_table_grad: float32 [16, 16384], P(None, 'inp')
Inputs may be any that keep to these rules, and one draw needn't show every extreme that they name: `gate_index`: each word holds two independent 4-bit table entries. `up_index`: each word holds two independent 4-bit table entries. `down_index`: each word holds two independent 4-bit table entries.
All inputs are finite; a program needn't handle non-finite values.
Results may differ from a plain program's by a relative error of at most 0.0072.
Values may be sent and summed in bfloat16 or wider, within the bound.
No kernel may reach another device: no remote copies, remote signals or barrier semaphores. Data moves between devices by JAX's collectives and lax.ppermute only.
A program may use at most 128 MiB of HBM per device.

v0:
```python
import functools

import jax
import jax.numpy as jnp
from jax import lax
from jax.experimental import pallas as pl
from jax.experimental.pallas import tpu as pltpu
from jax.sharding import PartitionSpec as P

BF16 = jnp.bfloat16
F32 = jnp.float32
I32 = jnp.int32
ENTRIES = 16
TOKENS = 128
LANES = 128
HBM_BYTES_PER_US = 3_000_000


def params(mib=60):
    return pltpu.CompilerParams(vmem_limit_bytes=mib * 1024 * 1024)


def cost(us):
    return pl.CostEstimate(flops=0, bytes_accessed=int(us * HBM_BYTES_PER_US), transcendentals=0)


def shape(dims, dtype):
    return jax.ShapeDtypeStruct(dims, dtype)


def whole(dims):
    return pl.BlockSpec(dims, lambda i: (0,) * len(dims))


def dot(a, b):
    return jnp.dot(a, b, preferred_element_type=F32)


def dot_nt(a, b):
    return lax.dot_general(a, b, (((1,), (1,)), ((), ())), preferred_element_type=F32)


def dot_tn(a, b):
    return lax.dot_general(a, b, (((0,), (0,)), ((), ())), preferred_element_type=F32)


def iotas(size):
    return lax.broadcasted_iota(I32, (size, size), 0), lax.broadcasted_iota(I32, (size, size), 1)


def one_hot(hits, dtype=BF16):
    return jnp.where(hits, 1.0, 0.0).astype(dtype)


def split_matrix(block):
    source, target = iotas(block)
    half = block // 2
    return one_hot(source == jnp.where(target < half, 2 * target, 2 * (target - half) + 1))


def merge_matrix(block, dtype=BF16):
    source, target = iotas(block)
    half = block // 2
    return one_hot(target == jnp.where(source < half, 2 * source, 2 * (source - half) + 1), dtype)


def token_of(row, core):
    return (((row >> 3) & 7) * 2 + (core ^ (row >> 6))) * 8 + (row & 7)


def to_rows(core):
    row, token = iotas(TOKENS)
    return one_hot(token == token_of(row, core))


def to_owners(core, hid):
    owned, row = iotas(TOKENS)
    bits = ((owned >> 6) & 1) | ((owned >> 4) & 2) | ((owned >> 2) & 4) | (owned & 8)
    return one_hot(token_of(row, core) == (bits ^ hid) * 8 + (owned & 7))


SCALAR = pl.BlockSpec(memory_space=pltpu.SMEM)
ANYWHERE = pl.BlockSpec(memory_space=pl.ANY)


def lookup(low, high, entry):
    at = entry & 7
    from_low = jnp.take_along_axis(low, at, axis=0, mode="promise_in_bounds")
    from_high = jnp.take_along_axis(high, at, axis=0, mode="promise_in_bounds")
    return jnp.where(entry >= 8, from_high, from_low)


def decode_block(index_ref, table_ref, weight_ref):
    words, cols = index_ref.shape

    def tile(j, carry):
        at = pl.ds(pl.multiple_of(j * LANES, LANES), LANES)
        low, high = table_ref[0:8, at], table_ref[8:16, at]
        for row in range(0, words, 16):
            even, odd = [], []
            for part in (row, row + 8):
                word = index_ref[part : part + 8, at]
                even.append(lookup(low, high, word & 15))
                odd.append(lookup(low, high, (word >> 4) & 15))
            weight_ref[row : row + 16, at] = jnp.concatenate(even, axis=0).astype(BF16)
            weight_ref[words + row : words + row + 16, at] = jnp.concatenate(odd, axis=0).astype(BF16)
        return carry

    lax.fori_loop(0, cols // LANES, tile, 0)


def forward_down_kernel(place_ref, grad_ref, index_ref, table_ref, near_ref, far_ref, ordered_ref, weight_ref):
    @pl.when(pl.program_id(0) == 0)
    def _():
        ordered_ref[...] = dot(to_rows(place_ref[0]), grad_ref[...]).astype(BF16)

    decode_block(index_ref, table_ref, weight_ref)
    hidden = dot_nt(ordered_ref[...], weight_ref[...])
    hidden = jnp.dot(
        hidden, merge_matrix(hidden.shape[1], F32), precision=lax.Precision.HIGHEST, preferred_element_type=F32
    )
    near_ref[...] = hidden[: TOKENS // 2]
    far_ref[...] = hidden[TOKENS // 2 :]


def forward_down(place, grad, index, table):
    words, width = index.shape
    block = 256
    half = TOKENS // 2
    return pl.pallas_call(
        forward_down_kernel,
        grid=(pl.cdiv(2 * words, block),),
        in_specs=[
            SCALAR,
            whole((TOKENS, width)),
            pl.BlockSpec((block // 2, width), lambda i: (i, 0)),
            whole((ENTRIES, width)),
        ],
        out_specs=[
            pl.BlockSpec((half, block), lambda i: (0, i)),
            pl.BlockSpec((half, block), lambda i: (0, i)),
            whole((TOKENS, width)),
        ],
        out_shape=[
            shape((half, 2 * words), F32),
            shape((half, 2 * words), F32),
            shape((TOKENS, width), BF16),
        ],
        scratch_shapes=[pltpu.VMEM((block, width), BF16)],
        compiler_params=params(),
        cost_estimate=cost(5),
        name="forward_down",
    )(place, grad, index, table)


def forward_up_kernel(first, *refs):
    if first:
        place_ref, x_ref, index_ref, table_ref, near_ref, far_ref, weight_ref, ordered_ref, sum_ref = refs
        x = dot(to_rows(place_ref[0]), x_ref[...]).astype(BF16)
        x = dot(x, split_matrix(x.shape[1])).astype(BF16)
        ordered_ref[...] = x
    else:
        x_ref, index_ref, table_ref, near_ref, far_ref, weight_ref, sum_ref = refs
        x = x_ref[...]
    decode_block(index_ref, table_ref, weight_ref)
    step = pl.program_id(0)

    @pl.when(step == 0)
    def _():
        sum_ref[...] = jnp.zeros_like(sum_ref)

    sum_ref[...] += dot(x, weight_ref[...])

    @pl.when(step == pl.num_programs(0) - 1)
    def _():
        near_ref[...] = sum_ref[: TOKENS // 2, :]
        far_ref[...] = sum_ref[TOKENS // 2 :, :]


def forward_up(place, x, index, table):
    first = place is not None
    words, width = index.shape
    block = 256
    half = TOKENS // 2
    by_column = pl.BlockSpec((TOKENS, block), lambda i: (0, i))
    return pl.pallas_call(
        functools.partial(forward_up_kernel, first),
        grid=(2 * words // block,),
        in_specs=[SCALAR] * first
        + [by_column, pl.BlockSpec((block // 2, width), lambda i: (i, 0)), whole((ENTRIES, width))],
        out_specs=[whole((half, width)), whole((half, width)), pl.BlockSpec((block, width), lambda i: (i, 0))]
        + [by_column] * first,
        out_shape=[shape((half, width), F32), shape((half, width), F32), shape((2 * words, width), BF16)]
        + [shape((TOKENS, 2 * words), BF16)] * first,
        scratch_shapes=[pltpu.VMEM((TOKENS, width), F32)],
        compiler_params=params(),
        cost_estimate=cost(5),
        name="forward_gate" if first else "forward_up",
    )(*([place] * first + [x, index, table]))


def entry_sums_kernel(x_ref, index_ref, after_ref, out_ref, entry_ref):
    words = index_ref.shape[0]
    half = 128
    for row in range(0, words, 16):
        word = index_ref[row : row + 16, :]
        at = row // half * 2 * half + row % half
        entry_ref[at : at + 16, :] = (word & 15).astype(jnp.int16)
        entry_ref[at + half : at + half + 16, :] = ((word >> 4) & 15).astype(jnp.int16)
    one, zero = jnp.ones((), BF16), jnp.zeros((), BF16)
    for entry in range(ENTRIES):
        chosen = jnp.where(entry_ref[...] == jnp.int16(entry), one, zero)
        out_ref[entry] = dot(x_ref[...], chosen).astype(BF16)


def entry_sums(x, index, after):
    words, width = index.shape
    wide = 256
    return pl.pallas_call(
        entry_sums_kernel,
        grid=(pl.cdiv(width, wide),),
        in_specs=[whole((TOKENS, 2 * words)), pl.BlockSpec((words, wide), lambda i: (0, i)), ANYWHERE],
        out_specs=pl.BlockSpec((ENTRIES, TOKENS, wide), lambda i: (0, 0, i)),
        out_shape=shape((ENTRIES, TOKENS, width), BF16),
        scratch_shapes=[pltpu.VMEM((2 * words, wide), jnp.int16)],
        compiler_params=params(),
        cost_estimate=cost(11),
        name="entry_sums",
    )(x, index, after)


def table_sums_kernel(near_ref, far_ref, sums_ref, after_ref, out_ref, grad_ref):
    entry = pl.program_id(0)

    @pl.when(entry == 0)
    def _():
        grad_ref[: TOKENS // 2, :] = near_ref[...].astype(F32)
        grad_ref[TOKENS // 2 :, :] = far_ref[...].astype(F32)

    product = sums_ref[0].astype(F32) * grad_ref[...]
    out_ref[pl.ds(entry, 1), :] = jnp.sum(product, axis=0, keepdims=True)


def table_sums(near, far, part, sums, after):
    width = sums.shape[2]
    half = TOKENS // 2
    return pl.pallas_call(
        table_sums_kernel,
        grid=(ENTRIES,),
        in_specs=[
            pl.BlockSpec((half, width), lambda i: (0, part)),
            pl.BlockSpec((half, width), lambda i: (0, part)),
            pl.BlockSpec((1, TOKENS, width), lambda i: (i, 0, 0)),
            ANYWHERE,
        ],
        out_specs=whole((ENTRIES, width)),
        out_shape=shape((ENTRIES, width), F32),
        scratch_shapes=[pltpu.VMEM((TOKENS, width), F32)],
        compiler_params=params(),
        cost_estimate=cost(3),
        name="table_sums",
    )(near, far, sums, after)


def down_bins_kernel(near_ref, far_ref, grad_ref, index_ref, out_ref, activ_ref, wgrad_ref):
    block = 128
    half = block // 2
    words, wide = index_ref.shape

    @pl.when(pl.program_id(0) == 0)
    def _():
        for at in range(0, 2 * words, block):
            cols = slice(at, at + block)
            activ = jnp.concatenate([near_ref[:, cols], far_ref[:, cols]], axis=0)
            activ_ref[:, cols] = dot(activ, split_matrix(block)).astype(BF16)

    wgrad_ref[...] = dot_tn(activ_ref[...], grad_ref[...]).astype(BF16)
    zero = jnp.zeros((), BF16)
    for lane in range(0, wide, LANES):
        cols = slice(lane, lane + LANES)

        def add_block(i, totals):
            part = [None] * ENTRIES
            for row in range(0, half, 16):
                word = index_ref[pl.ds(pl.multiple_of(i * half + row, 16), 16), cols]
                for entries, offset in ((word & 15, 0), ((word >> 4) & 15, half)):
                    entries = entries.astype(jnp.int16)
                    grads = wgrad_ref[pl.ds(pl.multiple_of(i * block + offset + row, 16), 16), cols]
                    for entry in range(ENTRIES):
                        chosen = jnp.where(entries == jnp.int16(entry), grads, zero)
                        part[entry] = chosen if part[entry] is None else part[entry] + chosen
            done = []
            for entry in range(ENTRIES):
                both = part[entry].astype(F32)
                done.append(totals[entry] + both[:8] + both[8:])
            return tuple(done)

        start = tuple(jnp.zeros((8, LANES), F32) for _ in range(ENTRIES))
        totals = lax.fori_loop(0, 2 * words // block, add_block, start)
        for entry in range(ENTRIES):
            out_ref[entry : entry + 1, cols] = jnp.sum(totals[entry], axis=0, keepdims=True)


def down_bins(near, far, part, grad, index):
    words, width = index.shape
    wide = 256
    half = TOKENS // 2
    return pl.pallas_call(
        down_bins_kernel,
        grid=(width // wide,),
        in_specs=[
            pl.BlockSpec((half, 2 * words), lambda i: (0, part)),
            pl.BlockSpec((half, 2 * words), lambda i: (0, part)),
            pl.BlockSpec((TOKENS, wide), lambda i: (0, i)),
            pl.BlockSpec((words, wide), lambda i: (0, i)),
        ],
        out_specs=pl.BlockSpec((ENTRIES, wide), lambda i: (0, i)),
        out_shape=shape((ENTRIES, width), F32),
        scratch_shapes=[pltpu.VMEM((TOKENS, 2 * words), BF16), pltpu.VMEM((2 * words, wide), BF16)],
        compiler_params=params(),
        cost_estimate=cost(10),
        name="down_bins",
    )(near, far, grad, index)


def input_grad_kernel(place_ref, gn_ref, gf_ref, un_ref, uf_ref, wg_ref, wu_ref, after_ref, out_ref):
    gate = jnp.concatenate([gn_ref[...], gf_ref[...]], axis=0)
    up = jnp.concatenate([un_ref[...], uf_ref[...]], axis=0)
    part = (dot_nt(gate, wg_ref[...]) + dot_nt(up, wu_ref[...])).astype(BF16)
    part = dot(to_owners(place_ref[0], place_ref[1]), part).astype(BF16)
    out_ref[...] = dot(part, merge_matrix(part.shape[1])).astype(BF16)


def input_grads(place, near, far, w_gate, w_up, after):
    rows, width = w_gate.shape
    block = 256
    half = TOKENS // 2
    gate = pl.BlockSpec((half, width), lambda i: (0, 0))
    up = pl.BlockSpec((half, width), lambda i: (0, 1))
    weights = pl.BlockSpec((block, width), lambda i: (i, 0))
    return pl.pallas_call(
        input_grad_kernel,
        grid=(rows // block,),
        in_specs=[SCALAR, gate, gate, up, up, weights, weights, ANYWHERE],
        out_specs=pl.BlockSpec((TOKENS, block), lambda i: (0, i)),
        out_shape=shape((TOKENS, rows), BF16),
        compiler_params=params(),
        cost_estimate=cost(3.5),
        name="input_grad",
    )(place, near, far, near, far, w_gate, w_up, after)


ONE_CORE = [[2 * place + core for place in range(8)] for core in range(2)]


def other_core(array):
    return lax.ppermute(array, "inp", [(i, i ^ 1) for i in range(16)])


def exchange_inp(pieces):
    return lax.all_to_all(pieces, "inp", 0, 0, tiled=True, axis_index_groups=ONE_CORE)


def copies(array, count):
    return jnp.broadcast_to(array[None], (count,) + array.shape)


def total(arrays):
    return functools.reduce(jnp.add, [a.astype(F32) for a in arrays])


def sum_inp(gate, up, core):
    own = jnp.where(core == 0, gate, up) + other_core(jnp.where(core == 0, up, gate))
    own = total(exchange_inp(copies(own.astype(BF16), 8)))
    other = other_core(own)
    return jnp.where(core == 0, own, other), jnp.where(core == 0, other, own)


def hid_step(bit, rows, bins):
    half = rows.shape[0] // 2
    coarse = lax.reduce_precision(bins, 8, 7)
    sent = jnp.concatenate([rows[half:].astype(BF16), coarse.astype(BF16), (bins - coarse).astype(BF16)], axis=0)
    back = lax.ppermute(sent, "hid", [(i, i ^ bit) for i in range(16)]).astype(F32)
    bins = bins + (back[half : half + ENTRIES] + back[half + ENTRIES :])
    return rows[:half].astype(F32) + back[:half], bins


def local_hidden(pre_gate, pre_up, hidden_grad):
    sig_gate = jax.nn.sigmoid(pre_gate)
    silu_gate = pre_gate * sig_gate
    activ = (silu_gate * pre_up).astype(BF16)
    gate_grad = (hidden_grad * pre_up * sig_gate * (1.0 + pre_gate * (1.0 - sig_gate))).astype(BF16)
    up_grad = (hidden_grad * silu_gate).astype(BF16)
    return activ, gate_grad, up_grad


def shards(inputs, out_grad, gate_index, up_index, down_index, gate_table, up_table, down_table):
    width = gate_index.shape[1]
    core = lax.axis_index("inp") % 2
    place = jnp.stack([core, lax.axis_index("hid")]).astype(I32)

    hidden_near, hidden_far, grad = forward_down(place, out_grad, down_index, down_table)
    hidden_back = other_core(hidden_far)
    gate_near, gate_far, w_gate, x = forward_up(place, inputs, gate_index, gate_table)
    gate_back = other_core(gate_far)
    up_near, up_far, w_up = forward_up(None, x, up_index, up_table)
    up_back = other_core(up_far)
    pair_sums = jnp.concatenate(
        [(gate_near + gate_back).astype(BF16), (up_near + up_back).astype(BF16), (hidden_near + hidden_back).astype(BF16)],
        axis=1,
    ).reshape(8, 8, 3 * width)
    pieces = exchange_inp(pair_sums)
    gate_sums = entry_sums(x, gate_index, pair_sums)
    pieces, gate_sums = lax.optimization_barrier((pieces, gate_sums))
    pre = total(pieces)
    activ, gate_grad, up_grad = local_hidden(pre[:, :width], pre[:, width : 2 * width], pre[:, 2 * width :])
    grads = copies(jnp.concatenate([gate_grad, up_grad, activ], axis=1), 8)
    near = exchange_inp(grads)
    up_sums = entry_sums(x, up_index, grads)
    near, up_sums = lax.optimization_barrier((near, up_sums))
    near = near.reshape(TOKENS // 2, 3 * width)
    activ_near, grad_near = near[:, 2 * width :], near[:, : 2 * width]
    activ_far, grad_far = other_core(activ_near), other_core(grad_near)

    down_sum = down_bins(activ_near, activ_far, 0, grad, down_index)
    part = input_grads(place, grad_near, grad_far, w_gate, w_up, down_sum)
    gate_part = table_sums(grad_near, grad_far, 0, gate_sums, part)
    part, down_sum = hid_step(1, part, down_sum)
    up_part = table_sums(grad_near, grad_far, 1, up_sums, part)
    gate_sum, up_sum = sum_inp(gate_part, up_part, core)
    for bit in (2, 4, 8):
        part, down_sum = hid_step(bit, part, down_sum)
    input_grad = part.astype(BF16)
    scale = 1.0 / TOKENS
    return input_grad, gate_sum * scale, up_sum * scale, down_sum * scale


def solution(mesh):
    in_specs = (
        P(None, "inp"),
        P(None, "inp"),
        P("inp", "hid"),
        P("inp", "hid"),
        P("hid", "inp"),
        P(None, "hid"),
        P(None, "hid"),
        P(None, "inp"),
    )
    out_specs = (P("hid", "inp"), P(None, "hid"), P(None, "hid"), P(None, "inp"))
    return jax.shard_map(shards, mesh=mesh, in_specs=in_specs, out_specs=out_specs, check_vma=False)
```

profile of v0, /device:TPU:1, one launch (start us, length us, event | category | flops | bytes accessed | tf_op | source)
XLA Modules:
  0.0 145.8 jit_solution(1746411330359054349)
XLA Ops:
  0.6 0.6 pad_add_fusion.refs_0_.place_ref
  1.2 10.5 %forward_down.1 = (f32[64,1664]{1,0:T(8,128)}, f32[64,1664]{1,0:T(8,128)}, bf16[128,1024]{1,0:T(8,128)(2,1)}) custom-call(s32[2]{0:T(128)} %pad_add_fusion.refs_0_.place_ref, bf16[128,1024]{1,0:T(8,128)(2,1)} %grad_ref.1, s32[832,1024]{1,0:T(8,128)} %index_ref.7, f32[16,1024]{1,0:T(8,128)} %table_ref.1), custom_call_target="tpu_custom_call" | custom-call | bytes 15000000 | tf_op jit(solution)/shard_map/forward_down/pallas_call | solution.py:130
  11.8 0.0 copy-start.7
  11.8 3.3 %collective-permute-start.2 = (f32[64,1664]{1,0:T(8,128)}, f32[64,1664]{1,0:T(8,128)S(1)}, u32[]{:S(2)}, u32[]{:S(2)}) collective-permute-start(f32[64,1664]{1,0:T(8,128)} %get-tuple-element.24), channel_id=1, source_target_pairs={{0,16},{16,0},{32,48},{48,32},{64,80},{80,64},{96,112},{112,96},{1... | collective-permute-start | bytes 1277960 | tf_op jit(solution)/shard_map/ppermute | solution.py:357
  15.1 8.1 %forward_gate.1 = (f32[64,1664]{1,0:T(8,128)}, f32[64,1664]{1,0:T(8,128)}, bf16[1024,1664]{1,0:T(8,128)(2,1)}, bf16[128,1024]{1,0:T(8,128)(2,1)}) custom-call(s32[2]{0:T(128)} %pad_add_fusion.refs_0_.place_ref, bf16[128,1024]{1,0:T(8,128)(2,1)} %refs_1_.2, s32[512,1664]{1,0:T(8,128)} %index_ref.5, f32[16,1664]{1,0:T(8,128)} %refs_3_.1), custom_call_target="tpu_custom_call" | custom-call | bytes 15000000 | tf_op jit(solution)/shard_map/forward_gate/pallas_call | solution.py:186
  23.2 0.1 collective-permute-start
  23.3 7.2 %forward_up.1 = (f32[64,1664]{1,0:T(8,128)}, f32[64,1664]{1,0:T(8,128)}, bf16[1024,1664]{1,0:T(8,128)(2,1)}) custom-call(bf16[128,1024]{1,0:T(8,128)(2,1)} %get-tuple-element.20.refs_0_.x_ref, s32[512,1664]{1,0:T(8,128)} %index_ref.6, f32[16,1664]{1,0:T(8,128)} %refs_2_.3), custom_call_target="tpu_custom_call" | custom-call | bytes 15000000 | tf_op jit(solution)/shard_map/forward_up/pallas_call | solution.py:186
  30.5 0.5 collective-permute-start.1
  31.0 0.0 collective-permute-done.2
  31.0 0.0 copy-done.7
  31.0 0.0 collective-permute-done
  31.0 0.0 copy-done.8
  31.1 1.5 %collective-permute-done.1 = f32[64,1664]{1,0:T(8,128)S(1)} collective-permute-done((f32[64,1664]{1,0:T(8,128)}, f32[64,1664]{1,0:T(8,128)S(1)}, u32[]{:S(2)}, u32[]{:S(2)}) %collective-permute-start.1) | collective-permute-done | bytes 426016 | tf_op jit(solution)/shard_map/ppermute | solution.py:357
  32.6 1.1 add_convert_fusion.1
  33.7 0.9 maximum_bitcast_fusion.after_ref
  34.5 3.8 %all-to-all-start = ((bf16[8,8,4992]{2,1,0:T(8,128)(2,1)}), bf16[8,8,4992]{2,1,0:T(8,128)(2,1)S(1)}, u32[]{:S(2)}, u32[]{:S(2)}) async-start(bf16[8,8,4992]{2,1,0:T(8,128)(2,1)} %maximum_bitcast_fusion.after_ref), calls=%async_computation | async-start | bytes 1277952 | tf_op jit(solution)/shard_map/all_to_all | solution.py:361
  38.3 11.6 %entry_sums.2.sums_ref = bf16[16,128,1664]{2,1,0:T(8,128)(2,1)} custom-call(bf16[128,1024]{1,0:T(8,128)(2,1)} %get-tuple-element.20.refs_0_.x_ref, s32[512,1664]{1,0:T(8,128)} %index_ref.5, bf16[8,8,4992]{2,1,0:T(8,128)(2,1)} %maximum_bitcast_fusion.after_ref), custom_call_target="tpu_custom_call" | custom-call | bytes 33000000 | tf_op jit(solution)/shard_map/entry_sums/pallas_call | solution.py:219
  50.0 0.0 all-to-all-done
  50.0 0.1 add_bitcast_fusion
  50.1 0.9 broadcast_in_dim.4.after_ref
  51.0 5.1 %all-to-all-start.1 = ((bf16[8,8,4992]{2,1,0:T(8,128)(2,1)}), bf16[8,8,4992]{2,1,0:T(8,128)(2,1)S(1)}, u32[]{:S(2)}, u32[]{:S(2)}) async-start(bf16[8,8,4992]{2,1,0:T(8,128)(2,1)} %broadcast_in_dim.4.after_ref), calls=%async_computation.1 | async-start | bytes 1277952 | tf_op jit(solution)/shard_map/all_to_all | solution.py:361
  56.1 11.6 %entry_sums.3.sums_ref = bf16[16,128,1664]{2,1,0:T(8,128)(2,1)} custom-call(bf16[128,1024]{1,0:T(8,128)(2,1)} %get-tuple-element.20.refs_0_.x_ref, s32[512,1664]{1,0:T(8,128)} %index_ref.6, bf16[8,8,4992]{2,1,0:T(8,128)(2,1)} %broadcast_in_dim.4.after_ref), custom_call_target="tpu_custom_call" | custom-call | bytes 33000000 | tf_op jit(solution)/shard_map/entry_sums/pallas_call | solution.py:219
  67.7 0.0 all-to-all-done.1
  67.7 0.0 copy-start.6
  67.8 1.3 collective-permute-start.4
  69.1 0.0 copy-start
  69.1 0.1 collective-permute-start.3
  69.2 0.9 collective-permute-done.4.far_ref
  70.2 0.0 copy-done.6
  70.2 0.7 copy-done.9
  70.8 11.4 %down_bins.1.after_ref = f32[16,1024]{1,0:T(8,128)} custom-call(bf16[64,1664]{1,0:T(8,128)(2,1)} %copy-done.6, bf16[64,1664]{1,0:T(8,128)(2,1)} %copy-done.9, bf16[128,1024]{1,0:T(8,128)(2,1)} %get-tuple-element.29.grad_ref, s32[832,1024]{1,0:T(8,128)} %index_ref.7), custom_call_target="tpu_custom_call" | custom-call | bytes 30000000 | tf_op jit(solution)/shard_map/down_bins/pallas_call | solution.py:308
  82.2 0.8 reduce-precision_convert_fusion.3
  83.1 0.0 collective-permute-done.3.gf_ref.uf_ref.far_ref
  83.1 0.0 copy-start.1
  83.1 0.0 copy-done
  83.1 0.8 copy-done.1
  83.9 6.6 %input_grad.1.after_ref = bf16[128,1024]{1,0:T(8,128)(2,1)} custom-call(s32[2]{0:T(128)} %pad_add_fusion.refs_0_.place_ref, bf16[64,3328]{1,0:T(8,128)(2,1)} %copy-done, bf16[64,3328]{1,0:T(8,128)(2,1)} %copy-done.1, bf16[64,3328]{1,0:T(8,128)(2,1)} %copy-done, bf16[64,3328]{1,0:T(8,128)(2,1)} %copy-done.1, bf16[1024,1664]{1,0:T(8,128)(2,1)} %get-tuple-element.27.wg_ref, ...), custom_call_target="tpu_custom_call" | custom-call | bytes 10500000 | tf_op jit(solution)/shard_map/input_grad/pallas_call | solution.py:341
  90.5 0.9 slice.109
  91.4 1.3 collective-permute-start.5
  92.7 10.4 %table_sums.2 = f32[16,1664]{1,0:T(8,128)} custom-call(bf16[64,3328]{1,0:T(8,128)(2,1)} %copy-done, bf16[64,3328]{1,0:T(8,128)(2,1)} %copy-done.1, bf16[16,128,1664]{2,1,0:T(8,128)(2,1)} %entry_sums.2.sums_ref, bf16[128,1024]{1,0:T(8,128)(2,1)} %input_grad.1.after_ref), custom_call_target="tpu_custom_call" | custom-call | bytes 9000000 | tf_op jit(solution)/shard_map/table_sums/pallas_call | solution.py:247
  103.1 0.0 collective-permute-done.5
  103.2 0.0 copy-done.4
  103.2 0.0 copy-start.3
  103.3 0.0 copy-start.5
  103.3 2.5 %collective-permute-start.6 = (bf16[64,1024]{1,0:T(8,128)(2,1)S(1)}, bf16[64,1024]{1,0:T(8,128)(2,1)S(1)}, u32[]{:S(2)}, u32[]{:S(2)}) collective-permute-start(bf16[64,1024]{1,0:T(8,128)(2,1)S(1)} %pad_maximum_fusion.1), channel_id=1, source_target_pairs={{0,2},{1,3},{2,0},{3,1},{4,6},{5,7},{6,4},{7,5},{8,10},{9,11},{10,... | collective-permute-start | bytes 393224 | tf_op jit(solution)/shard_map/ppermute | solution.py:383
  105.8 10.4 %table_sums.3 = f32[16,1664]{1,0:T(8,128)} custom-call(bf16[64,3328]{1,0:T(8,128)(2,1)} %copy-done, bf16[64,3328]{1,0:T(8,128)(2,1)} %copy-done.1, bf16[16,128,1664]{2,1,0:T(8,128)(2,1)} %entry_sums.3.sums_ref, f32[64,1024]{1,0:T(8,128)} %copy-done.3), custom_call_target="tpu_custom_call" | custom-call | bytes 9000000 | tf_op jit(solution)/shard_map/table_sums/pallas_call | solution.py:247
  116.3 1.9 %collective-permute-start.9 = (f32[16,1664]{1,0:T(8,128)S(1)}, f32[16,1664]{1,0:T(8,128)S(1)}, u32[]{:S(2)}, u32[]{:S(2)}) collective-permute-start(f32[16,1664]{1,0:T(8,128)S(1)} %broadcast_select_fusion), channel_id=1, source_target_pairs={{0,16},{16,0},{32,48},{48,32},{64,80},{80,64},{96,112},{112,96},{1... | collective-permute-start | bytes 319496 | tf_op jit(solution)/shard_map/ppermute | solution.py:357
  118.2 0.0 collective-permute-done.6
  118.2 0.9 slice_add_fusion.1
  119.2 3.1 %collective-permute-start.7 = (bf16[48,1024]{1,0:T(8,128)(2,1)S(1)}, bf16[48,1024]{1,0:T(8,128)(2,1)S(1)}, u32[]{:S(2)}, u32[]{:S(2)}) collective-permute-start(bf16[48,1024]{1,0:T(8,128)(2,1)S(1)} %pad_maximum_fusion.2), channel_id=1, source_target_pairs={{0,4},{1,5},{2,6},{3,7},{4,0},{5,1},{6,2},{7,3},{8,12},{9,13},{10,... | collective-permute-start | bytes 294920 | tf_op jit(solution)/shard_map/ppermute | solution.py:383
  122.3 0.0 collective-permute-done.9
  122.3 0.9 add_convert_fusion.3
  123.2 0.8 broadcast_in_dim.5
  124.0 5.4 %all-to-all-start.2 = ((bf16[8,16,1664]{2,1,0:T(8,128)(2,1)}), bf16[8,16,1664]{2,1,0:T(8,128)(2,1)S(1)}, u32[]{:S(2)}, u32[]{:S(2)}) async-start(bf16[8,16,1664]{2,1,0:T(8,128)(2,1)} %broadcast_in_dim.5), calls=%async_computation.2 | async-start | bytes 851968 | tf_op jit(solution)/shard_map/all_to_all | solution.py:361
  129.4 0.0 collective-permute-done.7
  129.5 4.3 %collective-permute-start.8 = (bf16[40,1024]{1,0:T(8,128)(2,1)S(1)}, bf16[40,1024]{1,0:T(8,128)(2,1)S(1)}, u32[]{:S(2)}, u32[]{:S(2)}) collective-permute-start(bf16[40,1024]{1,0:T(8,128)(2,1)S(1)} %pad_maximum_fusion.3), channel_id=1, source_target_pairs={{0,8},{1,9},{2,10},{3,11},{4,12},{5,13},{6,14},{7,15},{8,0},{9,1},... | collective-permute-start | bytes 245768 | tf_op jit(solution)/shard_map/ppermute | solution.py:383
  133.8 9.1 %collective-permute-done.8 = bf16[40,1024]{1,0:T(8,128)(2,1)S(1)} collective-permute-done((bf16[40,1024]{1,0:T(8,128)(2,1)S(1)}, bf16[40,1024]{1,0:T(8,128)(2,1)S(1)}, u32[]{:S(2)}, u32[]{:S(2)}) %collective-permute-start.8) | collective-permute-done | bytes 81952 | tf_op jit(solution)/shard_map/ppermute | solution.py:383
  142.9 0.6 fusion.5
  143.6 0.0 all-to-all-done.2
  143.6 0.1 add_bitcast_fusion.1
  143.6 0.5 collective-permute-start.10
  144.1 0.6 fusion.10
  144.7 0.3 collective-permute-done.10
  145.1 0.8 select_multiply_fusion
  (32 shorter events, 0.5 us)
Async XLA Ops:
  11.8 19.2 %copy-start.7 = (f32[64,1664]{1,0:T(8,128)S(1)}, f32[64,1664]{1,0:T(8,128)}, u32[]{:S(2)}) copy-start(f32[64,1664]{1,0:T(8,128)} %get-tuple-element.23) | copy-start | bytes 1277956
  11.8 19.2 %collective-permute-start.2 = (f32[64,1664]{1,0:T(8,128)}, f32[64,1664]{1,0:T(8,128)S(1)}, u32[]{:S(2)}, u32[]{:S(2)}) collective-permute-start(f32[64,1664]{1,0:T(8,128)} %get-tuple-element.24), channel_id=1, source_target_pairs={{0,16},{16,0},{32,48},{48,32},{64,80},{80,64},{96,112},{112,96},{1... | collective-permute-start | bytes 1277960 | tf_op jit(solution)/shard_map/ppermute | solution.py:357
  23.2 7.9 %copy-start.8 = (f32[64,1664]{1,0:T(8,128)S(1)}, f32[64,1664]{1,0:T(8,128)}, u32[]{:S(2)}) copy-start(f32[64,1664]{1,0:T(8,128)} %get-tuple-element.18) | copy-start | bytes 1277956
  23.2 7.8 %collective-permute-start = (f32[64,1664]{1,0:T(8,128)}, f32[64,1664]{1,0:T(8,128)S(1)}, u32[]{:S(2)}, u32[]{:S(2)}) collective-permute-start(f32[64,1664]{1,0:T(8,128)} %get-tuple-element.19), channel_id=1, source_target_pairs={{0,16},{16,0},{32,48},{48,32},{64,80},{80,64},{96,112},{112,96},{1... | collective-permute-start | bytes 1277960 | tf_op jit(solution)/shard_map/ppermute | solution.py:357
  30.5 2.1 %collective-permute-start.1 = (f32[64,1664]{1,0:T(8,128)}, f32[64,1664]{1,0:T(8,128)S(1)}, u32[]{:S(2)}, u32[]{:S(2)}) collective-permute-start(f32[64,1664]{1,0:T(8,128)} %get-tuple-element.22), channel_id=1, source_target_pairs={{0,16},{16,0},{32,48},{48,32},{64,80},{80,64},{96,112},{112,96},{1... | collective-permute-start | bytes 1277960 | tf_op jit(solution)/shard_map/ppermute | solution.py:357
  34.5 15.4 %all-to-all-start = ((bf16[8,8,4992]{2,1,0:T(8,128)(2,1)}), bf16[8,8,4992]{2,1,0:T(8,128)(2,1)S(1)}, u32[]{:S(2)}, u32[]{:S(2)}) async-start(bf16[8,8,4992]{2,1,0:T(8,128)(2,1)} %maximum_bitcast_fusion.after_ref), calls=%async_computation | async-start | bytes 1277952 | tf_op jit(solution)/shard_map/all_to_all | solution.py:361
  51.0 16.7 %all-to-all-start.1 = ((bf16[8,8,4992]{2,1,0:T(8,128)(2,1)}), bf16[8,8,4992]{2,1,0:T(8,128)(2,1)S(1)}, u32[]{:S(2)}, u32[]{:S(2)}) async-start(bf16[8,8,4992]{2,1,0:T(8,128)(2,1)} %broadcast_in_dim.4.after_ref), calls=%async_computation.1 | async-start | bytes 1277952 | tf_op jit(solution)/shard_map/all_to_all | solution.py:361
  67.7 2.4 %copy-start.6 = (bf16[64,1664]{1,0:T(8,128)(2,1)}, bf16[64,1664]{1,0:T(8,128)(2,1)S(1)}, u32[]{:S(2)}) copy-start(bf16[64,1664]{1,0:T(8,128)(2,1)S(1)} %slice.107.near_ref) | copy-start | bytes 638980
  67.8 2.4 %collective-permute-start.4 = (bf16[64,1664]{1,0:T(8,128)(2,1)S(1)}, bf16[64,1664]{1,0:T(8,128)(2,1)S(1)}, u32[]{:S(2)}, u32[]{:S(2)}) collective-permute-start(bf16[64,1664]{1,0:T(8,128)(2,1)S(1)} %slice.107.near_ref), channel_id=1, source_target_pairs={{0,16},{16,0},{32,48},{48,32},{64,80},{80,64},{96,112},{112,96},{1... | collective-permute-start | bytes 638984 | tf_op jit(solution)/shard_map/ppermute | solution.py:357
  69.1 14.0 %copy-start = (bf16[64,3328]{1,0:T(8,128)(2,1)}, bf16[64,3328]{1,0:T(8,128)(2,1)S(1)}, u32[]{:S(2)}) copy-start(bf16[64,3328]{1,0:T(8,128)(2,1)S(1)} %slice.106.gn_ref.un_ref.near_ref) | copy-start | bytes 1277956
  69.1 14.0 %collective-permute-start.3 = (bf16[64,3328]{1,0:T(8,128)(2,1)S(1)}, bf16[64,3328]{1,0:T(8,128)(2,1)S(1)}, u32[]{:S(2)}, u32[]{:S(2)}) collective-permute-start(bf16[64,3328]{1,0:T(8,128)(2,1)S(1)} %slice.106.gn_ref.un_ref.near_ref), channel_id=1, source_target_pairs={{0,16},{16,0},{32,48},{48,32},{64,80},{80,64},{96,112},{112,96},{1... | collective-permute-start | bytes 1277960 | tf_op jit(solution)/shard_map/ppermute | solution.py:357
  70.2 0.7 copy-start.9
  83.1 0.8 copy-start.1
  91.4 11.7 %collective-permute-start.5 = (bf16[96,1024]{1,0:T(8,128)(2,1)S(1)}, bf16[96,1024]{1,0:T(8,128)(2,1)S(1)}, u32[]{:S(2)}, u32[]{:S(2)}) collective-permute-start(bf16[96,1024]{1,0:T(8,128)(2,1)S(1)} %pad_maximum_fusion), channel_id=1, source_target_pairs={{0,1},{1,0},{2,3},{3,2},{4,5},{5,4},{6,7},{7,6},{8,9},{9,8},{10,11... | collective-permute-start | bytes 589832 | tf_op jit(solution)/shard_map/ppermute | solution.py:383
  92.7 10.5 %copy-start.2 = (bf16[128,1024]{1,0:T(8,128)(2,1)S(1)}, bf16[128,1024]{1,0:T(8,128)(2,1)}, u32[]{:S(2)}) copy-start(bf16[128,1024]{1,0:T(8,128)(2,1)} %input_grad.1.after_ref) | copy-start | bytes 786436
  92.7 10.5 %copy-start.4 = (f32[16,1024]{1,0:T(8,128)S(1)}, f32[16,1024]{1,0:T(8,128)}, u32[]{:S(2)}) copy-start(f32[16,1024]{1,0:T(8,128)} %down_bins.1.after_ref) | copy-start | bytes 196612
  103.2 2.6 %copy-start.3 = (f32[64,1024]{1,0:T(8,128)}, f32[64,1024]{1,0:T(8,128)S(1)}, u32[]{:S(2)}) copy-start(f32[64,1024]{1,0:T(8,128)S(1)} %slice_add_fusion.after_ref) | copy-start | bytes 786436
  103.3 12.9 %copy-start.5 = (f32[16,1664]{1,0:T(8,128)S(1)}, f32[16,1664]{1,0:T(8,128)}, u32[]{:S(2)}) copy-start(f32[16,1664]{1,0:T(8,128)} %table_sums.2) | copy-start | bytes 319492
  103.3 14.9 %collective-permute-start.6 = (bf16[64,1024]{1,0:T(8,128)(2,1)S(1)}, bf16[64,1024]{1,0:T(8,128)(2,1)S(1)}, u32[]{:S(2)}, u32[]{:S(2)}) collective-permute-start(bf16[64,1024]{1,0:T(8,128)(2,1)S(1)} %pad_maximum_fusion.1), channel_id=1, source_target_pairs={{0,2},{1,3},{2,0},{3,1},{4,6},{5,7},{6,4},{7,5},{8,10},{9,11},{10,... | collective-permute-start | bytes 393224 | tf_op jit(solution)/shard_map/ppermute | solution.py:383
  116.3 6.0 %collective-permute-start.9 = (f32[16,1664]{1,0:T(8,128)S(1)}, f32[16,1664]{1,0:T(8,128)S(1)}, u32[]{:S(2)}, u32[]{:S(2)}) collective-permute-start(f32[16,1664]{1,0:T(8,128)S(1)} %broadcast_select_fusion), channel_id=1, source_target_pairs={{0,16},{16,0},{32,48},{48,32},{64,80},{80,64},{96,112},{112,96},{1... | collective-permute-start | bytes 319496 | tf_op jit(solution)/shard_map/ppermute | solution.py:357
  119.2 10.2 %collective-permute-start.7 = (bf16[48,1024]{1,0:T(8,128)(2,1)S(1)}, bf16[48,1024]{1,0:T(8,128)(2,1)S(1)}, u32[]{:S(2)}, u32[]{:S(2)}) collective-permute-start(bf16[48,1024]{1,0:T(8,128)(2,1)S(1)} %pad_maximum_fusion.2), channel_id=1, source_target_pairs={{0,4},{1,5},{2,6},{3,7},{4,0},{5,1},{6,2},{7,3},{8,12},{9,13},{10,... | collective-permute-start | bytes 294920 | tf_op jit(solution)/shard_map/ppermute | solution.py:383
  124.0 19.6 %all-to-all-start.2 = ((bf16[8,16,1664]{2,1,0:T(8,128)(2,1)}), bf16[8,16,1664]{2,1,0:T(8,128)(2,1)S(1)}, u32[]{:S(2)}, u32[]{:S(2)}) async-start(bf16[8,16,1664]{2,1,0:T(8,128)(2,1)} %broadcast_in_dim.5), calls=%async_computation.2 | async-start | bytes 851968 | tf_op jit(solution)/shard_map/all_to_all | solution.py:361
  129.5 13.4 %collective-permute-start.8 = (bf16[40,1024]{1,0:T(8,128)(2,1)S(1)}, bf16[40,1024]{1,0:T(8,128)(2,1)S(1)}, u32[]{:S(2)}, u32[]{:S(2)}) collective-permute-start(bf16[40,1024]{1,0:T(8,128)(2,1)S(1)} %pad_maximum_fusion.3), channel_id=1, source_target_pairs={{0,8},{1,9},{2,10},{3,11},{4,12},{5,13},{6,14},{7,15},{8,0},{9,1},... | collective-permute-start | bytes 245768 | tf_op jit(solution)/shard_map/ppermute | solution.py:383
  143.6 1.4 collective-permute-start.10
where the time goes:
time: 147 us; the launch traced here: 146 us
  Pallas kernels  87.8 us (60%)
  starting transfers between devices  33.3 us (23%)
  waiting for transfers between devices  11.9 us (8%)
  other arithmetic  7.75 us (5%)
  local copies, waits for them, and re-layouts  4.12 us (3%)
    pallas_call x2, Pallas kernels, entry_sums(): pl.pallas_call(entry_sums_kernel, grid=(pl.cdiv(width, wide),), in_specs=...  23.2 us
    pallas_call x2, Pallas kernels, table_sums(): pl.pallas_call(table_sums_kernel, grid=(ENTRIES,), in_specs=[pl.BlockSpec...  20.8 us
    pallas_call x2, Pallas kernels, forward_up(): pl.pallas_call(functools.partial(forward_up_kernel, first), grid=(2 * wor...  15.3 us
    all_to_all x3, starting transfers between devices, exchange_inp(): lax.all_to_all(pieces, 'inp', 0, 0, tiled=True, axis_index_groups=ONE_CORE)  14.3 us
    pallas_call x1, Pallas kernels, down_bins(): pl.pallas_call(down_bins_kernel, grid=(width // wide,), in_specs=[pl.Bloc...  11.4 us
    ppermute x4, starting transfers between devices, hid_step(): lax.ppermute(sent, 'hid', [(i, i ^ bit) for i in range(16)]).astype(F32)  11.2 us
    pallas_call x1, Pallas kernels, forward_down(): pl.pallas_call(forward_down_kernel, grid=(pl.cdiv(2 * words, block),), in...  10.5 us
    ppermute x4, waiting for transfers between devices, hid_step(): lax.ppermute(sent, 'hid', [(i, i ^ bit) for i in range(16)]).astype(F32)  9.13 us
  transfers between devices with their start and end apart: 14, of which 4 were waited for; matrix products, arithmetic and copies ran while one was open for 3% of the time, Pallas kernels for 49%

commit v1 on v0

v1 whole, which is shorter than its diff:
```python
import functools

import jax
import jax.numpy as jnp
from jax import lax
from jax.experimental import pallas as pl
from jax.experimental.pallas import tpu as pltpu
from jax.sharding import PartitionSpec as P

BF16 = jnp.bfloat16
F32 = jnp.float32
I32 = jnp.int32
ENTRIES = 16
TOKENS = 128
LANES = 128
HBM_BYTES_PER_US = 3_000_000


def params(mib=16):
    return pltpu.CompilerParams(vmem_limit_bytes=mib * 1024 * 1024)


def cost(us):
    return pl.CostEstimate(flops=0, bytes_accessed=int(us * HBM_BYTES_PER_US), transcendentals=0)


def shape(dims, dtype):
    return jax.ShapeDtypeStruct(dims, dtype)


def dot(a, b):
    return jnp.dot(a, b, preferred_element_type=F32)


def dot_nt(a, b):
    return lax.dot_general(a, b, (((1,), (1,)), ((), ())), preferred_element_type=F32)


def dot_tn(a, b):
    return lax.dot_general(a, b, (((0,), (0,)), ((), ())), preferred_element_type=F32)


def iotas(size):
    return lax.broadcasted_iota(I32, (size, size), 0), lax.broadcasted_iota(I32, (size, size), 1)


def one_hot(hits, dtype=BF16):
    return jnp.where(hits, 1.0, 0.0).astype(dtype)


def split_matrix(block):
    source, target = iotas(block)
    half = block // 2
    return one_hot(source == jnp.where(target < half, 2 * target, 2 * (target - half) + 1))


def merge_matrix(block, dtype=BF16):
    source, target = iotas(block)
    half = block // 2
    return one_hot(target == jnp.where(source < half, 2 * source, 2 * (source - half) + 1), dtype)


def token_of(row, core):
    return (((row >> 3) & 7) * 2 + (core ^ (row >> 6))) * 8 + (row & 7)


def to_rows(core):
    row, token = iotas(TOKENS)
    return one_hot(token == token_of(row, core))


def to_owners(core, hid):
    owned, row = iotas(TOKENS)
    bits = ((owned >> 6) & 1) | ((owned >> 4) & 2) | ((owned >> 2) & 4) | (owned & 8)
    return one_hot(token_of(row, core) == (bits ^ hid) * 8 + (owned & 7))


SCALAR = pl.BlockSpec(memory_space=pltpu.SMEM)
ANYWHERE = pl.BlockSpec(memory_space=pl.ANY)
IN_HBM = pl.BlockSpec(memory_space=pltpu.HBM)
IN_VMEM = pl.BlockSpec(memory_space=pltpu.VMEM)
WIDE = 256
HALF = TOKENS // 2


def lookup(low, high, at, is_high):
    from_low = jnp.take_along_axis(low, at, axis=0, mode="promise_in_bounds")
    from_high = jnp.take_along_axis(high, at, axis=0, mode="promise_in_bounds")
    return jnp.where(is_high, from_high, from_low)


def decode_rows(index_ref, table_ref, weight_ref, begin, words):
    def tile(j, carry):
        cols = pl.ds(pl.multiple_of(j * LANES, LANES), LANES)
        low, high = table_ref[0:8, cols], table_ref[8:16, cols]
        for row in range(0, words, 16):
            even, odd = [], []
            for part in (row, row + 8):
                word = index_ref[begin + part : begin + part + 8, cols]
                even.append(lookup(low, high, word & 7, (word & 8) != 0))
                odd.append(lookup(low, high, (word >> 4) & 7, (word & 128) != 0))
            weight_ref[row : row + 16, cols] = jnp.concatenate(even, axis=0).astype(BF16)
            weight_ref[words + row : words + row + 16, cols] = jnp.concatenate(odd, axis=0).astype(BF16)
        return carry

    lax.fori_loop(0, index_ref.shape[1] // LANES, tile, 0)


def blocks_of(size, block):
    return [(at, min(block, size - at)) for at in range(0, size, block)]


def row_copies(from_ref, to_ref, sems, block):
    return [
        pltpu.make_async_copy(from_ref.at[pl.ds(at, rows)], to_ref.at[pl.ds(at, rows)], sems.at[i])
        for i, (at, rows) in enumerate(blocks_of(from_ref.shape[0], block))
    ]


def in_hbm(*arrays):
    return [pltpu.with_memory_space_constraint(each, pltpu.HBM) for each in arrays]


def start_all(copies):
    for each in copies:
        each.start()


def wait_all(copies):
    for each in copies:
        each.wait()


def forward_down_kernel(
    place_ref, raw_hbm, table_hbm, index_hbm, next_hbm, near_ref, far_ref, ordered_hbm, *refs
):
    count = len(next_hbm)
    next_refs = refs[:count]
    raw_ref, table_ref, index_ref, ordered_ref, weight_ref, sems, next_sems, sem = refs[count:]
    words = index_ref.shape[0]
    loads = row_copies(index_hbm, index_ref, sems, LANES)
    small = [pltpu.make_async_copy(raw_hbm, raw_ref, next_sems.at[count])]
    small.append(pltpu.make_async_copy(table_hbm, table_ref, next_sems.at[count + 1]))
    later = [pltpu.make_async_copy(a, b, next_sems.at[i]) for i, (a, b) in enumerate(zip(next_hbm, next_refs))]
    start_all(small + loads + later)
    wait_all(small)
    ordered_ref[...] = dot(to_rows(place_ref[0]), raw_ref[...]).astype(BF16)
    store = pltpu.make_async_copy(ordered_ref, ordered_hbm, sem)
    store.start()
    for load, (at, rows) in zip(loads, blocks_of(words, LANES)):
        load.wait()
        decode_rows(index_ref, table_ref, weight_ref, at, rows)
        hidden = dot_nt(ordered_ref[...], weight_ref[: 2 * rows, :])
        hidden = jnp.dot(hidden, merge_matrix(2 * rows, F32), precision=lax.Precision.HIGHEST, preferred_element_type=F32)
        near_ref[:, 2 * at : 2 * (at + rows)] = hidden[:HALF]
        far_ref[:, 2 * at : 2 * (at + rows)] = hidden[HALF:]
    store.wait()
    wait_all(later)


def forward_down(place, grad, table, index, brought):
    words, width = index.shape
    count = len(brought)

    def kernel(*refs):
        forward_down_kernel(*refs[:4], refs[4 : 4 + count], *refs[4 + count :])

    return pl.pallas_call(
        kernel,
        in_specs=[SCALAR] + [IN_HBM] * (3 + count),
        out_specs=[IN_VMEM, IN_VMEM, IN_HBM] + [IN_VMEM] * count,
        out_shape=[
            pltpu.VMEM((HALF, 2 * words), F32),
            pltpu.VMEM((HALF, 2 * words), F32),
            pltpu.HBM((TOKENS, width), BF16),
        ]
        + [pltpu.VMEM(each.shape, each.dtype) for each in brought],
        scratch_shapes=[
            pltpu.VMEM(grad.shape, BF16),
            pltpu.VMEM(table.shape, F32),
            pltpu.VMEM(index.shape, I32),
            pltpu.VMEM((TOKENS, width), BF16),
            pltpu.VMEM((WIDE, width), BF16),
            pltpu.SemaphoreType.DMA((pl.cdiv(words, LANES),)),
            pltpu.SemaphoreType.DMA((count + 2,)),
            pltpu.SemaphoreType.DMA,
        ],
        compiler_params=params(),
        cost_estimate=cost(5),
        name="forward_down",
    )(place, *in_hbm(grad, table, index, *brought))


def forward_up_kernel(first, *refs):
    if first:
        place_ref, raw_ref, index_ref, table_ref, next_hbm, near_ref, far_ref, weight_hbm = refs[:8]
        x_ref, x_hbm, next_ref, weight_ref, sems, next_sems = refs[8:]
        later = [pltpu.make_async_copy(next_hbm, next_ref, next_sems.at[0])]
        start_all(later)
        x = dot(to_rows(place_ref[0]), raw_ref[...]).astype(BF16)
        for at in range(0, x.shape[1], WIDE):
            x_ref[:, at : at + WIDE] = dot(x[:, at : at + WIDE], split_matrix(WIDE)).astype(BF16)
        later.append(pltpu.make_async_copy(x_ref, x_hbm, next_sems.at[1]))
        start_all(later[1:])
    else:
        x_ref, index_ref, table_ref, near_ref, far_ref, weight_hbm, weight_ref, sems = refs
        later = []
    stores = row_copies(weight_ref, weight_hbm, sems, WIDE)
    for store, at in zip(stores, range(0, index_ref.shape[0], LANES)):
        decode_rows(index_ref, table_ref, weight_ref.at[pl.ds(2 * at, WIDE)], at, LANES)
        store.start()
    for at, cols in blocks_of(index_ref.shape[1], WIDE):
        sums = dot(x_ref[...], weight_ref[:, at : at + cols])
        near_ref[:, at : at + cols] = sums[:HALF]
        far_ref[:, at : at + cols] = sums[HALF:]
    wait_all(stores + later)


def forward_up(place, x, index, table, later_index):
    first = place is not None
    words, width = index.shape
    ordered = (TOKENS, 2 * words)
    return pl.pallas_call(
        functools.partial(forward_up_kernel, first),
        in_specs=[SCALAR] * first + [IN_VMEM] * 3 + [IN_HBM] * first,
        out_specs=[IN_VMEM, IN_VMEM, IN_HBM] + [IN_VMEM, IN_HBM, IN_VMEM] * first,
        out_shape=[
            pltpu.VMEM((HALF, width), F32),
            pltpu.VMEM((HALF, width), F32),
            pltpu.HBM((2 * words, width), BF16),
        ]
        + [pltpu.VMEM(ordered, BF16), pltpu.HBM(ordered, BF16), pltpu.VMEM((words, width), I32)] * first,
        scratch_shapes=[pltpu.VMEM((2 * words, width), BF16), pltpu.SemaphoreType.DMA((2 * words // WIDE,))]
        + [pltpu.SemaphoreType.DMA((2,))] * first,
        compiler_params=params(),
        cost_estimate=cost(5),
        name="forward_gate" if first else "forward_up",
    )(*([place] * first + [x, index, table] + in_hbm(*[later_index] * first)))


def entry_sums_kernel(x_ref, index_ref, after_ref, out_ref, entry_ref):
    words = index_ref.shape[0]
    for row in range(0, words, 16):
        word = index_ref[row : row + 16, :]
        to = row // LANES * WIDE + row % LANES
        entry_ref[to : to + 16, :] = (word & 15).astype(jnp.int16)
        entry_ref[to + LANES : to + LANES + 16, :] = ((word >> 4) & 15).astype(jnp.int16)
    one, zero = jnp.ones((), BF16), jnp.zeros((), BF16)
    for entry in range(ENTRIES):
        chosen = jnp.where(entry_ref[...] == jnp.int16(entry), one, zero)
        out_ref[entry] = dot(x_ref[...], chosen).astype(BF16)


def entry_sums(x, index, after):
    words, width = index.shape
    return pl.pallas_call(
        entry_sums_kernel,
        grid=(pl.cdiv(width, WIDE),),
        in_specs=[
            pl.BlockSpec((TOKENS, 2 * words), lambda i: (0, 0)),
            pl.BlockSpec((words, WIDE), lambda i: (0, i)),
            ANYWHERE,
        ],
        out_specs=pl.BlockSpec((ENTRIES, TOKENS, WIDE), lambda i: (0, 0, i)),
        out_shape=shape((ENTRIES, TOKENS, width), BF16),
        scratch_shapes=[pltpu.VMEM((2 * words, WIDE), jnp.int16)],
        compiler_params=params(60),
        cost_estimate=cost(11),
        name="entry_sums",
    )(x, index, after)


def table_sums_kernel(part, near_ref, far_ref, sums_hbm, after_ref, out_ref, grad_ref, sums_ref, sems):
    count = ENTRIES // sems.shape[0]
    loads = row_copies(sums_hbm, sums_ref, sems, count)
    start_all(loads)
    width = sums_ref.shape[2]
    grad_ref[:HALF, :] = near_ref[:, part * width : (part + 1) * width].astype(F32)
    grad_ref[HALF:, :] = far_ref[:, part * width : (part + 1) * width].astype(F32)
    for load, begin in zip(loads, range(0, ENTRIES, count)):
        load.wait()

        def tile(j, carry, begin=begin):
            cols = pl.ds(pl.multiple_of(j * LANES, LANES), LANES)
            rows = []
            for entry in range(begin, begin + count):
                acc = None
                for row in range(0, TOKENS, 16):
                    product = sums_ref[entry, row : row + 16, cols].astype(F32) * grad_ref[row : row + 16, cols]
                    acc = product if acc is None else acc + product
                rows.append(jnp.sum(acc, axis=0, keepdims=True))
            out_ref[begin : begin + count, cols] = jnp.concatenate(rows, axis=0)
            return carry

        lax.fori_loop(0, width // LANES, tile, 0)


def table_sums(near, far, part, sums, after):
    width = sums.shape[2]
    return pl.pallas_call(
        functools.partial(table_sums_kernel, part),
        in_specs=[IN_VMEM, IN_VMEM, IN_HBM, ANYWHERE],
        out_specs=IN_VMEM,
        out_shape=pltpu.VMEM((ENTRIES, width), F32),
        scratch_shapes=[
            pltpu.VMEM((TOKENS, width), F32),
            pltpu.VMEM(sums.shape, BF16),
            pltpu.SemaphoreType.DMA((4,)),
        ],
        compiler_params=params(),
        cost_estimate=cost(4.5),
        name="table_sums",
    )(near, far, *in_hbm(sums), after)


def down_bins_kernel(near_ref, far_ref, grad_hbm, index_hbm, next_hbm, out_ref, next_refs, *scratch):
    grad_ref, index_ref, activ_ref, wgrad_ref, sems = scratch
    loads = [pltpu.make_async_copy(grad_hbm, grad_ref, sems.at[0])]
    loads.append(pltpu.make_async_copy(index_hbm, index_ref, sems.at[1]))
    loads += [pltpu.make_async_copy(a, b, sems.at[2 + i]) for i, (a, b) in enumerate(zip(next_hbm, next_refs))]
    start_all(loads)
    block = LANES
    half = block // 2
    words, width = index_ref.shape
    split = split_matrix(block)
    for at in range(0, 2 * words, block):
        cols = slice(at, at + block)
        activ = jnp.concatenate([near_ref[:, cols], far_ref[:, cols]], axis=0)
        activ_ref[:, cols] = dot(activ, split).astype(BF16)
    wait_all(loads[:1])
    for at in range(0, width, WIDE):
        wgrad_ref[:, at : at + WIDE] = dot_tn(activ_ref[...], grad_ref[:, at : at + WIDE]).astype(BF16)
    wait_all(loads[1:2])
    zero = jnp.zeros((), BF16)

    def lanes(j, carry):
        cols = pl.ds(pl.multiple_of(j * LANES, LANES), LANES)

        def add_block(i, totals):
            part = [None] * ENTRIES
            for row in range(0, half, 16):
                word = index_ref[pl.ds(pl.multiple_of(i * half + row, 16), 16), cols].astype(jnp.int16)
                for entries, offset in ((word & 15, 0), ((word >> 4) & 15, half)):
                    grads = wgrad_ref[pl.ds(pl.multiple_of(i * block + offset + row, 16), 16), cols]
                    for entry in range(ENTRIES):
                        chosen = jnp.where(entries == jnp.int16(entry), grads, zero)
                        part[entry] = chosen if part[entry] is None else part[entry] + chosen
            done = []
            for entry in range(ENTRIES):
                both = part[entry].astype(F32)
                done.append(totals[entry] + both[:8] + both[8:])
            return tuple(done)

        start = tuple(jnp.zeros((8, LANES), F32) for _ in range(ENTRIES))
        totals = lax.fori_loop(0, 2 * words // block, add_block, start)
        out_ref[:, cols] = jnp.concatenate([jnp.sum(each, axis=0, keepdims=True) for each in totals], axis=0)
        return carry

    lax.fori_loop(0, width // LANES, lanes, 0)
    wait_all(loads[2:])


def down_bins(near, far, grad, index, brought):
    words, width = index.shape
    count = len(brought)

    def kernel(*refs):
        out = 4 + count
        down_bins_kernel(*refs[:4], refs[4:out], refs[out], refs[out + 1 : out + 1 + count], *refs[out + 1 + count :])

    return pl.pallas_call(
        kernel,
        in_specs=[IN_VMEM] * 2 + [IN_HBM] * (2 + count),
        out_specs=[IN_VMEM] * (1 + count),
        out_shape=[pltpu.VMEM((ENTRIES, width), F32)] + [pltpu.VMEM(each.shape, each.dtype) for each in brought],
        scratch_shapes=[
            pltpu.VMEM((TOKENS, width), BF16),
            pltpu.VMEM((words, width), I32),
            pltpu.VMEM((TOKENS, 2 * words), BF16),
            pltpu.VMEM((2 * words, width), BF16),
            pltpu.SemaphoreType.DMA((2 + count,)),
        ],
        compiler_params=params(),
        cost_estimate=cost(10),
        name="down_bins",
    )(near, far, *in_hbm(grad, index, *brought))


def put_bins(bins, sent_ref):
    coarse = bins.astype(BF16)
    sent_ref[:ENTRIES] = coarse
    sent_ref[ENTRIES : 2 * ENTRIES] = (bins - coarse.astype(F32)).astype(BF16)


def input_grad_kernel(
    place_ref, near_ref, far_ref, wg_ref, wu_ref, bins_ref, kept_ref, sent_ref
):
    rows, width = wg_ref.shape
    gate = jnp.concatenate([near_ref[:, :width], far_ref[:, :width]], axis=0)
    up = jnp.concatenate([near_ref[:, width:], far_ref[:, width:]], axis=0)
    order = to_owners(place_ref[0], place_ref[1])
    merge = merge_matrix(WIDE)
    for at in range(0, rows, WIDE):
        part = (dot_nt(gate, wg_ref[at : at + WIDE, :]) + dot_nt(up, wu_ref[at : at + WIDE, :])).astype(BF16)
        part = dot(dot(order, part).astype(BF16), merge)
        kept_ref[:, at : at + WIDE] = part[:HALF]
        sent_ref[2 * ENTRIES :, at : at + WIDE] = part[HALF:].astype(BF16)
    put_bins(bins_ref[...], sent_ref)


def input_grads(place, near, far, w_gate, w_up, bins):
    width = w_gate.shape[0]
    return pl.pallas_call(
        input_grad_kernel,
        in_specs=[SCALAR] + [IN_VMEM] * 5,
        out_specs=[IN_VMEM] * 2,
        out_shape=[pltpu.VMEM((HALF, width), F32), pltpu.VMEM((2 * ENTRIES + HALF, width), BF16)],
        compiler_params=params(),
        cost_estimate=cost(3.5),
        name="input_grad",
    )(place, near, far, w_gate, w_up, bins)


def add_received_kernel(kept_ref, bins_ref, back_ref, rows_ref, sums_ref, sent_ref):
    bins = bins_ref[...] + (back_ref[:ENTRIES].astype(F32) + back_ref[ENTRIES : 2 * ENTRIES].astype(F32))
    rows = kept_ref[...] + back_ref[2 * ENTRIES :].astype(F32)
    rows_ref[...] = rows[: rows_ref.shape[0]]
    sums_ref[...] = bins
    put_bins(bins, sent_ref)
    sent_ref[2 * ENTRIES :] = rows[rows.shape[0] - sent_ref.shape[0] + 2 * ENTRIES :].astype(BF16)


def add_received(kept, bins, back):
    rows, width = kept.shape
    half = max(rows // 2, 16)
    return pl.pallas_call(
        add_received_kernel,
        in_specs=[IN_VMEM] * 3,
        out_specs=[IN_VMEM] * 3,
        out_shape=[
            pltpu.VMEM((half, width), F32),
            pltpu.VMEM(bins.shape, F32),
            pltpu.VMEM((2 * ENTRIES + half, width), BF16),
        ],
        compiler_params=params(),
        cost_estimate=cost(0.7),
        name="add_received",
    )(kept, bins, back)


ONE_CORE = [[2 * place + core for place in range(8)] for core in range(2)]


def other_core(array):
    return lax.ppermute(array, "inp", [(i, i ^ 1) for i in range(16)])


def exchange_inp(pieces):
    return lax.all_to_all(pieces, "inp", 0, 0, tiled=True, axis_index_groups=ONE_CORE)


def copies(array, count):
    return jnp.broadcast_to(array[None], (count,) + array.shape)


def total(arrays):
    return functools.reduce(jnp.add, [a.astype(F32) for a in arrays])


def sum_inp(gate, up, core):
    own = jnp.where(core == 0, gate, up) + other_core(jnp.where(core == 0, up, gate))
    own = total(exchange_inp(copies(own.astype(BF16), 8)))
    other = other_core(own)
    return jnp.where(core == 0, own, other), jnp.where(core == 0, other, own)


def other_hid(array, bit):
    return lax.ppermute(array, "hid", [(i, i ^ bit) for i in range(16)])


def local_hidden(pre_gate, pre_up, hidden_grad):
    sig_gate = jax.nn.sigmoid(pre_gate)
    silu_gate = pre_gate * sig_gate
    activ = (silu_gate * pre_up).astype(BF16)
    gate_grad = (hidden_grad * pre_up * sig_gate * (1.0 + pre_gate * (1.0 - sig_gate))).astype(BF16)
    up_grad = (hidden_grad * silu_gate).astype(BF16)
    return activ, gate_grad, up_grad


def shards(inputs, out_grad, gate_index, up_index, down_index, gate_table, up_table, down_table):
    width = gate_index.shape[1]
    core = lax.axis_index("inp") % 2
    place = jnp.stack([core, lax.axis_index("hid")]).astype(I32)

    hidden_near, hidden_far, grad, x, gate_words, gate_lookup, up_lookup = forward_down(
        place, out_grad, down_table, down_index, (inputs, gate_index, gate_table, up_table)
    )
    hidden_back = other_core(hidden_far)
    gate_near, gate_far, w_gate, x_near, x, up_words = forward_up(place, x, gate_words, gate_lookup, up_index)
    gate_back = other_core(gate_far)
    up_near, up_far, w_up = forward_up(None, x_near, up_words, up_lookup, None)
    up_back = other_core(up_far)
    pair_sums = jnp.concatenate(
        [(gate_near + gate_back).astype(BF16), (up_near + up_back).astype(BF16), (hidden_near + hidden_back).astype(BF16)],
        axis=1,
    ).reshape(8, 8, 3 * width)
    pieces = exchange_inp(pair_sums)
    gate_sums = entry_sums(x, gate_index, pair_sums)
    pieces, gate_sums = lax.optimization_barrier((pieces, gate_sums))
    pre = total(pieces)
    activ, gate_grad, up_grad = local_hidden(pre[:, :width], pre[:, width : 2 * width], pre[:, 2 * width :])
    grads = copies(jnp.concatenate([gate_grad, up_grad, activ], axis=1), 8)
    near = exchange_inp(grads)
    up_sums = entry_sums(x, up_index, grads)
    near, up_sums = lax.optimization_barrier((near, up_sums))
    near = near.reshape(TOKENS // 2, 3 * width)
    activ_near, grad_near = near[:, 2 * width :], near[:, : 2 * width]
    activ_far, grad_far = other_core(activ_near), other_core(grad_near)

    down_sum, w_gate, w_up = down_bins(activ_near, activ_far, grad, down_index, (w_gate, w_up))
    kept, sent = input_grads(place, grad_near, grad_far, w_gate, w_up, down_sum)
    gate_part = table_sums(grad_near, grad_far, 0, gate_sums, sent)
    kept, down_sum, sent = add_received(kept, down_sum, other_hid(sent, 1))
    up_part = table_sums(grad_near, grad_far, 1, up_sums, sent)
    gate_sum, up_sum = sum_inp(gate_part, up_part, core)
    kept, down_sum, sent = add_received(kept, down_sum, other_hid(sent, 2))
    kept, down_sum, sent = add_received(kept, down_sum, other_hid(sent, 4))
    back = other_hid(sent, 8).astype(F32)
    input_grad = (kept[:8] + back[2 * ENTRIES + 8 :]).astype(BF16)
    down_sum = down_sum + (back[:ENTRIES] + back[ENTRIES : 2 * ENTRIES])
    scale = 1.0 / TOKENS
    return input_grad, gate_sum * scale, up_sum * scale, down_sum * scale


def solution(mesh):
    in_specs = (
        P(None, "inp"),
        P(None, "inp"),
        P("inp", "hid"),
        P("inp", "hid"),
        P("hid", "inp"),
        P(None, "hid"),
        P(None, "hid"),
        P(None, "inp"),
    )
    out_specs = (P("hid", "inp"), P(None, "hid"), P(None, "hid"), P(None, "inp"))
    return jax.shard_map(shards, mesh=mesh, in_specs=in_specs, out_specs=out_specs, check_vma=False)
```

time: 147 us -> 123 us (0.84)
  Pallas kernels: 87.8 us -> 63.9 us
  starting transfers between devices: 33.3 us -> 37.9 us
  other arithmetic: 7.75 us -> 3.32 us
  waiting for transfers between devices: 11.9 us -> 14.5 us
  local copies, waits for them, and re-layouts: 4.12 us -> 1.7 us
    pallas_call x9 -> x12, Pallas kernels: 87.8 us -> 63.9 us  [the longest x2 23.3 us: entry_sums(): pl.pallas_call(entry_sums_kernel, grid=(pl.cdiv(width, WIDE),), in_specs=...]
    ppermute x7, starting transfers between devices: 7.7 us -> 11.2 us  [other_core(): return lax.ppermute(array, 'inp', [(i, i ^ 1) for i in range(16)])]
  transfers between devices with their start and end apart: 14 -> 14, of which waited for: 4 -> 8; matrix products, arithmetic and copies ran while one was open for 3% -> 1% of each run, Pallas kernels for 49% -> 37%
where the time goes in v1:
time: 123 us; the launch traced here: 122 us
  Pallas kernels  63.9 us (52%)
  starting transfers between devices  37.9 us (31%)
  waiting for transfers between devices  14.5 us (12%)
  other arithmetic  3.32 us (3%)
  local copies, waits for them, and re-layouts  1.7 us (1%)
    pallas_call x2, Pallas kernels, entry_sums(): pl.pallas_call(entry_sums_kernel, grid=(pl.cdiv(width, WIDE),), in_specs=...  23.3 us
    all_to_all x3, starting transfers between devices, exchange_inp(): lax.all_to_all(pieces, 'inp', 0, 0, tiled=True, axis_index_groups=ONE_CORE)  14.3 us
    ppermute x4, starting transfers between devices, other_hid(): return lax.ppermute(array, 'hid', [(i, i ^ bit) for i in range(16)])  12.4 us
    ppermute x7, starting transfers between devices, other_core(): return lax.ppermute(array, 'inp', [(i, i ^ 1) for i in range(16)])  11.2 us
    ppermute x4, waiting for transfers between devices, other_hid(): return lax.ppermute(array, 'hid', [(i, i ^ bit) for i in range(16)])  10.5 us
    pallas_call x1, Pallas kernels, down_bins(): pl.pallas_call(kernel, in_specs=[IN_VMEM] * 2 + [IN_HBM] * (2 + count), o...  9.9 us
    pallas_call x1, Pallas kernels, forward_down(): pl.pallas_call(kernel, in_specs=[SCALAR] + [IN_HBM] * (3 + count), out_sp...  9.78 us
    pallas_call x2, Pallas kernels, forward_up(): pl.pallas_call(functools.partial(forward_up_kernel, first), in_specs=[SCA...  8.48 us
  transfers between devices with their start and end apart: 14, of which 8 were waited for; matrix products, arithmetic and copies ran while one was open for 1% of the time, Pallas kernels for 37%

profile of v1, /device:TPU:1, one launch (start us, length us, event | category | flops | bytes accessed | tf_op | source)
XLA Modules:
  0.0 122.1 jit_solution(16026474910649890876)
XLA Ops:
  0.6 0.1 pad_add_fusion.refs_0_.place_ref
  0.7 9.8 %forward_down.1 = (f32[64,1664]{1,0:T(8,128)S(1)}, f32[64,1664]{1,0:T(8,128)S(1)}, bf16[128,1024]{1,0:T(8,128)(2,1)}, bf16[128,1024]{1,0:T(8,128)(2,1)S(1)}, s32...) custom-call(s32[2]{0:T(128)S(1)} %pad_add_fusion.refs_0_.place_ref, ...), custom_call_target="tpu_custom_call" | custom-call | bytes 15000000 | tf_op jit(solution)/shard_map/forward_down/pallas_call | solution.py:168
  10.5 3.3 %collective-permute-start.2 = (f32[64,1664]{1,0:T(8,128)S(1)}, f32[64,1664]{1,0:T(8,128)S(1)}, u32[]{:S(2)}, u32[]{:S(2)}) collective-permute-start(f32[64,1664]{1,0:T(8,128)S(1)} %get-tuple-element.49), channel_id=1, source_target_pairs={{0,16},{16,0},{32,48},{48,32},{64,80},{80,64},{96,112},{112,96},{1... | collective-permute-start | bytes 1277960 | tf_op jit(solution)/shard_map/ppermute | solution.py:455
  13.8 4.7 %forward_gate.1 = (f32[64,1664]{1,0:T(8,128)S(1)}, f32[64,1664]{1,0:T(8,128)S(1)}, bf16[1024,1664]{1,0:T(8,128)(2,1)}, bf16[128,1024]{1,0:T(8,128)(2,1)S(1)}, bf...) custom-call(s32[2]{0:T(128)S(1)} %pad_add_fusion.refs_0_.place_ref, bf16[128,1024]{1,0:T(8,128)(2,1)S(1)} %get-tuple-element.38.refs_1_, ...), custom_call_target="tpu_custom_call" | custom-call | bytes 15000000 | tf_op jit(solution)/shard_map/forward_gate/pallas_call | solution.py:223
  18.5 0.1 collective-permute-start
  18.6 3.8 %forward_up.1 = (f32[64,1664]{1,0:T(8,128)S(1)}, f32[64,1664]{1,0:T(8,128)S(1)}, bf16[1024,1664]{1,0:T(8,128)(2,1)}) custom-call(bf16[128,1024]{1,0:T(8,128)(2,1)S(1)} %get-tuple-element.43.refs_0_, s32[512,1664]{1,0:T(8,128)S(1)} %get-tuple-element.44.refs_1_, f32[16,1664]{1,0:T(8,128)S(1)} %get-tuple-element.45.refs_2_), custom_call_target="tpu_custom_call" | custom-call | bytes 15000000 | tf_op jit(solution)/shard_map/forward_up/pallas_call | solution.py:223
  22.4 0.6 collective-permute-start.1
  23.0 0.0 collective-permute-done.2
  23.1 0.0 collective-permute-done
  23.1 1.3 %collective-permute-done.1 = f32[64,1664]{1,0:T(8,128)S(1)} collective-permute-done((f32[64,1664]{1,0:T(8,128)S(1)}, f32[64,1664]{1,0:T(8,128)S(1)}, u32[]{:S(2)}, u32[]{:S(2)}) %collective-permute-start.1) | collective-permute-done | bytes 426016 | tf_op jit(solution)/shard_map/ppermute | solution.py:455
  24.4 0.9 maximum_bitcast_fusion.after_ref
  25.3 3.8 %all-to-all-start = ((bf16[8,8,4992]{2,1,0:T(8,128)(2,1)}), bf16[8,8,4992]{2,1,0:T(8,128)(2,1)S(1)}, u32[]{:S(2)}, u32[]{:S(2)}) async-start(bf16[8,8,4992]{2,1,0:T(8,128)(2,1)} %maximum_bitcast_fusion.after_ref), calls=%async_computation | async-start | bytes 1277952 | tf_op jit(solution)/shard_map/all_to_all | solution.py:459
  29.1 11.7 %entry_sums.2.sums_hbm = bf16[16,128,1664]{2,1,0:T(8,128)(2,1)} custom-call(bf16[128,1024]{1,0:T(8,128)(2,1)} %get-tuple-element.50.x_ref, s32[512,1664]{1,0:T(8,128)} %index_ref.2, bf16[8,8,4992]{2,1,0:T(8,128)(2,1)} %maximum_bitcast_fusion.after_ref), custom_call_target="tpu_custom_call" | custom-call | bytes 33000000 | tf_op jit(solution)/shard_map/entry_sums/pallas_call | solution.py:256
  40.8 0.0 all-to-all-done
  40.8 0.1 add_bitcast_fusion
  40.9 0.9 broadcast_in_dim.4.after_ref
  41.8 5.1 %all-to-all-start.1 = ((bf16[8,8,4992]{2,1,0:T(8,128)(2,1)}), bf16[8,8,4992]{2,1,0:T(8,128)(2,1)S(1)}, u32[]{:S(2)}, u32[]{:S(2)}) async-start(bf16[8,8,4992]{2,1,0:T(8,128)(2,1)} %broadcast_in_dim.4.after_ref), calls=%async_computation.1 | async-start | bytes 1277952 | tf_op jit(solution)/shard_map/all_to_all | solution.py:459
  46.9 11.7 %entry_sums.3.sums_hbm = bf16[16,128,1664]{2,1,0:T(8,128)(2,1)} custom-call(bf16[128,1024]{1,0:T(8,128)(2,1)} %get-tuple-element.50.x_ref, s32[512,1664]{1,0:T(8,128)} %index_ref.3, bf16[8,8,4992]{2,1,0:T(8,128)(2,1)} %broadcast_in_dim.4.after_ref), custom_call_target="tpu_custom_call" | custom-call | bytes 33000000 | tf_op jit(solution)/shard_map/entry_sums/pallas_call | solution.py:256
  58.6 0.0 all-to-all-done.1
  58.6 1.3 %collective-permute-start.3 = (bf16[64,3328]{1,0:T(8,128)(2,1)S(1)}, bf16[64,3328]{1,0:T(8,128)(2,1)S(1)}, u32[]{:S(2)}, u32[]{:S(2)}) collective-permute-start(bf16[64,3328]{1,0:T(8,128)(2,1)S(1)} %slice.39.near_ref), channel_id=1, source_target_pairs={{0,16},{16,0},{32,48},{48,32},{64,80},{80,64},{96,112},{112,96},{1... | collective-permute-start | bytes 1277960 | tf_op jit(solution)/shard_map/ppermute | solution.py:455
  59.9 0.3 collective-permute-start.4
  60.2 1.4 %collective-permute-done.4.refs_1_ = bf16[64,1664]{1,0:T(8,128)(2,1)S(1)} collective-permute-done((bf16[64,1664]{1,0:T(8,128)(2,1)S(1)}, bf16[64,1664]{1,0:T(8,128)(2,1)S(1)}, u32[]{:S(2)}, u32[]{:S(2)}) %collective-permute-start.4) | collective-permute-done | bytes 213024 | tf_op jit(solution)/shard_map/ppermute | solution.py:455
  61.7 9.9 %down_bins.1 = (f32[16,1024]{1,0:T(8,128)S(1)}, bf16[1024,1664]{1,0:T(8,128)(2,1)S(1)}, bf16[1024,1664]{1,0:T(8,128)(2,1)S(1)}) custom-call(bf16[64,1664]{1,0:T(8,128)(2,1)S(1)} %slice.40.refs_0_, bf16[64,1664]{1,0:T(8,128)(2,1)S(1)} %collective-permute-done.4.refs_1_, bf16[128,1024]{1,0:T(8,128)(2,1)} %get-tuple-element.53.refs_2_, s32[832,1024]{1,0:T(8,128)} %refs_3_.3, ...), custom_call_target="tpu_custom_call" | custom-call | bytes 30000000 | tf_op jit(solution)/shard_map/down_bins/pallas_call | solution.py:371
  71.6 0.0 collective-permute-done.3.far_ref
  71.6 5.1 %input_grad.1 = (f32[64,1024]{1,0:T(8,128)S(1)}, bf16[96,1024]{1,0:T(8,128)(2,1)S(1)}) custom-call(s32[2]{0:T(128)S(1)} %pad_add_fusion.refs_0_.place_ref, bf16[64,3328]{1,0:T(8,128)(2,1)S(1)} %slice.39.near_ref, bf16[64,3328]{1,0:T(8,128)(2,1)S(1)} %collective-permute-done.3.far_ref, bf16[1024,1664]{1,0:T(8,128)(2,1)S(1)} %get-tuple-element.56.wg_ref, ...), custom_call_target="tpu_custom_call" | custom-call | bytes 10500000 | tf_op jit(solution)/shard_map/input_grad/pallas_call | solution.py:413
  76.7 1.3 %collective-permute-start.5 = (bf16[96,1024]{1,0:T(8,128)(2,1)S(1)}, bf16[96,1024]{1,0:T(8,128)(2,1)S(1)}, u32[]{:S(2)}, u32[]{:S(2)}) collective-permute-start(bf16[96,1024]{1,0:T(8,128)(2,1)S(1)} %get-tuple-element.60.after_ref), channel_id=1, source_target_pairs={{0,1},{1,0},{2,3},{3,2},{4,5},{5,4},{6,7},{7,6},{8,9},{9,8},{10,11... | collective-permute-start | bytes 589832 | tf_op jit(solution)/shard_map/ppermute | solution.py:478
  78.0 3.6 %table_sums.2 = f32[16,1664]{1,0:T(8,128)S(1)} custom-call(bf16[64,3328]{1,0:T(8,128)(2,1)S(1)} %slice.39.near_ref, bf16[64,3328]{1,0:T(8,128)(2,1)S(1)} %collective-permute-done.3.far_ref, bf16[16,128,1664]{2,1,0:T(8,128)(2,1)} %entry_sums.2.sums_hbm, bf16[96,1024]{1,0:T(8,128)(2,1)S(1)} %get-tuple-element.60.after_ref), custom_call_target="tpu_custom_call" | custom-call | bytes 13500000 | tf_op jit(solution)/shard_map/table_sums/pallas_call | solution.py:300
  81.6 1.3 %collective-permute-done.5.back_ref = bf16[96,1024]{1,0:T(8,128)(2,1)S(1)} collective-permute-done((bf16[96,1024]{1,0:T(8,128)(2,1)S(1)}, bf16[96,1024]{1,0:T(8,128)(2,1)S(1)}, u32[]{:S(2)}, u32[]{:S(2)}) %collective-permute-start.5) | collective-permute-done | bytes 196640 | tf_op jit(solution)/shard_map/ppermute | solution.py:478
  83.0 3.6 %table_sums.3 = f32[16,1664]{1,0:T(8,128)S(1)} custom-call(bf16[64,3328]{1,0:T(8,128)(2,1)S(1)} %slice.39.near_ref, bf16[64,3328]{1,0:T(8,128)(2,1)S(1)} %collective-permute-done.3.far_ref, bf16[16,128,1664]{2,1,0:T(8,128)(2,1)} %entry_sums.3.sums_hbm, bf16[64,1024]{1,0:T(8,128)(2,1)S(1)} %get-tuple-element.63.after_ref), custom_call_target="tpu_custom_call" | custom-call | bytes 13500000 | tf_op jit(solution)/shard_map/table_sums/pallas_call | solution.py:300
  86.7 1.2 %collective-permute-start.9 = (f32[16,1664]{1,0:T(8,128)S(1)}, f32[16,1664]{1,0:T(8,128)S(1)}, u32[]{:S(2)}, u32[]{:S(2)}) collective-permute-start(f32[16,1664]{1,0:T(8,128)S(1)} %broadcast_select_fusion), channel_id=1, source_target_pairs={{0,16},{16,0},{32,48},{48,32},{64,80},{80,64},{96,112},{112,96},{1... | collective-permute-start | bytes 319496 | tf_op jit(solution)/shard_map/ppermute | solution.py:455
  87.9 1.0 collective-permute-done.9
  88.9 0.8 broadcast_in_dim.5
  89.7 5.4 %all-to-all-start.2 = ((bf16[8,16,1664]{2,1,0:T(8,128)(2,1)}), bf16[8,16,1664]{2,1,0:T(8,128)(2,1)S(1)}, u32[]{:S(2)}, u32[]{:S(2)}) async-start(bf16[8,16,1664]{2,1,0:T(8,128)(2,1)} %broadcast_in_dim.5), calls=%async_computation.2 | async-start | bytes 851968 | tf_op jit(solution)/shard_map/all_to_all | solution.py:459
  95.1 2.7 %collective-permute-start.6 = (bf16[64,1024]{1,0:T(8,128)(2,1)S(1)}, bf16[64,1024]{1,0:T(8,128)(2,1)S(1)}, u32[]{:S(2)}, u32[]{:S(2)}) collective-permute-start(bf16[64,1024]{1,0:T(8,128)(2,1)S(1)} %get-tuple-element.63.after_ref), channel_id=1, source_target_pairs={{0,2},{1,3},{2,0},{3,1},{4,6},{5,7},{6,4},{7,5},{8,10},{9,11},{10,... | collective-permute-start | bytes 393224 | tf_op jit(solution)/shard_map/ppermute | solution.py:478
  97.8 3.2 %collective-permute-done.6.back_ref = bf16[64,1024]{1,0:T(8,128)(2,1)S(1)} collective-permute-done((bf16[64,1024]{1,0:T(8,128)(2,1)S(1)}, bf16[64,1024]{1,0:T(8,128)(2,1)S(1)}, u32[]{:S(2)}, u32[]{:S(2)}) %collective-permute-start.6) | collective-permute-done | bytes 131104 | tf_op jit(solution)/shard_map/ppermute | solution.py:478
  101.0 3.1 %collective-permute-start.7 = (bf16[48,1024]{1,0:T(8,128)(2,1)S(1)}, bf16[48,1024]{1,0:T(8,128)(2,1)S(1)}, u32[]{:S(2)}, u32[]{:S(2)}) collective-permute-start(bf16[48,1024]{1,0:T(8,128)(2,1)S(1)} %get-tuple-element.66), channel_id=1, source_target_pairs={{0,4},{1,5},{2,6},{3,7},{4,0},{5,1},{6,2},{7,3},{8,12},{9,13},{10,... | collective-permute-start | bytes 294920 | tf_op jit(solution)/shard_map/ppermute | solution.py:478
  104.1 3.7 %collective-permute-done.7.back_ref = bf16[48,1024]{1,0:T(8,128)(2,1)S(1)} collective-permute-done((bf16[48,1024]{1,0:T(8,128)(2,1)S(1)}, bf16[48,1024]{1,0:T(8,128)(2,1)S(1)}, u32[]{:S(2)}, u32[]{:S(2)}) %collective-permute-start.7) | collective-permute-done | bytes 98336 | tf_op jit(solution)/shard_map/ppermute | solution.py:478
  107.8 5.2 %collective-permute-start.8 = (bf16[48,1024]{1,0:T(8,128)(2,1)S(1)}, bf16[48,1024]{1,0:T(8,128)(2,1)S(1)}, u32[]{:S(2)}, u32[]{:S(2)}) collective-permute-start(bf16[48,1024]{1,0:T(8,128)(2,1)S(1)} %get-tuple-element.68), channel_id=1, source_target_pairs={{0,8},{1,9},{2,10},{3,11},{4,12},{5,13},{6,14},{7,15},{8,0},{9,1},... | collective-permute-start | bytes 294920 | tf_op jit(solution)/shard_map/ppermute | solution.py:478
  113.0 2.3 %collective-permute-done.8 = bf16[48,1024]{1,0:T(8,128)(2,1)S(1)} collective-permute-done((bf16[48,1024]{1,0:T(8,128)(2,1)S(1)}, bf16[48,1024]{1,0:T(8,128)(2,1)S(1)}, u32[]{:S(2)}, u32[]{:S(2)}) %collective-permute-start.8) | collective-permute-done | bytes 98336 | tf_op jit(solution)/shard_map/ppermute | solution.py:478
  115.4 0.6 fusion.1
  116.0 0.0 all-to-all-done.2
  116.0 0.1 add_bitcast_fusion.1
  116.1 4.4 %collective-permute-start.10 = (f32[16,1664]{1,0:T(8,128)S(1)}, f32[16,1664]{1,0:T(8,128)S(1)}, u32[]{:S(2)}, u32[]{:S(2)}) collective-permute-start(f32[16,1664]{1,0:T(8,128)S(1)} %add_bitcast_fusion.1), channel_id=1, source_target_pairs={{0,16},{16,0},{32,48},{48,32},{64,80},{80,64},{96,112},{112,96},{1... | collective-permute-start | bytes 319496 | tf_op jit(solution)/shard_map/ppermute | solution.py:455
  120.4 0.6 fusion.3
  121.1 0.3 collective-permute-done.10
  121.4 0.8 select_multiply_fusion
  (13 shorter events, 0.4 us)
Async XLA Ops:
  10.5 12.5 %collective-permute-start.2 = (f32[64,1664]{1,0:T(8,128)S(1)}, f32[64,1664]{1,0:T(8,128)S(1)}, u32[]{:S(2)}, u32[]{:S(2)}) collective-permute-start(f32[64,1664]{1,0:T(8,128)S(1)} %get-tuple-element.49), channel_id=1, source_target_pairs={{0,16},{16,0},{32,48},{48,32},{64,80},{80,64},{96,112},{112,96},{1... | collective-permute-start | bytes 1277960 | tf_op jit(solution)/shard_map/ppermute | solution.py:455
  18.5 4.5 %collective-permute-start = (f32[64,1664]{1,0:T(8,128)S(1)}, f32[64,1664]{1,0:T(8,128)S(1)}, u32[]{:S(2)}, u32[]{:S(2)}) collective-permute-start(f32[64,1664]{1,0:T(8,128)S(1)} %get-tuple-element.42), channel_id=1, source_target_pairs={{0,16},{16,0},{32,48},{48,32},{64,80},{80,64},{96,112},{112,96},{1... | collective-permute-start | bytes 1277960 | tf_op jit(solution)/shard_map/ppermute | solution.py:455
  22.4 2.0 %collective-permute-start.1 = (f32[64,1664]{1,0:T(8,128)S(1)}, f32[64,1664]{1,0:T(8,128)S(1)}, u32[]{:S(2)}, u32[]{:S(2)}) collective-permute-start(f32[64,1664]{1,0:T(8,128)S(1)} %get-tuple-element.47), channel_id=1, source_target_pairs={{0,16},{16,0},{32,48},{48,32},{64,80},{80,64},{96,112},{112,96},{1... | collective-permute-start | bytes 1277960 | tf_op jit(solution)/shard_map/ppermute | solution.py:455
  25.3 15.5 %all-to-all-start = ((bf16[8,8,4992]{2,1,0:T(8,128)(2,1)}), bf16[8,8,4992]{2,1,0:T(8,128)(2,1)S(1)}, u32[]{:S(2)}, u32[]{:S(2)}) async-start(bf16[8,8,4992]{2,1,0:T(8,128)(2,1)} %maximum_bitcast_fusion.after_ref), calls=%async_computation | async-start | bytes 1277952 | tf_op jit(solution)/shard_map/all_to_all | solution.py:459
  41.8 16.8 %all-to-all-start.1 = ((bf16[8,8,4992]{2,1,0:T(8,128)(2,1)}), bf16[8,8,4992]{2,1,0:T(8,128)(2,1)S(1)}, u32[]{:S(2)}, u32[]{:S(2)}) async-start(bf16[8,8,4992]{2,1,0:T(8,128)(2,1)} %broadcast_in_dim.4.after_ref), calls=%async_computation.1 | async-start | bytes 1277952 | tf_op jit(solution)/shard_map/all_to_all | solution.py:459
  58.6 13.0 %collective-permute-start.3 = (bf16[64,3328]{1,0:T(8,128)(2,1)S(1)}, bf16[64,3328]{1,0:T(8,128)(2,1)S(1)}, u32[]{:S(2)}, u32[]{:S(2)}) collective-permute-start(bf16[64,3328]{1,0:T(8,128)(2,1)S(1)} %slice.39.near_ref), channel_id=1, source_target_pairs={{0,16},{16,0},{32,48},{48,32},{64,80},{80,64},{96,112},{112,96},{1... | collective-permute-start | bytes 1277960 | tf_op jit(solution)/shard_map/ppermute | solution.py:455
  59.9 1.7 %collective-permute-start.4 = (bf16[64,1664]{1,0:T(8,128)(2,1)S(1)}, bf16[64,1664]{1,0:T(8,128)(2,1)S(1)}, u32[]{:S(2)}, u32[]{:S(2)}) collective-permute-start(bf16[64,1664]{1,0:T(8,128)(2,1)S(1)} %slice.40.refs_0_), channel_id=1, source_target_pairs={{0,16},{16,0},{32,48},{48,32},{64,80},{80,64},{96,112},{112,96},{1... | collective-permute-start | bytes 638984 | tf_op jit(solution)/shard_map/ppermute | solution.py:455
  76.7 6.3 %collective-permute-start.5 = (bf16[96,1024]{1,0:T(8,128)(2,1)S(1)}, bf16[96,1024]{1,0:T(8,128)(2,1)S(1)}, u32[]{:S(2)}, u32[]{:S(2)}) collective-permute-start(bf16[96,1024]{1,0:T(8,128)(2,1)S(1)} %get-tuple-element.60.after_ref), channel_id=1, source_target_pairs={{0,1},{1,0},{2,3},{3,2},{4,5},{5,4},{6,7},{7,6},{8,9},{9,8},{10,11... | collective-permute-start | bytes 589832 | tf_op jit(solution)/shard_map/ppermute | solution.py:478
  86.7 2.2 %collective-permute-start.9 = (f32[16,1664]{1,0:T(8,128)S(1)}, f32[16,1664]{1,0:T(8,128)S(1)}, u32[]{:S(2)}, u32[]{:S(2)}) collective-permute-start(f32[16,1664]{1,0:T(8,128)S(1)} %broadcast_select_fusion), channel_id=1, source_target_pairs={{0,16},{16,0},{32,48},{48,32},{64,80},{80,64},{96,112},{112,96},{1... | collective-permute-start | bytes 319496 | tf_op jit(solution)/shard_map/ppermute | solution.py:455
  89.7 26.3 %all-to-all-start.2 = ((bf16[8,16,1664]{2,1,0:T(8,128)(2,1)}), bf16[8,16,1664]{2,1,0:T(8,128)(2,1)S(1)}, u32[]{:S(2)}, u32[]{:S(2)}) async-start(bf16[8,16,1664]{2,1,0:T(8,128)(2,1)} %broadcast_in_dim.5), calls=%async_computation.2 | async-start | bytes 851968 | tf_op jit(solution)/shard_map/all_to_all | solution.py:459
  95.1 5.9 %collective-permute-start.6 = (bf16[64,1024]{1,0:T(8,128)(2,1)S(1)}, bf16[64,1024]{1,0:T(8,128)(2,1)S(1)}, u32[]{:S(2)}, u32[]{:S(2)}) collective-permute-start(bf16[64,1024]{1,0:T(8,128)(2,1)S(1)} %get-tuple-element.63.after_ref), channel_id=1, source_target_pairs={{0,2},{1,3},{2,0},{3,1},{4,6},{5,7},{6,4},{7,5},{8,10},{9,11},{10,... | collective-permute-start | bytes 393224 | tf_op jit(solution)/shard_map/ppermute | solution.py:478
  101.0 6.7 %collective-permute-start.7 = (bf16[48,1024]{1,0:T(8,128)(2,1)S(1)}, bf16[48,1024]{1,0:T(8,128)(2,1)S(1)}, u32[]{:S(2)}, u32[]{:S(2)}) collective-permute-start(bf16[48,1024]{1,0:T(8,128)(2,1)S(1)} %get-tuple-element.66), channel_id=1, source_target_pairs={{0,4},{1,5},{2,6},{3,7},{4,0},{5,1},{6,2},{7,3},{8,12},{9,13},{10,... | collective-permute-start | bytes 294920 | tf_op jit(solution)/shard_map/ppermute | solution.py:478
  107.8 7.6 %collective-permute-start.8 = (bf16[48,1024]{1,0:T(8,128)(2,1)S(1)}, bf16[48,1024]{1,0:T(8,128)(2,1)S(1)}, u32[]{:S(2)}, u32[]{:S(2)}) collective-permute-start(bf16[48,1024]{1,0:T(8,128)(2,1)S(1)} %get-tuple-element.68), channel_id=1, source_target_pairs={{0,8},{1,9},{2,10},{3,11},{4,12},{5,13},{6,14},{7,15},{8,0},{9,1},... | collective-permute-start | bytes 294920 | tf_op jit(solution)/shard_map/ppermute | solution.py:478
  116.1 5.3 %collective-permute-start.10 = (f32[16,1664]{1,0:T(8,128)S(1)}, f32[16,1664]{1,0:T(8,128)S(1)}, u32[]{:S(2)}, u32[]{:S(2)}) collective-permute-start(f32[16,1664]{1,0:T(8,128)S(1)} %add_bitcast_fusion.1), channel_id=1, source_target_pairs={{0,16},{16,0},{32,48},{48,32},{64,80},{80,64},{96,112},{112,96},{1... | collective-permute-start | bytes 319496 | tf_op jit(solution)/shard_map/ppermute | solution.py:455

commit v2 on v1

--- a/solution.py
+++ b/solution.py
@@ -44,8 +44,8 @@
     return lax.broadcasted_iota(I32, (size, size), 0), lax.broadcasted_iota(I32, (size, size), 1)
 
 
-def one_hot(hits, dtype=BF16):
-    return jnp.where(hits, 1.0, 0.0).astype(dtype)
+def one_hot(hits):
+    return jnp.where(hits, 1.0, 0.0).astype(BF16)
 
 
 def split_matrix(block):
@@ -54,10 +54,10 @@
     return one_hot(source == jnp.where(target < half, 2 * target, 2 * (target - half) + 1))
 
 
-def merge_matrix(block, dtype=BF16):
+def merge_matrix(block):
     source, target = iotas(block)
     half = block // 2
-    return one_hot(target == jnp.where(source < half, 2 * source, 2 * (source - half) + 1), dtype)
+    return one_hot(target == jnp.where(source < half, 2 * source, 2 * (source - half) + 1))
 
 
 def token_of(row, core):
@@ -147,11 +147,14 @@
     ordered_ref[...] = dot(to_rows(place_ref[0]), raw_ref[...]).astype(BF16)
     store = pltpu.make_async_copy(ordered_ref, ordered_hbm, sem)
     store.start()
+    merge = {rows: merge_matrix(2 * rows) for _, rows in blocks_of(words, LANES)}
     for load, (at, rows) in zip(loads, blocks_of(words, LANES)):
         load.wait()
         decode_rows(index_ref, table_ref, weight_ref, at, rows)
         hidden = dot_nt(ordered_ref[...], weight_ref[: 2 * rows, :])
-        hidden = jnp.dot(hidden, merge_matrix(2 * rows, F32), precision=lax.Precision.HIGHEST, preferred_element_type=F32)
+        coarse = hidden.astype(BF16)
+        fine = (hidden - coarse.astype(F32)).astype(BF16)
+        hidden = dot(coarse, merge[rows]) + dot(fine, merge[rows])
         near_ref[:, 2 * at : 2 * (at + rows)] = hidden[:HALF]
         far_ref[:, 2 * at : 2 * (at + rows)] = hidden[HALF:]
     store.wait()
@@ -238,47 +241,70 @@
     )(*([place] * first + [x, index, table] + in_hbm(*[later_index] * first)))
 
 
-def entry_sums_kernel(x_ref, index_ref, after_ref, out_ref, entry_ref):
-    words = index_ref.shape[0]
-    for row in range(0, words, 16):
-        word = index_ref[row : row + 16, :]
-        to = row // LANES * WIDE + row % LANES
-        entry_ref[to : to + 16, :] = (word & 15).astype(jnp.int16)
-        entry_ref[to + LANES : to + LANES + 16, :] = ((word >> 4) & 15).astype(jnp.int16)
+def entry_sums_kernel(x_ref, left_ref, right_ref, last_ref, after_ref, out_ref, entry_ref):
+    words = left_ref.shape[0]
+
+    def unpack(half_ref, cols):
+        for row in range(0, words, 16):
+            word = half_ref[row : row + 16, :]
+            to = row // LANES * WIDE + row % LANES
+            entry_ref[to : to + 16, cols] = (word & 15).astype(jnp.int16)
+            entry_ref[to + LANES : to + LANES + 16, cols] = ((word >> 4) & 15).astype(jnp.int16)
+
+    last = pl.program_id(0) == pl.num_programs(0) - 1
+    unpack(left_ref, slice(0, LANES))
+    pl.when(jnp.logical_not(last))(lambda: unpack(right_ref, slice(LANES, WIDE)))
+    pl.when(last)(lambda: unpack(last_ref, slice(LANES, WIDE)))
+    x = x_ref[...]
     one, zero = jnp.ones((), BF16), jnp.zeros((), BF16)
-    for entry in range(ENTRIES):
+    rest = jnp.sum(x.astype(F32), axis=1, keepdims=True)
+    for entry in range(ENTRIES - 1):
         chosen = jnp.where(entry_ref[...] == jnp.int16(entry), one, zero)
-        out_ref[entry] = dot(x_ref[...], chosen).astype(BF16)
-
-
-def entry_sums(x, index, after):
-    words, width = index.shape
+        sums = dot(x, chosen)
+        out_ref[entry] = sums.astype(BF16)
+        rest = rest - sums
+    out_ref[ENTRIES - 1] = rest.astype(BF16)
+
+
+def entry_sums(x, index, first, last_index, last, blocks, after):
+    words = index.shape[0]
+    limit = index.shape[1] // LANES - 1
     return pl.pallas_call(
         entry_sums_kernel,
-        grid=(pl.cdiv(width, WIDE),),
+        grid=(blocks,),
         in_specs=[
             pl.BlockSpec((TOKENS, 2 * words), lambda i: (0, 0)),
-            pl.BlockSpec((words, WIDE), lambda i: (0, i)),
+            pl.BlockSpec((words, LANES), lambda i: (0, first + 2 * i)),
+            pl.BlockSpec((words, LANES), lambda i: (0, jnp.minimum(first + 2 * i + 1, limit))),
+            pl.BlockSpec((words, LANES), lambda i: (0, last)),
             ANYWHERE,
         ],
         out_specs=pl.BlockSpec((ENTRIES, TOKENS, WIDE), lambda i: (0, 0, i)),
-        out_shape=shape((ENTRIES, TOKENS, width), BF16),
+        out_shape=shape((ENTRIES, TOKENS, blocks * WIDE), BF16),
         scratch_shapes=[pltpu.VMEM((2 * words, WIDE), jnp.int16)],
         compiler_params=params(60),
         cost_estimate=cost(11),
         name="entry_sums",
-    )(x, index, after)
-
-
-def table_sums_kernel(part, near_ref, far_ref, sums_hbm, after_ref, out_ref, grad_ref, sums_ref, sems):
+    )(x, index, index, last_index, after)
+
+
+def table_sums_kernel(part, pieces, near_ref, far_ref, *refs):
+    sums_hbm = refs[: len(pieces)]
+    after_ref, out_ref, grad_ref, sums_ref, sems = refs[len(pieces) :]
     count = ENTRIES // sems.shape[0]
-    loads = row_copies(sums_hbm, sums_ref, sems, count)
-    start_all(loads)
+    loads = []
+    for i in range(sems.shape[0]):
+        entries = pl.ds(i * count, count)
+        loads.append([])
+        for j, (begin, cols, to) in enumerate(pieces):
+            source = sums_hbm[j].at[entries, :, pl.ds(begin, cols)]
+            loads[i].append(pltpu.make_async_copy(source, sums_ref.at[entries, :, pl.ds(to, cols)], sems.at[i, j]))
+        start_all(loads[i])
     width = sums_ref.shape[2]
     grad_ref[:HALF, :] = near_ref[:, part * width : (part + 1) * width].astype(F32)
     grad_ref[HALF:, :] = far_ref[:, part * width : (part + 1) * width].astype(F32)
     for load, begin in zip(loads, range(0, ENTRIES, count)):
-        load.wait()
+        wait_all(load)
 
         def tile(j, carry, begin=begin):
             cols = pl.ds(pl.multiple_of(j * LANES, LANES), LANES)
@@ -295,22 +321,22 @@
         lax.fori_loop(0, width // LANES, tile, 0)
 
 
-def table_sums(near, far, part, sums, after):
-    width = sums.shape[2]
-    return pl.pallas_call(
-        functools.partial(table_sums_kernel, part),
-        in_specs=[IN_VMEM, IN_VMEM, IN_HBM, ANYWHERE],
+def table_sums(near, far, part, sums, pieces, after):
+    width = sum(cols for _, cols, _ in pieces)
+    return pl.pallas_call(
+        functools.partial(table_sums_kernel, part, pieces),
+        in_specs=[IN_VMEM, IN_VMEM] + [IN_HBM] * len(sums) + [ANYWHERE],
         out_specs=IN_VMEM,
         out_shape=pltpu.VMEM((ENTRIES, width), F32),
         scratch_shapes=[
             pltpu.VMEM((TOKENS, width), F32),
-            pltpu.VMEM(sums.shape, BF16),
-            pltpu.SemaphoreType.DMA((4,)),
+            pltpu.VMEM((ENTRIES, TOKENS, width), BF16),
+            pltpu.SemaphoreType.DMA((4, len(pieces))),
         ],
         compiler_params=params(),
         cost_estimate=cost(4.5),
         name="table_sums",
-    )(near, far, *in_hbm(sums), after)
+    )(near, far, *in_hbm(*sums), after)
 
 
 def down_bins_kernel(near_ref, far_ref, grad_hbm, index_hbm, next_hbm, out_ref, next_refs, *scratch):
@@ -421,7 +447,7 @@
     )(place, near, far, w_gate, w_up, bins)
 
 
-def add_received_kernel(kept_ref, bins_ref, back_ref, rows_ref, sums_ref, sent_ref):
+def add_received_kernel(kept_ref, bins_ref, back_ref, after_ref, rows_ref, sums_ref, sent_ref):
     bins = bins_ref[...] + (back_ref[:ENTRIES].astype(F32) + back_ref[ENTRIES : 2 * ENTRIES].astype(F32))
     rows = kept_ref[...] + back_ref[2 * ENTRIES :].astype(F32)
     rows_ref[...] = rows[: rows_ref.shape[0]]
@@ -430,12 +456,12 @@
     sent_ref[2 * ENTRIES :] = rows[rows.shape[0] - sent_ref.shape[0] + 2 * ENTRIES :].astype(BF16)
 
 
-def add_received(kept, bins, back):
+def add_received(kept, bins, back, after):
     rows, width = kept.shape
     half = max(rows // 2, 16)
     return pl.pallas_call(
         add_received_kernel,
-        in_specs=[IN_VMEM] * 3,
+        in_specs=[IN_VMEM] * 3 + [ANYWHERE],
         out_specs=[IN_VMEM] * 3,
         out_shape=[
             pltpu.VMEM((half, width), F32),
@@ -445,7 +471,7 @@
         compiler_params=params(),
         cost_estimate=cost(0.7),
         name="add_received",
-    )(kept, bins, back)
+    )(kept, bins, back, after)
 
 
 ONE_CORE = [[2 * place + core for place in range(8)] for core in range(2)]
@@ -467,11 +493,40 @@
     return functools.reduce(jnp.add, [a.astype(F32) for a in arrays])
 
 
-def sum_inp(gate, up, core):
-    own = jnp.where(core == 0, gate, up) + other_core(jnp.where(core == 0, up, gate))
-    own = total(exchange_inp(copies(own.astype(BF16), 8)))
-    other = other_core(own)
-    return jnp.where(core == 0, own, other), jnp.where(core == 0, other, own)
+def choose_kernel(place_ref, gate_ref, up_ref, after_ref, own_ref, other_ref):
+    gate_here = place_ref[0] == 0
+    own_ref[...] = jnp.where(gate_here, gate_ref[...], up_ref[...])
+    other_ref[...] = jnp.where(gate_here, up_ref[...], gate_ref[...])
+
+
+def choose(place, gate, up, after):
+    return pl.pallas_call(
+        choose_kernel,
+        in_specs=[SCALAR, IN_VMEM, IN_VMEM, ANYWHERE],
+        out_specs=[IN_VMEM] * 2,
+        out_shape=[pltpu.VMEM(gate.shape, F32)] * 2,
+        compiler_params=params(),
+        cost_estimate=cost(0.7),
+        name="choose",
+    )(place, gate, up, after)
+
+
+def add_and_copy_kernel(own_ref, back_ref, after_ref, out_ref):
+    both = (own_ref[...] + back_ref[...]).astype(BF16)
+    for place in range(out_ref.shape[0]):
+        out_ref[place] = both
+
+
+def add_and_copy(own, back, after):
+    return pl.pallas_call(
+        add_and_copy_kernel,
+        in_specs=[IN_VMEM] * 2 + [ANYWHERE],
+        out_specs=IN_VMEM,
+        out_shape=shape((8,) + own.shape, BF16),
+        compiler_params=params(),
+        cost_estimate=cost(0.7),
+        name="add_and_copy",
+    )(own, back, after)
 
 
 def other_hid(array, bit):
@@ -505,13 +560,14 @@
         axis=1,
     ).reshape(8, 8, 3 * width)
     pieces = exchange_inp(pair_sums)
-    gate_sums = entry_sums(x, gate_index, pair_sums)
+    columns = width // LANES
+    gate_sums = entry_sums(x, gate_index, 0, up_index, 0, (columns + 1) // 2, pair_sums)
     pieces, gate_sums = lax.optimization_barrier((pieces, gate_sums))
     pre = total(pieces)
     activ, gate_grad, up_grad = local_hidden(pre[:, :width], pre[:, width : 2 * width], pre[:, 2 * width :])
     grads = copies(jnp.concatenate([gate_grad, up_grad, activ], axis=1), 8)
     near = exchange_inp(grads)
-    up_sums = entry_sums(x, up_index, grads)
+    up_sums = entry_sums(x, up_index, 1, up_index, columns - 1, columns // 2, grads)
     near, up_sums = lax.optimization_barrier((near, up_sums))
     near = near.reshape(TOKENS // 2, 3 * width)
     activ_near, grad_near = near[:, 2 * width :], near[:, : 2 * width]
@@ -519,12 +575,17 @@
 
     down_sum, w_gate, w_up = down_bins(activ_near, activ_far, grad, down_index, (w_gate, w_up))
     kept, sent = input_grads(place, grad_near, grad_far, w_gate, w_up, down_sum)
-    gate_part = table_sums(grad_near, grad_far, 0, gate_sums, sent)
-    kept, down_sum, sent = add_received(kept, down_sum, other_hid(sent, 1))
-    up_part = table_sums(grad_near, grad_far, 1, up_sums, sent)
-    gate_sum, up_sum = sum_inp(gate_part, up_part, core)
-    kept, down_sum, sent = add_received(kept, down_sum, other_hid(sent, 2))
-    kept, down_sum, sent = add_received(kept, down_sum, other_hid(sent, 4))
+    gate_part = table_sums(grad_near, grad_far, 0, [gate_sums], [(0, width, 0)], sent)
+    kept, down_sum, sent = add_received(kept, down_sum, other_hid(sent, 1), gate_part)
+    pieces = [(width, LANES, 0), (0, width - LANES, LANES)]
+    up_part = table_sums(grad_near, grad_far, 1, [gate_sums, up_sums], pieces, sent)
+    kept, down_sum, sent = add_received(kept, down_sum, other_hid(sent, 2), up_part)
+    own, other = choose(place, gate_part, up_part, sent)
+    back = other_core(other)
+    kept, down_sum, sent = add_received(kept, down_sum, other_hid(sent, 4), back)
+    own = total(exchange_inp(add_and_copy(own, back, sent)))
+    other = other_core(own)
+    gate_sum, up_sum = jnp.where(core == 0, own, other), jnp.where(core == 0, other, own)
     back = other_hid(sent, 8).astype(F32)
     input_grad = (kept[:8] + back[2 * ENTRIES + 8 :]).astype(BF16)
     down_sum = down_sum + (back[:ENTRIES] + back[ENTRIES : 2 * ENTRIES])

time: 123 us -> 122 us (level)
  starting transfers between devices: 37.9 us -> 35.3 us
  waiting for transfers between devices: 14.5 us -> 16 us
    ppermute x4, waiting for transfers between devices: 10.5 us -> 12.9 us  [other_hid(): return lax.ppermute(array, 'hid', [(i, i ^ bit) for i in range(16)])]
    ppermute x7, starting transfers between devices: 11.2 us -> 9.84 us  [other_core(): return lax.ppermute(array, 'inp', [(i, i ^ 1) for i in range(16)])]
    pallas_call x7 -> x9, Pallas kernels: 30.7 us -> 31.5 us  [the longest x2 22.7 us: entry_sums(): pl.pallas_call(entry_sums_kernel, grid=(blocks,), in_specs=[pl.BlockSpec(...]
  transfers between devices with their start and end apart: 14 -> 14, of which waited for: 8 -> 6; matrix products, arithmetic and copies ran while one was open for 1% -> 1% of each run, Pallas kernels for 37% -> 40%
where the time goes in v2:
time: 122 us; the launch traced here: 120 us
  Pallas kernels  63.9 us (52%)
  starting transfers between devices  35.3 us (29%)
  waiting for transfers between devices  16 us (13%)
  other arithmetic  3.32 us (3%)
    pallas_call x2, Pallas kernels, entry_sums(): pl.pallas_call(entry_sums_kernel, grid=(blocks,), in_specs=[pl.BlockSpec(...  22.7 us
    all_to_all x3, starting transfers between devices, exchange_inp(): lax.all_to_all(pieces, 'inp', 0, 0, tiled=True, axis_index_groups=ONE_CORE)  13.5 us
    ppermute x4, waiting for transfers between devices, other_hid(): return lax.ppermute(array, 'hid', [(i, i ^ bit) for i in range(16)])  12.9 us
    ppermute x4, starting transfers between devices, other_hid(): return lax.ppermute(array, 'hid', [(i, i ^ bit) for i in range(16)])  12 us
    pallas_call x1, Pallas kernels, down_bins(): pl.pallas_call(kernel, in_specs=[IN_VMEM] * 2 + [IN_HBM] * (2 + count), o...  9.91 us
    ppermute x7, starting transfers between devices, other_core(): return lax.ppermute(array, 'inp', [(i, i ^ 1) for i in range(16)])  9.84 us
    pallas_call x1, Pallas kernels, forward_down(): pl.pallas_call(kernel, in_specs=[SCALAR] + [IN_HBM] * (3 + count), out_sp...  8.92 us
    pallas_call x2, Pallas kernels, forward_up(): pl.pallas_call(functools.partial(forward_up_kernel, first), in_specs=[SCA...  8.48 us
  transfers between devices with their start and end apart: 14, of which 6 were waited for; matrix products, arithmetic and copies ran while one was open for 1% of the time, Pallas kernels for 40%

profile of v2, /device:TPU:1, one launch (start us, length us, event | category | flops | bytes accessed | tf_op | source)
XLA Modules:
  0.0 120.3 jit_solution(2167082919502528242)
XLA Ops:
  0.6 0.1 pad_add_fusion.refs_0_.place_ref
  0.7 8.9 %forward_down.1 = (f32[64,1664]{1,0:T(8,128)S(1)}, f32[64,1664]{1,0:T(8,128)S(1)}, bf16[128,1024]{1,0:T(8,128)(2,1)}, bf16[128,1024]{1,0:T(8,128)(2,1)S(1)}, s32...) custom-call(s32[2]{0:T(128)S(1)} %pad_add_fusion.refs_0_.place_ref, ...), custom_call_target="tpu_custom_call" | custom-call | bytes 15000000 | tf_op jit(solution)/shard_map/forward_down/pallas_call | solution.py:171
  9.6 3.3 %collective-permute-start.2 = (f32[64,1664]{1,0:T(8,128)S(1)}, f32[64,1664]{1,0:T(8,128)S(1)}, u32[]{:S(2)}, u32[]{:S(2)}) collective-permute-start(f32[64,1664]{1,0:T(8,128)S(1)} %get-tuple-element.51), channel_id=1, source_target_pairs={{0,16},{16,0},{32,48},{48,32},{64,80},{80,64},{96,112},{112,96},{1... | collective-permute-start | bytes 1277960 | tf_op jit(solution)/shard_map/ppermute | solution.py:481
  13.0 4.7 %forward_gate.1 = (f32[64,1664]{1,0:T(8,128)S(1)}, f32[64,1664]{1,0:T(8,128)S(1)}, bf16[1024,1664]{1,0:T(8,128)(2,1)}, bf16[128,1024]{1,0:T(8,128)(2,1)S(1)}, bf...) custom-call(s32[2]{0:T(128)S(1)} %pad_add_fusion.refs_0_.place_ref, bf16[128,1024]{1,0:T(8,128)(2,1)S(1)} %get-tuple-element.40.refs_1_, ...), custom_call_target="tpu_custom_call" | custom-call | bytes 15000000 | tf_op jit(solution)/shard_map/forward_gate/pallas_call | solution.py:226
  17.7 0.1 collective-permute-start
  17.8 3.8 %forward_up.1 = (f32[64,1664]{1,0:T(8,128)S(1)}, f32[64,1664]{1,0:T(8,128)S(1)}, bf16[1024,1664]{1,0:T(8,128)(2,1)}) custom-call(bf16[128,1024]{1,0:T(8,128)(2,1)S(1)} %get-tuple-element.45.refs_0_, s32[512,1664]{1,0:T(8,128)S(1)} %get-tuple-element.46.refs_1_, f32[16,1664]{1,0:T(8,128)S(1)} %get-tuple-element.47.refs_2_), custom_call_target="tpu_custom_call" | custom-call | bytes 15000000 | tf_op jit(solution)/shard_map/forward_up/pallas_call | solution.py:226
  21.6 0.6 collective-permute-start.1
  22.1 0.0 collective-permute-done.2
  22.2 0.0 collective-permute-done
  22.3 1.3 %collective-permute-done.1 = f32[64,1664]{1,0:T(8,128)S(1)} collective-permute-done((f32[64,1664]{1,0:T(8,128)S(1)}, f32[64,1664]{1,0:T(8,128)S(1)}, u32[]{:S(2)}, u32[]{:S(2)}) %collective-permute-start.1) | collective-permute-done | bytes 426016 | tf_op jit(solution)/shard_map/ppermute | solution.py:481
  23.6 0.9 maximum_bitcast_fusion.after_ref
  24.5 3.8 %all-to-all-start = ((bf16[8,8,4992]{2,1,0:T(8,128)(2,1)}), bf16[8,8,4992]{2,1,0:T(8,128)(2,1)S(1)}, u32[]{:S(2)}, u32[]{:S(2)}) async-start(bf16[8,8,4992]{2,1,0:T(8,128)(2,1)} %maximum_bitcast_fusion.after_ref), calls=%async_computation | async-start | bytes 1277952 | tf_op jit(solution)/shard_map/all_to_all | solution.py:485
  28.3 12.0 %entry_sums.2.refs_0_ = bf16[16,128,1792]{2,1,0:T(8,128)(2,1)} custom-call(bf16[128,1024]{1,0:T(8,128)(2,1)} %get-tuple-element.52.x_ref, s32[512,1664]{1,0:T(8,128)} %right_ref.2, s32[512,1664]{1,0:T(8,128)} %right_ref.2, s32[512,1664]{1,0:T(8,128)} %last_ref.3, bf16[8,8,4992]{2,1,0:T(8,128)(2,1)} %maximum_bitcast_fusion.after_ref), custom_call_target="tpu_custom_call" | custom-call | bytes 33000000 | tf_op jit(solution)/shard_map/entry_sums/pallas_call | solution.py:272
  40.3 0.0 all-to-all-done
  40.3 0.1 add_bitcast_fusion
  40.5 0.9 broadcast_in_dim.2.after_ref
  41.3 5.1 %all-to-all-start.1 = ((bf16[8,8,4992]{2,1,0:T(8,128)(2,1)}), bf16[8,8,4992]{2,1,0:T(8,128)(2,1)S(1)}, u32[]{:S(2)}, u32[]{:S(2)}) async-start(bf16[8,8,4992]{2,1,0:T(8,128)(2,1)} %broadcast_in_dim.2.after_ref), calls=%async_computation.1 | async-start | bytes 1277952 | tf_op jit(solution)/shard_map/all_to_all | solution.py:485
  46.4 10.7 %entry_sums.3.refs_1_ = bf16[16,128,1536]{2,1,0:T(8,128)(2,1)} custom-call(bf16[128,1024]{1,0:T(8,128)(2,1)} %get-tuple-element.52.x_ref, s32[512,1664]{1,0:T(8,128)} %last_ref.3, s32[512,1664]{1,0:T(8,128)} %last_ref.3, s32[512,1664]{1,0:T(8,128)} %last_ref.3, bf16[8,8,4992]{2,1,0:T(8,128)(2,1)} %broadcast_in_dim.2.after_ref), custom_call_target="tpu_custom_call" | custom-call | bytes 33000000 | tf_op jit(solution)/shard_map/entry_sums/pallas_call | solution.py:272
  57.2 0.0 all-to-all-done.1
  57.2 1.6 %collective-permute-start.3 = (bf16[64,3328]{1,0:T(8,128)(2,1)S(1)}, bf16[64,3328]{1,0:T(8,128)(2,1)S(1)}, u32[]{:S(2)}, u32[]{:S(2)}) collective-permute-start(bf16[64,3328]{1,0:T(8,128)(2,1)S(1)} %slice.39.near_ref), channel_id=1, source_target_pairs={{0,16},{16,0},{32,48},{48,32},{64,80},{80,64},{96,112},{112,96},{1... | collective-permute-start | bytes 1277960 | tf_op jit(solution)/shard_map/ppermute | solution.py:481
  58.8 0.3 collective-permute-start.4
  59.1 1.4 %collective-permute-done.4.refs_1_ = bf16[64,1664]{1,0:T(8,128)(2,1)S(1)} collective-permute-done((bf16[64,1664]{1,0:T(8,128)(2,1)S(1)}, bf16[64,1664]{1,0:T(8,128)(2,1)S(1)}, u32[]{:S(2)}, u32[]{:S(2)}) %collective-permute-start.4) | collective-permute-done | bytes 213024 | tf_op jit(solution)/shard_map/ppermute | solution.py:481
  60.6 9.9 %down_bins.1 = (f32[16,1024]{1,0:T(8,128)S(1)}, bf16[1024,1664]{1,0:T(8,128)(2,1)S(1)}, bf16[1024,1664]{1,0:T(8,128)(2,1)S(1)}) custom-call(bf16[64,1664]{1,0:T(8,128)(2,1)S(1)} %slice.40.refs_0_, bf16[64,1664]{1,0:T(8,128)(2,1)S(1)} %collective-permute-done.4.refs_1_, bf16[128,1024]{1,0:T(8,128)(2,1)} %get-tuple-element.55.refs_2_, s32[832,1024]{1,0:T(8,128)} %refs_3_.3, ...), custom_call_target="tpu_custom_call" | custom-call | bytes 30000000 | tf_op jit(solution)/shard_map/down_bins/pallas_call | solution.py:397
  70.5 0.0 collective-permute-done.3.far_ref
  70.5 5.1 %input_grad.1 = (f32[64,1024]{1,0:T(8,128)S(1)}, bf16[96,1024]{1,0:T(8,128)(2,1)S(1)}) custom-call(s32[2]{0:T(128)S(1)} %pad_add_fusion.refs_0_.place_ref, bf16[64,3328]{1,0:T(8,128)(2,1)S(1)} %slice.39.near_ref, bf16[64,3328]{1,0:T(8,128)(2,1)S(1)} %collective-permute-done.3.far_ref, bf16[1024,1664]{1,0:T(8,128)(2,1)S(1)} %get-tuple-element.58.wg_ref, ...), custom_call_target="tpu_custom_call" | custom-call | bytes 10500000 | tf_op jit(solution)/shard_map/input_grad/pallas_call | solution.py:439
  75.6 1.3 %collective-permute-start.5 = (bf16[96,1024]{1,0:T(8,128)(2,1)S(1)}, bf16[96,1024]{1,0:T(8,128)(2,1)S(1)}, u32[]{:S(2)}, u32[]{:S(2)}) collective-permute-start(bf16[96,1024]{1,0:T(8,128)(2,1)S(1)} %get-tuple-element.62.refs_1_), channel_id=1, source_target_pairs={{0,1},{1,0},{2,3},{3,2},{4,5},{5,4},{6,7},{7,6},{8,9},{9,8},{10,11... | collective-permute-start | bytes 589832 | tf_op jit(solution)/shard_map/ppermute | solution.py:533
  76.9 3.6 %table_sums.2.after_ref.gate_ref = f32[16,1664]{1,0:T(8,128)S(1)} custom-call(bf16[64,3328]{1,0:T(8,128)(2,1)S(1)} %slice.39.near_ref, bf16[64,3328]{1,0:T(8,128)(2,1)S(1)} %collective-permute-done.3.far_ref, bf16[16,128,1792]{2,1,0:T(8,128)(2,1)} %entry_sums.2.refs_0_, bf16[96,1024]{1,0:T(8,128)(2,1)S(1)} %get-tuple-element.62.refs_1_), custom_call_target="tpu_custom_call" | custom-call | bytes 13500000 | tf_op jit(solution)/shard_map/table_sums/pallas_call | solution.py:326
  80.6 1.3 %collective-permute-done.5.back_ref = bf16[96,1024]{1,0:T(8,128)(2,1)S(1)} collective-permute-done((bf16[96,1024]{1,0:T(8,128)(2,1)S(1)}, bf16[96,1024]{1,0:T(8,128)(2,1)S(1)}, u32[]{:S(2)}, u32[]{:S(2)}) %collective-permute-start.5) | collective-permute-done | bytes 196640 | tf_op jit(solution)/shard_map/ppermute | solution.py:533
  81.9 2.8 %collective-permute-start.6 = (bf16[64,1024]{1,0:T(8,128)(2,1)S(1)}, bf16[64,1024]{1,0:T(8,128)(2,1)S(1)}, u32[]{:S(2)}, u32[]{:S(2)}) collective-permute-start(bf16[64,1024]{1,0:T(8,128)(2,1)S(1)} %get-tuple-element.66.refs_2_), channel_id=1, source_target_pairs={{0,2},{1,3},{2,0},{3,1},{4,6},{5,7},{6,4},{7,5},{8,10},{9,11},{10,... | collective-permute-start | bytes 393224 | tf_op jit(solution)/shard_map/ppermute | solution.py:533
  84.8 3.7 %table_sums.3.after_ref.up_ref = f32[16,1664]{1,0:T(8,128)S(1)} custom-call(bf16[64,3328]{1,0:T(8,128)(2,1)S(1)} %slice.39.near_ref, bf16[64,3328]{1,0:T(8,128)(2,1)S(1)} %collective-permute-done.3.far_ref, bf16[16,128,1792]{2,1,0:T(8,128)(2,1)} %entry_sums.2.refs_0_, bf16[16,128,1536]{2,1,0:T(8,128)(2,1)} %entry_sums.3.refs_1_, ...), custom_call_target="tpu_custom_call" | custom-call | bytes 13500000 | tf_op jit(solution)/shard_map/table_sums/pallas_call | solution.py:326
  88.5 0.0 collective-permute-done.6.back_ref
  88.5 0.6 choose.1
  89.1 1.5 %collective-permute-start.8 = (f32[16,1664]{1,0:T(8,128)S(1)}, f32[16,1664]{1,0:T(8,128)S(1)}, u32[]{:S(2)}, u32[]{:S(2)}) collective-permute-start(f32[16,1664]{1,0:T(8,128)S(1)} %get-tuple-element.71), channel_id=1, source_target_pairs={{0,16},{16,0},{32,48},{48,32},{64,80},{80,64},{96,112},{112,96},{1... | collective-permute-start | bytes 319496 | tf_op jit(solution)/shard_map/ppermute | solution.py:481
  90.6 3.0 %collective-permute-start.7 = (bf16[48,1024]{1,0:T(8,128)(2,1)S(1)}, bf16[48,1024]{1,0:T(8,128)(2,1)S(1)}, u32[]{:S(2)}, u32[]{:S(2)}) collective-permute-start(bf16[48,1024]{1,0:T(8,128)(2,1)S(1)} %get-tuple-element.70.after_ref), channel_id=1, source_target_pairs={{0,4},{1,5},{2,6},{3,7},{4,0},{5,1},{6,2},{7,3},{8,12},{9,13},{10,... | collective-permute-start | bytes 294920 | tf_op jit(solution)/shard_map/ppermute | solution.py:533
  93.6 5.2 %collective-permute-done.7.back_ref = bf16[48,1024]{1,0:T(8,128)(2,1)S(1)} collective-permute-done((bf16[48,1024]{1,0:T(8,128)(2,1)S(1)}, bf16[48,1024]{1,0:T(8,128)(2,1)S(1)}, u32[]{:S(2)}, u32[]{:S(2)}) %collective-permute-start.7) | collective-permute-done | bytes 98336 | tf_op jit(solution)/shard_map/ppermute | solution.py:533
  98.8 0.0 collective-permute-done.8.after_ref.back_ref
  98.8 0.8 add_and_copy.1
  99.6 4.6 %all-to-all-start.2 = ((bf16[8,16,1664]{2,1,0:T(8,128)(2,1)}), bf16[8,16,1664]{2,1,0:T(8,128)(2,1)S(1)}, u32[]{:S(2)}, u32[]{:S(2)}) async-start(bf16[8,16,1664]{2,1,0:T(8,128)(2,1)} %add_and_copy.1), calls=%async_computation.2 | async-start | bytes 851968 | tf_op jit(solution)/shard_map/all_to_all | solution.py:485
  104.2 4.8 %collective-permute-start.9 = (bf16[48,1024]{1,0:T(8,128)(2,1)S(1)}, bf16[48,1024]{1,0:T(8,128)(2,1)S(1)}, u32[]{:S(2)}, u32[]{:S(2)}) collective-permute-start(bf16[48,1024]{1,0:T(8,128)(2,1)S(1)} %get-tuple-element.73.after_ref), channel_id=1, source_target_pairs={{0,8},{1,9},{2,10},{3,11},{4,12},{5,13},{6,14},{7,15},{8,0},{9,1},... | collective-permute-start | bytes 294920 | tf_op jit(solution)/shard_map/ppermute | solution.py:533
  109.0 6.5 %collective-permute-done.9 = bf16[48,1024]{1,0:T(8,128)(2,1)S(1)} collective-permute-done((bf16[48,1024]{1,0:T(8,128)(2,1)S(1)}, bf16[48,1024]{1,0:T(8,128)(2,1)S(1)}, u32[]{:S(2)}, u32[]{:S(2)}) %collective-permute-start.9) | collective-permute-done | bytes 98336 | tf_op jit(solution)/shard_map/ppermute | solution.py:533
  115.5 0.6 fusion.1
  116.1 0.0 all-to-all-done.2
  116.1 0.1 add_bitcast_fusion.1
  116.2 2.4 %collective-permute-start.10 = (f32[16,1664]{1,0:T(8,128)S(1)}, f32[16,1664]{1,0:T(8,128)S(1)}, u32[]{:S(2)}, u32[]{:S(2)}) collective-permute-start(f32[16,1664]{1,0:T(8,128)S(1)} %add_bitcast_fusion.1), channel_id=1, source_target_pairs={{0,16},{16,0},{32,48},{48,32},{64,80},{80,64},{96,112},{112,96},{1... | collective-permute-start | bytes 319496 | tf_op jit(solution)/shard_map/ppermute | solution.py:481
  118.6 0.6 fusion.3
  119.2 0.3 collective-permute-done.10
  119.6 0.8 select_multiply_fusion
  (11 shorter events, 0.4 us)
Async XLA Ops:
  9.6 12.5 %collective-permute-start.2 = (f32[64,1664]{1,0:T(8,128)S(1)}, f32[64,1664]{1,0:T(8,128)S(1)}, u32[]{:S(2)}, u32[]{:S(2)}) collective-permute-start(f32[64,1664]{1,0:T(8,128)S(1)} %get-tuple-element.51), channel_id=1, source_target_pairs={{0,16},{16,0},{32,48},{48,32},{64,80},{80,64},{96,112},{112,96},{1... | collective-permute-start | bytes 1277960 | tf_op jit(solution)/shard_map/ppermute | solution.py:481
  17.7 4.5 %collective-permute-start = (f32[64,1664]{1,0:T(8,128)S(1)}, f32[64,1664]{1,0:T(8,128)S(1)}, u32[]{:S(2)}, u32[]{:S(2)}) collective-permute-start(f32[64,1664]{1,0:T(8,128)S(1)} %get-tuple-element.44), channel_id=1, source_target_pairs={{0,16},{16,0},{32,48},{48,32},{64,80},{80,64},{96,112},{112,96},{1... | collective-permute-start | bytes 1277960 | tf_op jit(solution)/shard_map/ppermute | solution.py:481
  21.6 2.0 %collective-permute-start.1 = (f32[64,1664]{1,0:T(8,128)S(1)}, f32[64,1664]{1,0:T(8,128)S(1)}, u32[]{:S(2)}, u32[]{:S(2)}) collective-permute-start(f32[64,1664]{1,0:T(8,128)S(1)} %get-tuple-element.49), channel_id=1, source_target_pairs={{0,16},{16,0},{32,48},{48,32},{64,80},{80,64},{96,112},{112,96},{1... | collective-permute-start | bytes 1277960 | tf_op jit(solution)/shard_map/ppermute | solution.py:481
  24.5 15.8 %all-to-all-start = ((bf16[8,8,4992]{2,1,0:T(8,128)(2,1)}), bf16[8,8,4992]{2,1,0:T(8,128)(2,1)S(1)}, u32[]{:S(2)}, u32[]{:S(2)}) async-start(bf16[8,8,4992]{2,1,0:T(8,128)(2,1)} %maximum_bitcast_fusion.after_ref), calls=%async_computation | async-start | bytes 1277952 | tf_op jit(solution)/shard_map/all_to_all | solution.py:485
  41.3 15.8 %all-to-all-start.1 = ((bf16[8,8,4992]{2,1,0:T(8,128)(2,1)}), bf16[8,8,4992]{2,1,0:T(8,128)(2,1)S(1)}, u32[]{:S(2)}, u32[]{:S(2)}) async-start(bf16[8,8,4992]{2,1,0:T(8,128)(2,1)} %broadcast_in_dim.2.after_ref), calls=%async_computation.1 | async-start | bytes 1277952 | tf_op jit(solution)/shard_map/all_to_all | solution.py:485
  57.2 13.3 %collective-permute-start.3 = (bf16[64,3328]{1,0:T(8,128)(2,1)S(1)}, bf16[64,3328]{1,0:T(8,128)(2,1)S(1)}, u32[]{:S(2)}, u32[]{:S(2)}) collective-permute-start(bf16[64,3328]{1,0:T(8,128)(2,1)S(1)} %slice.39.near_ref), channel_id=1, source_target_pairs={{0,16},{16,0},{32,48},{48,32},{64,80},{80,64},{96,112},{112,96},{1... | collective-permute-start | bytes 1277960 | tf_op jit(solution)/shard_map/ppermute | solution.py:481
  58.8 1.7 %collective-permute-start.4 = (bf16[64,1664]{1,0:T(8,128)(2,1)S(1)}, bf16[64,1664]{1,0:T(8,128)(2,1)S(1)}, u32[]{:S(2)}, u32[]{:S(2)}) collective-permute-start(bf16[64,1664]{1,0:T(8,128)(2,1)S(1)} %slice.40.refs_0_), channel_id=1, source_target_pairs={{0,16},{16,0},{32,48},{48,32},{64,80},{80,64},{96,112},{112,96},{1... | collective-permute-start | bytes 638984 | tf_op jit(solution)/shard_map/ppermute | solution.py:481
  75.6 6.3 %collective-permute-start.5 = (bf16[96,1024]{1,0:T(8,128)(2,1)S(1)}, bf16[96,1024]{1,0:T(8,128)(2,1)S(1)}, u32[]{:S(2)}, u32[]{:S(2)}) collective-permute-start(bf16[96,1024]{1,0:T(8,128)(2,1)S(1)} %get-tuple-element.62.refs_1_), channel_id=1, source_target_pairs={{0,1},{1,0},{2,3},{3,2},{4,5},{5,4},{6,7},{7,6},{8,9},{9,8},{10,11... | collective-permute-start | bytes 589832 | tf_op jit(solution)/shard_map/ppermute | solution.py:533
  81.9 6.5 %collective-permute-start.6 = (bf16[64,1024]{1,0:T(8,128)(2,1)S(1)}, bf16[64,1024]{1,0:T(8,128)(2,1)S(1)}, u32[]{:S(2)}, u32[]{:S(2)}) collective-permute-start(bf16[64,1024]{1,0:T(8,128)(2,1)S(1)} %get-tuple-element.66.refs_2_), channel_id=1, source_target_pairs={{0,2},{1,3},{2,0},{3,1},{4,6},{5,7},{6,4},{7,5},{8,10},{9,11},{10,... | collective-permute-start | bytes 393224 | tf_op jit(solution)/shard_map/ppermute | solution.py:533
  89.1 9.7 %collective-permute-start.8 = (f32[16,1664]{1,0:T(8,128)S(1)}, f32[16,1664]{1,0:T(8,128)S(1)}, u32[]{:S(2)}, u32[]{:S(2)}) collective-permute-start(f32[16,1664]{1,0:T(8,128)S(1)} %get-tuple-element.71), channel_id=1, source_target_pairs={{0,16},{16,0},{32,48},{48,32},{64,80},{80,64},{96,112},{112,96},{1... | collective-permute-start | bytes 319496 | tf_op jit(solution)/shard_map/ppermute | solution.py:481
  90.6 8.2 %collective-permute-start.7 = (bf16[48,1024]{1,0:T(8,128)(2,1)S(1)}, bf16[48,1024]{1,0:T(8,128)(2,1)S(1)}, u32[]{:S(2)}, u32[]{:S(2)}) collective-permute-start(bf16[48,1024]{1,0:T(8,128)(2,1)S(1)} %get-tuple-element.70.after_ref), channel_id=1, source_target_pairs={{0,4},{1,5},{2,6},{3,7},{4,0},{5,1},{6,2},{7,3},{8,12},{9,13},{10,... | collective-permute-start | bytes 294920 | tf_op jit(solution)/shard_map/ppermute | solution.py:533
  99.6 16.5 %all-to-all-start.2 = ((bf16[8,16,1664]{2,1,0:T(8,128)(2,1)}), bf16[8,16,1664]{2,1,0:T(8,128)(2,1)S(1)}, u32[]{:S(2)}, u32[]{:S(2)}) async-start(bf16[8,16,1664]{2,1,0:T(8,128)(2,1)} %add_and_copy.1), calls=%async_computation.2 | async-start | bytes 851968 | tf_op jit(solution)/shard_map/all_to_all | solution.py:485
  104.2 11.3 %collective-permute-start.9 = (bf16[48,1024]{1,0:T(8,128)(2,1)S(1)}, bf16[48,1024]{1,0:T(8,128)(2,1)S(1)}, u32[]{:S(2)}, u32[]{:S(2)}) collective-permute-start(bf16[48,1024]{1,0:T(8,128)(2,1)S(1)} %get-tuple-element.73.after_ref), channel_id=1, source_target_pairs={{0,8},{1,9},{2,10},{3,11},{4,12},{5,13},{6,14},{7,15},{8,0},{9,1},... | collective-permute-start | bytes 294920 | tf_op jit(solution)/shard_map/ppermute | solution.py:533
  116.2 3.4 %collective-permute-start.10 = (f32[16,1664]{1,0:T(8,128)S(1)}, f32[16,1664]{1,0:T(8,128)S(1)}, u32[]{:S(2)}, u32[]{:S(2)}) collective-permute-start(f32[16,1664]{1,0:T(8,128)S(1)} %add_bitcast_fusion.1), channel_id=1, source_target_pairs={{0,16},{16,0},{32,48},{48,32},{64,80},{80,64},{96,112},{112,96},{1... | collective-permute-start | bytes 319496 | tf_op jit(solution)/shard_map/ppermute | solution.py:481

commit v3 on v2

--- a/solution.py
+++ b/solution.py
@@ -69,10 +69,9 @@
     return one_hot(token == token_of(row, core))
 
 
-def to_owners(core, hid):
+def to_owners(core):
     owned, row = iotas(TOKENS)
-    bits = ((owned >> 6) & 1) | ((owned >> 4) & 2) | ((owned >> 2) & 4) | (owned & 8)
-    return one_hot(token_of(row, core) == (bits ^ hid) * 8 + (owned & 7))
+    return one_hot(token_of(row, core) == (((owned >> 3) & 3) * 4 + (owned >> 5)) * 8 + (owned & 7))
 
 
 SCALAR = pl.BlockSpec(memory_space=pltpu.SMEM)
@@ -142,14 +141,16 @@
     small = [pltpu.make_async_copy(raw_hbm, raw_ref, next_sems.at[count])]
     small.append(pltpu.make_async_copy(table_hbm, table_ref, next_sems.at[count + 1]))
     later = [pltpu.make_async_copy(a, b, next_sems.at[i]) for i, (a, b) in enumerate(zip(next_hbm, next_refs))]
-    start_all(small + loads + later)
+    start_all(small + loads)
     wait_all(small)
     ordered_ref[...] = dot(to_rows(place_ref[0]), raw_ref[...]).astype(BF16)
     store = pltpu.make_async_copy(ordered_ref, ordered_hbm, sem)
     store.start()
     merge = {rows: merge_matrix(2 * rows) for _, rows in blocks_of(words, LANES)}
-    for load, (at, rows) in zip(loads, blocks_of(words, LANES)):
+    for i, (load, (at, rows)) in enumerate(zip(loads, blocks_of(words, LANES))):
         load.wait()
+        if i == len(loads) // 2 - 1:
+            start_all(later)
         decode_rows(index_ref, table_ref, weight_ref, at, rows)
         hidden = dot_nt(ordered_ref[...], weight_ref[: 2 * rows, :])
         coarse = hidden.astype(BF16)
@@ -412,26 +413,22 @@
     )(near, far, *in_hbm(grad, index, *brought))
 
 
-def put_bins(bins, sent_ref):
-    coarse = bins.astype(BF16)
-    sent_ref[:ENTRIES] = coarse
-    sent_ref[ENTRIES : 2 * ENTRIES] = (bins - coarse.astype(F32)).astype(BF16)
-
-
-def input_grad_kernel(
-    place_ref, near_ref, far_ref, wg_ref, wu_ref, bins_ref, kept_ref, sent_ref
-):
+def input_grad_kernel(place_ref, near_ref, far_ref, wg_ref, wu_ref, bins_ref, sent_ref):
+    pieces = sent_ref.shape[0]
     rows, width = wg_ref.shape
     gate = jnp.concatenate([near_ref[:, :width], far_ref[:, :width]], axis=0)
     up = jnp.concatenate([near_ref[:, width:], far_ref[:, width:]], axis=0)
-    order = to_owners(place_ref[0], place_ref[1])
+    order = to_owners(place_ref[0])
     merge = merge_matrix(WIDE)
+    count = TOKENS // pieces
     for at in range(0, rows, WIDE):
         part = (dot_nt(gate, wg_ref[at : at + WIDE, :]) + dot_nt(up, wu_ref[at : at + WIDE, :])).astype(BF16)
-        part = dot(dot(order, part).astype(BF16), merge)
-        kept_ref[:, at : at + WIDE] = part[:HALF]
-        sent_ref[2 * ENTRIES :, at : at + WIDE] = part[HALF:].astype(BF16)
-    put_bins(bins_ref[...], sent_ref)
+        part = dot(dot(order, part).astype(BF16), merge).astype(BF16)
+        for piece in range(pieces):
+            sent_ref[piece, ENTRIES:, at : at + WIDE] = part[piece * count : (piece + 1) * count]
+    bins = bins_ref[...].astype(BF16)
+    for piece in range(pieces):
+        sent_ref[piece, :ENTRIES] = bins
 
 
 def input_grads(place, near, far, w_gate, w_up, bins):
@@ -439,39 +436,37 @@
     return pl.pallas_call(
         input_grad_kernel,
         in_specs=[SCALAR] + [IN_VMEM] * 5,
-        out_specs=[IN_VMEM] * 2,
-        out_shape=[pltpu.VMEM((HALF, width), F32), pltpu.VMEM((2 * ENTRIES + HALF, width), BF16)],
+        out_specs=IN_VMEM,
+        out_shape=shape((4, ENTRIES + TOKENS // 4, width), BF16),
         compiler_params=params(),
         cost_estimate=cost(3.5),
         name="input_grad",
     )(place, near, far, w_gate, w_up, bins)
 
 
-def add_received_kernel(kept_ref, bins_ref, back_ref, after_ref, rows_ref, sums_ref, sent_ref):
-    bins = bins_ref[...] + (back_ref[:ENTRIES].astype(F32) + back_ref[ENTRIES : 2 * ENTRIES].astype(F32))
-    rows = kept_ref[...] + back_ref[2 * ENTRIES :].astype(F32)
-    rows_ref[...] = rows[: rows_ref.shape[0]]
-    sums_ref[...] = bins
-    put_bins(bins, sent_ref)
-    sent_ref[2 * ENTRIES :] = rows[rows.shape[0] - sent_ref.shape[0] + 2 * ENTRIES :].astype(BF16)
-
-
-def add_received(kept, bins, back, after):
-    rows, width = kept.shape
-    half = max(rows // 2, 16)
-    return pl.pallas_call(
-        add_received_kernel,
-        in_specs=[IN_VMEM] * 3 + [ANYWHERE],
-        out_specs=[IN_VMEM] * 3,
-        out_shape=[
-            pltpu.VMEM((half, width), F32),
-            pltpu.VMEM(bins.shape, F32),
-            pltpu.VMEM((2 * ENTRIES + half, width), BF16),
-        ],
+def add_along_x_kernel(back_ref, after_ref, sent_ref):
+    pieces = back_ref.shape[0]
+    sums = back_ref[0].astype(F32)
+    for piece in range(1, pieces):
+        sums = sums + back_ref[piece].astype(F32)
+    bins = sums[:ENTRIES].astype(BF16)
+    for piece in range(pieces):
+        own = sums[ENTRIES + 8 * piece : ENTRIES + 8 * piece + 8]
+        sent_ref[piece, :ENTRIES] = bins
+        sent_ref[piece, ENTRIES:] = jnp.concatenate([own, own], axis=0).astype(BF16)
+
+
+def add_along_x(back, after):
+    width = back.shape[2]
+    return pl.pallas_call(
+        add_along_x_kernel,
+        in_specs=[IN_VMEM, ANYWHERE],
+        out_specs=IN_VMEM,
+        out_shape=shape((4, ENTRIES + 16, width), BF16),
         compiler_params=params(),
         cost_estimate=cost(0.7),
-        name="add_received",
-    )(kept, bins, back, after)
+        name="add_along_x",
+    )(back, after)
 
 
 ONE_CORE = [[2 * place + core for place in range(8)] for core in range(2)]
@@ -529,8 +524,12 @@
     )(own, back, after)
 
 
-def other_hid(array, bit):
-    return lax.ppermute(array, "hid", [(i, i ^ bit) for i in range(16)])
+SAME_Z = [[4 * z + x for x in range(4)] for z in range(4)]
+SAME_X = [[4 * z + x for z in range(4)] for x in range(4)]
+
+
+def exchange_hid(pieces, groups):
+    return lax.all_to_all(pieces, "hid", 0, 0, tiled=True, axis_index_groups=groups)
 
 
 def local_hidden(pre_gate, pre_up, hidden_grad):
@@ -574,21 +573,18 @@
     activ_far, grad_far = other_core(activ_near), other_core(grad_near)
 
     down_sum, w_gate, w_up = down_bins(activ_near, activ_far, grad, down_index, (w_gate, w_up))
-    kept, sent = input_grads(place, grad_near, grad_far, w_gate, w_up, down_sum)
+    sent = input_grads(place, grad_near, grad_far, w_gate, w_up, down_sum)
+    back_x = exchange_hid(sent, SAME_Z)
     gate_part = table_sums(grad_near, grad_far, 0, [gate_sums], [(0, width, 0)], sent)
-    kept, down_sum, sent = add_received(kept, down_sum, other_hid(sent, 1), gate_part)
     pieces = [(width, LANES, 0), (0, width - LANES, LANES)]
-    up_part = table_sums(grad_near, grad_far, 1, [gate_sums, up_sums], pieces, sent)
-    kept, down_sum, sent = add_received(kept, down_sum, other_hid(sent, 2), up_part)
-    own, other = choose(place, gate_part, up_part, sent)
-    back = other_core(other)
-    kept, down_sum, sent = add_received(kept, down_sum, other_hid(sent, 4), back)
-    own = total(exchange_inp(add_and_copy(own, back, sent)))
+    up_part = table_sums(grad_near, grad_far, 1, [gate_sums, up_sums], pieces, gate_part)
+    own, other = choose(place, gate_part, up_part, up_part)
+    own = total(exchange_inp(add_and_copy(own, other_core(other), back_x)))
     other = other_core(own)
     gate_sum, up_sum = jnp.where(core == 0, own, other), jnp.where(core == 0, other, own)
-    back = other_hid(sent, 8).astype(F32)
-    input_grad = (kept[:8] + back[2 * ENTRIES + 8 :]).astype(BF16)
-    down_sum = down_sum + (back[:ENTRIES] + back[ENTRIES : 2 * ENTRIES])
+    back = exchange_hid(add_along_x(back_x, own), SAME_X)
+    input_grad = total(back[:, ENTRIES : ENTRIES + 8]).astype(BF16)
+    down_sum = total(back[:, :ENTRIES])
     scale = 1.0 / TOKENS
     return input_grad, gate_sum * scale, up_sum * scale, down_sum * scale
 

time: 122 us -> 126 us (1.033)
  blocking collectives: 0 us -> 13.3 us
  starting transfers between devices: 35.3 us -> 28.5 us
  waiting for transfers between devices: 16 us -> 12.3 us
  Pallas kernels: 63.9 us -> 65.2 us
    all_to_all x0 -> x1, blocking collectives: none -> 13.3 us  [exchange_inp(): lax.all_to_all(pieces, 'inp', 0, 0, tiled=True, axis_index_groups=ONE_CORE)]
    ppermute x4 -> x0, waiting for transfers between devices: 12.9 us -> none  [other_hid(): return lax.ppermute(array, 'hid', [(i, i ^ bit) for i in range(16)])]
    ppermute x4 -> x0, starting transfers between devices: 12 us -> none  [other_hid(): return lax.ppermute(array, 'hid', [(i, i ^ bit) for i in range(16)])]
    all_to_all x0 -> x2, starting transfers between devices: none -> 11.3 us  [exchange_hid(): lax.all_to_all(pieces, 'hid', 0, 0, tiled=True, axis_index_groups=groups)]
    all_to_all x0 -> x2, waiting for transfers between devices: none -> 8.6 us  [exchange_hid(): lax.all_to_all(pieces, 'hid', 0, 0, tiled=True, axis_index_groups=groups)]
    all_to_all x3 -> x2, starting transfers between devices: 13.5 us -> 8.94 us  [exchange_inp(): lax.all_to_all(pieces, 'inp', 0, 0, tiled=True, axis_index_groups=ONE_CORE)]
    ppermute x7, starting transfers between devices: 9.84 us -> 8.27 us  [other_core(): return lax.ppermute(array, 'inp', [(i, i ^ 1) for i in range(16)])]
  transfers between devices with their start and end apart: 14 -> 11, of which waited for: 6 -> 4; matrix products, arithmetic and copies ran while one was open for 1% -> 1% of each run, Pallas kernels for 40% -> 40%
where the time goes in v3:
time: 126 us; the launch traced here: 124 us
  Pallas kernels  65.2 us (52%)
  starting transfers between devices  28.5 us (23%)
  blocking collectives  13.3 us (11%)
  waiting for transfers between devices  12.3 us (10%)
  other arithmetic  3.31 us (3%)
    pallas_call x2, Pallas kernels, entry_sums(): pl.pallas_call(entry_sums_kernel, grid=(blocks,), in_specs=[pl.BlockSpec(...  22.7 us
    all_to_all x1, blocking collectives, exchange_inp(): lax.all_to_all(pieces, 'inp', 0, 0, tiled=True, axis_index_groups=ONE_CORE)  13.3 us
    all_to_all x2, starting transfers between devices, exchange_hid(): lax.all_to_all(pieces, 'hid', 0, 0, tiled=True, axis_index_groups=groups)  11.3 us
    pallas_call x1, Pallas kernels, down_bins(): pl.pallas_call(kernel, in_specs=[IN_VMEM] * 2 + [IN_HBM] * (2 + count), o...  9.9 us
    pallas_call x1, Pallas kernels, forward_down(): pl.pallas_call(kernel, in_specs=[SCALAR] + [IN_HBM] * (3 + count), out_sp...  9.55 us
    all_to_all x2, starting transfers between devices, exchange_inp(): lax.all_to_all(pieces, 'inp', 0, 0, tiled=True, axis_index_groups=ONE_CORE)  8.94 us
    all_to_all x2, waiting for transfers between devices, exchange_hid(): lax.all_to_all(pieces, 'hid', 0, 0, tiled=True, axis_index_groups=groups)  8.6 us
    pallas_call x2, Pallas kernels, forward_up(): pl.pallas_call(functools.partial(forward_up_kernel, first), in_specs=[SCA...  8.46 us
  transfers between devices with their start and end apart: 11, of which 4 were waited for; matrix products, arithmetic and copies ran while one was open for 1% of the time, Pallas kernels for 40%

profile of v3, /device:TPU:1, one launch (start us, length us, event | category | flops | bytes accessed | tf_op | source)
XLA Modules:
  0.0 124.4 jit_solution(13686200910465171733)
XLA Ops:
  0.6 0.1 pad_add_fusion.refs_0_.place_ref
  0.7 9.6 %forward_down.1 = (f32[64,1664]{1,0:T(8,128)S(1)}, f32[64,1664]{1,0:T(8,128)S(1)}, bf16[128,1024]{1,0:T(8,128)(2,1)}, bf16[128,1024]{1,0:T(8,128)(2,1)S(1)}, s32...) custom-call(s32[2]{0:T(128)S(1)} %pad_add_fusion.refs_0_.place_ref, ...), custom_call_target="tpu_custom_call" | custom-call | bytes 15000000 | tf_op jit(solution)/shard_map/forward_down/pallas_call | solution.py:172
  10.3 3.3 %collective-permute-start.2 = (f32[64,1664]{1,0:T(8,128)S(1)}, f32[64,1664]{1,0:T(8,128)S(1)}, u32[]{:S(2)}, u32[]{:S(2)}) collective-permute-start(f32[64,1664]{1,0:T(8,128)S(1)} %get-tuple-element.40), channel_id=1, source_target_pairs={{0,16},{16,0},{32,48},{48,32},{64,80},{80,64},{96,112},{112,96},{1... | collective-permute-start | bytes 1277960 | tf_op jit(solution)/shard_map/ppermute | solution.py:476
  13.6 4.7 %forward_gate.1 = (f32[64,1664]{1,0:T(8,128)S(1)}, f32[64,1664]{1,0:T(8,128)S(1)}, bf16[1024,1664]{1,0:T(8,128)(2,1)}, bf16[128,1024]{1,0:T(8,128)(2,1)S(1)}, bf...) custom-call(s32[2]{0:T(128)S(1)} %pad_add_fusion.refs_0_.place_ref, bf16[128,1024]{1,0:T(8,128)(2,1)S(1)} %get-tuple-element.29.refs_1_, ...), custom_call_target="tpu_custom_call" | custom-call | bytes 15000000 | tf_op jit(solution)/shard_map/forward_gate/pallas_call | solution.py:227
  18.3 0.1 collective-permute-start
  18.4 3.8 %forward_up.1 = (f32[64,1664]{1,0:T(8,128)S(1)}, f32[64,1664]{1,0:T(8,128)S(1)}, bf16[1024,1664]{1,0:T(8,128)(2,1)}) custom-call(bf16[128,1024]{1,0:T(8,128)(2,1)S(1)} %get-tuple-element.34.refs_0_, s32[512,1664]{1,0:T(8,128)S(1)} %get-tuple-element.35.refs_1_, f32[16,1664]{1,0:T(8,128)S(1)} %get-tuple-element.36.refs_2_), custom_call_target="tpu_custom_call" | custom-call | bytes 15000000 | tf_op jit(solution)/shard_map/forward_up/pallas_call | solution.py:227
  22.2 0.6 collective-permute-start.1
  22.8 0.0 collective-permute-done.2
  22.8 0.0 collective-permute-done
  22.9 1.3 %collective-permute-done.1 = f32[64,1664]{1,0:T(8,128)S(1)} collective-permute-done((f32[64,1664]{1,0:T(8,128)S(1)}, f32[64,1664]{1,0:T(8,128)S(1)}, u32[]{:S(2)}, u32[]{:S(2)}) %collective-permute-start.1) | collective-permute-done | bytes 426016 | tf_op jit(solution)/shard_map/ppermute | solution.py:476
  24.2 0.9 maximum_bitcast_fusion.after_ref
  25.1 3.8 %all-to-all-start = ((bf16[8,8,4992]{2,1,0:T(8,128)(2,1)}), bf16[8,8,4992]{2,1,0:T(8,128)(2,1)S(1)}, u32[]{:S(2)}, u32[]{:S(2)}) async-start(bf16[8,8,4992]{2,1,0:T(8,128)(2,1)} %maximum_bitcast_fusion.after_ref), calls=%async_computation | async-start | bytes 1277952 | tf_op jit(solution)/shard_map/all_to_all | solution.py:480
  28.9 12.0 %entry_sums.2.refs_0_ = bf16[16,128,1792]{2,1,0:T(8,128)(2,1)} custom-call(bf16[128,1024]{1,0:T(8,128)(2,1)} %get-tuple-element.41.x_ref, s32[512,1664]{1,0:T(8,128)} %right_ref.2, s32[512,1664]{1,0:T(8,128)} %right_ref.2, s32[512,1664]{1,0:T(8,128)} %last_ref.3, bf16[8,8,4992]{2,1,0:T(8,128)(2,1)} %maximum_bitcast_fusion.after_ref), custom_call_target="tpu_custom_call" | custom-call | bytes 33000000 | tf_op jit(solution)/shard_map/entry_sums/pallas_call | solution.py:273
  40.9 0.0 all-to-all-done
  40.9 0.1 add_bitcast_fusion
  41.1 0.9 broadcast_in_dim.2.after_ref
  41.9 5.1 %all-to-all-start.1 = ((bf16[8,8,4992]{2,1,0:T(8,128)(2,1)}), bf16[8,8,4992]{2,1,0:T(8,128)(2,1)S(1)}, u32[]{:S(2)}, u32[]{:S(2)}) async-start(bf16[8,8,4992]{2,1,0:T(8,128)(2,1)} %broadcast_in_dim.2.after_ref), calls=%async_computation.1 | async-start | bytes 1277952 | tf_op jit(solution)/shard_map/all_to_all | solution.py:480
  47.1 10.7 %entry_sums.3.refs_1_ = bf16[16,128,1536]{2,1,0:T(8,128)(2,1)} custom-call(bf16[128,1024]{1,0:T(8,128)(2,1)} %get-tuple-element.41.x_ref, s32[512,1664]{1,0:T(8,128)} %last_ref.3, s32[512,1664]{1,0:T(8,128)} %last_ref.3, s32[512,1664]{1,0:T(8,128)} %last_ref.3, bf16[8,8,4992]{2,1,0:T(8,128)(2,1)} %broadcast_in_dim.2.after_ref), custom_call_target="tpu_custom_call" | custom-call | bytes 33000000 | tf_op jit(solution)/shard_map/entry_sums/pallas_call | solution.py:273
  57.8 0.0 all-to-all-done.1
  57.8 1.6 %collective-permute-start.3 = (bf16[64,3328]{1,0:T(8,128)(2,1)S(1)}, bf16[64,3328]{1,0:T(8,128)(2,1)S(1)}, u32[]{:S(2)}, u32[]{:S(2)}) collective-permute-start(bf16[64,3328]{1,0:T(8,128)(2,1)S(1)} %slice.33.near_ref), channel_id=1, source_target_pairs={{0,16},{16,0},{32,48},{48,32},{64,80},{80,64},{96,112},{112,96},{1... | collective-permute-start | bytes 1277960 | tf_op jit(solution)/shard_map/ppermute | solution.py:476
  59.5 0.3 collective-permute-start.4
  59.8 1.4 %collective-permute-done.4.refs_1_ = bf16[64,1664]{1,0:T(8,128)(2,1)S(1)} collective-permute-done((bf16[64,1664]{1,0:T(8,128)(2,1)S(1)}, bf16[64,1664]{1,0:T(8,128)(2,1)S(1)}, u32[]{:S(2)}, u32[]{:S(2)}) %collective-permute-start.4) | collective-permute-done | bytes 213024 | tf_op jit(solution)/shard_map/ppermute | solution.py:476
  61.2 9.9 %down_bins.1 = (f32[16,1024]{1,0:T(8,128)S(1)}, bf16[1024,1664]{1,0:T(8,128)(2,1)S(1)}, bf16[1024,1664]{1,0:T(8,128)(2,1)S(1)}) custom-call(bf16[64,1664]{1,0:T(8,128)(2,1)S(1)} %slice.34.refs_0_, bf16[64,1664]{1,0:T(8,128)(2,1)S(1)} %collective-permute-done.4.refs_1_, bf16[128,1024]{1,0:T(8,128)(2,1)} %get-tuple-element.44.refs_2_, s32[832,1024]{1,0:T(8,128)} %refs_3_.3, ...), custom_call_target="tpu_custom_call" | custom-call | bytes 30000000 | tf_op jit(solution)/shard_map/down_bins/pallas_call | solution.py:398
  71.1 0.0 collective-permute-done.3.far_ref
  71.1 5.9 %input_grad.1.refs_1_ = bf16[4,48,1024]{2,1,0:T(8,128)(2,1)} custom-call(s32[2]{0:T(128)S(1)} %pad_add_fusion.refs_0_.place_ref, bf16[64,3328]{1,0:T(8,128)(2,1)S(1)} %slice.33.near_ref, bf16[64,3328]{1,0:T(8,128)(2,1)S(1)} %collective-permute-done.3.far_ref, bf16[1024,1664]{1,0:T(8,128)(2,1)S(1)} %get-tuple-element.47.wg_ref, ...), custom_call_target="tpu_custom_call" | custom-call | bytes 10500000 | tf_op jit(solution)/shard_map/input_grad/pallas_call | solution.py:436
  77.0 4.0 %all-to-all-start.2 = ((bf16[4,48,1024]{2,1,0:T(8,128)(2,1)}), bf16[4,48,1024]{2,1,0:T(8,128)(2,1)S(1)}, u32[]{:S(2)}, u32[]{:S(2)}) async-start(bf16[4,48,1024]{2,1,0:T(8,128)(2,1)} %input_grad.1.refs_1_), calls=%async_computation.2 | async-start | bytes 786432 | tf_op jit(solution)/shard_map/all_to_all | solution.py:532
  81.0 3.6 %table_sums.2.refs_2_.gate_ref = f32[16,1664]{1,0:T(8,128)S(1)} custom-call(bf16[64,3328]{1,0:T(8,128)(2,1)S(1)} %slice.33.near_ref, bf16[64,3328]{1,0:T(8,128)(2,1)S(1)} %collective-permute-done.3.far_ref, bf16[16,128,1792]{2,1,0:T(8,128)(2,1)} %entry_sums.2.refs_0_, bf16[4,48,1024]{2,1,0:T(8,128)(2,1)} %input_grad.1.refs_1_), custom_call_target="tpu_custom_call" | custom-call | bytes 13500000 | tf_op jit(solution)/shard_map/table_sums/pallas_call | solution.py:327
  84.7 3.7 %table_sums.3.up_ref.after_ref = f32[16,1664]{1,0:T(8,128)S(1)} custom-call(bf16[64,3328]{1,0:T(8,128)(2,1)S(1)} %slice.33.near_ref, bf16[64,3328]{1,0:T(8,128)(2,1)S(1)} %collective-permute-done.3.far_ref, bf16[16,128,1792]{2,1,0:T(8,128)(2,1)} %entry_sums.2.refs_0_, bf16[16,128,1536]{2,1,0:T(8,128)(2,1)} %entry_sums.3.refs_1_, ...), custom_call_target="tpu_custom_call" | custom-call | bytes 13500000 | tf_op jit(solution)/shard_map/table_sums/pallas_call | solution.py:327
  88.4 0.6 choose.1
  88.9 0.7 collective-permute-start.5
  89.6 1.0 collective-permute-done.5.back_ref
  90.6 0.0 all-to-all-done.2.after_ref.back_ref
  90.6 13.3 %all_to_all.25 = bf16[8,16,1664]{2,1,0:T(8,128)(2,1)S(1)} all-to-all(bf16[8,16,1664]{2,1,0:T(8,128)(2,1)S(1)} %add_and_copy.1), channel_id=1, replica_groups={{0,32,64,96,128,160,192,224},{16,48,80,112,144,176,208,240},{1,33,65,97..., dimensions={0} | all-to-all | bytes 851968 | tf_op jit(solution)/shard_map/all_to_all | solution.py:480
  104.0 0.1 add_bitcast_fusion.1.after_ref
  104.0 1.7 %collective-permute-start.6 = (f32[16,1664]{1,0:T(8,128)S(1)}, f32[16,1664]{1,0:T(8,128)S(1)}, u32[]{:S(2)}, u32[]{:S(2)}) collective-permute-start(f32[16,1664]{1,0:T(8,128)S(1)} %add_bitcast_fusion.1.after_ref), channel_id=1, source_target_pairs={{0,16},{16,0},{32,48},{48,32},{64,80},{80,64},{96,112},{112,96},{1... | collective-permute-start | bytes 319496 | tf_op jit(solution)/shard_map/ppermute | solution.py:476
  105.7 0.7 add_along_x.1
  106.4 7.3 %all-to-all-start.4 = ((bf16[4,32,1024]{2,1,0:T(8,128)(2,1)}), bf16[4,32,1024]{2,1,0:T(8,128)(2,1)S(1)}, u32[]{:S(2)}, u32[]{:S(2)}) async-start(bf16[4,32,1024]{2,1,0:T(8,128)(2,1)} %add_along_x.1), calls=%async_computation.4 | async-start | bytes 524288 | tf_op jit(solution)/shard_map/all_to_all | solution.py:532
  113.7 0.0 collective-permute-done.6
  113.7 0.8 select_multiply_fusion
  114.5 8.6 %all-to-all-done.4 = bf16[4,32,1024]{2,1,0:T(8,128)(2,1)S(1)} async-done(((bf16[4,32,1024]{2,1,0:T(8,128)(2,1)}), bf16[4,32,1024]{2,1,0:T(8,128)(2,1)S(1)}, u32[]{:S(2)}, u32[]{:S(2)}) %all-to-all-start.4) | async-done | bytes 262176 | tf_op jit(solution)/shard_map/all_to_all | solution.py:532
  123.1 0.6 fusion.1
  123.7 0.7 multiply_bitcast_fusion
  (8 shorter events, 0.3 us)
Async XLA Ops:
  10.3 12.5 %collective-permute-start.2 = (f32[64,1664]{1,0:T(8,128)S(1)}, f32[64,1664]{1,0:T(8,128)S(1)}, u32[]{:S(2)}, u32[]{:S(2)}) collective-permute-start(f32[64,1664]{1,0:T(8,128)S(1)} %get-tuple-element.40), channel_id=1, source_target_pairs={{0,16},{16,0},{32,48},{48,32},{64,80},{80,64},{96,112},{112,96},{1... | collective-permute-start | bytes 1277960 | tf_op jit(solution)/shard_map/ppermute | solution.py:476
  18.3 4.5 %collective-permute-start = (f32[64,1664]{1,0:T(8,128)S(1)}, f32[64,1664]{1,0:T(8,128)S(1)}, u32[]{:S(2)}, u32[]{:S(2)}) collective-permute-start(f32[64,1664]{1,0:T(8,128)S(1)} %get-tuple-element.33), channel_id=1, source_target_pairs={{0,16},{16,0},{32,48},{48,32},{64,80},{80,64},{96,112},{112,96},{1... | collective-permute-start | bytes 1277960 | tf_op jit(solution)/shard_map/ppermute | solution.py:476
  22.2 2.0 %collective-permute-start.1 = (f32[64,1664]{1,0:T(8,128)S(1)}, f32[64,1664]{1,0:T(8,128)S(1)}, u32[]{:S(2)}, u32[]{:S(2)}) collective-permute-start(f32[64,1664]{1,0:T(8,128)S(1)} %get-tuple-element.38), channel_id=1, source_target_pairs={{0,16},{16,0},{32,48},{48,32},{64,80},{80,64},{96,112},{112,96},{1... | collective-permute-start | bytes 1277960 | tf_op jit(solution)/shard_map/ppermute | solution.py:476
  25.1 15.8 %all-to-all-start = ((bf16[8,8,4992]{2,1,0:T(8,128)(2,1)}), bf16[8,8,4992]{2,1,0:T(8,128)(2,1)S(1)}, u32[]{:S(2)}, u32[]{:S(2)}) async-start(bf16[8,8,4992]{2,1,0:T(8,128)(2,1)} %maximum_bitcast_fusion.after_ref), calls=%async_computation | async-start | bytes 1277952 | tf_op jit(solution)/shard_map/all_to_all | solution.py:480
  41.9 15.9 %all-to-all-start.1 = ((bf16[8,8,4992]{2,1,0:T(8,128)(2,1)}), bf16[8,8,4992]{2,1,0:T(8,128)(2,1)S(1)}, u32[]{:S(2)}, u32[]{:S(2)}) async-start(bf16[8,8,4992]{2,1,0:T(8,128)(2,1)} %broadcast_in_dim.2.after_ref), calls=%async_computation.1 | async-start | bytes 1277952 | tf_op jit(solution)/shard_map/all_to_all | solution.py:480
  57.8 13.3 %collective-permute-start.3 = (bf16[64,3328]{1,0:T(8,128)(2,1)S(1)}, bf16[64,3328]{1,0:T(8,128)(2,1)S(1)}, u32[]{:S(2)}, u32[]{:S(2)}) collective-permute-start(bf16[64,3328]{1,0:T(8,128)(2,1)S(1)} %slice.33.near_ref), channel_id=1, source_target_pairs={{0,16},{16,0},{32,48},{48,32},{64,80},{80,64},{96,112},{112,96},{1... | collective-permute-start | bytes 1277960 | tf_op jit(solution)/shard_map/ppermute | solution.py:476
  59.5 1.7 %collective-permute-start.4 = (bf16[64,1664]{1,0:T(8,128)(2,1)S(1)}, bf16[64,1664]{1,0:T(8,128)(2,1)S(1)}, u32[]{:S(2)}, u32[]{:S(2)}) collective-permute-start(bf16[64,1664]{1,0:T(8,128)(2,1)S(1)} %slice.34.refs_0_), channel_id=1, source_target_pairs={{0,16},{16,0},{32,48},{48,32},{64,80},{80,64},{96,112},{112,96},{1... | collective-permute-start | bytes 638984 | tf_op jit(solution)/shard_map/ppermute | solution.py:476
  77.0 13.6 %all-to-all-start.2 = ((bf16[4,48,1024]{2,1,0:T(8,128)(2,1)}), bf16[4,48,1024]{2,1,0:T(8,128)(2,1)S(1)}, u32[]{:S(2)}, u32[]{:S(2)}) async-start(bf16[4,48,1024]{2,1,0:T(8,128)(2,1)} %input_grad.1.refs_1_), calls=%async_computation.2 | async-start | bytes 786432 | tf_op jit(solution)/shard_map/all_to_all | solution.py:532
  88.9 1.6 %collective-permute-start.5 = (f32[16,1664]{1,0:T(8,128)S(1)}, f32[16,1664]{1,0:T(8,128)S(1)}, u32[]{:S(2)}, u32[]{:S(2)}) collective-permute-start(f32[16,1664]{1,0:T(8,128)S(1)} %get-tuple-element.53), channel_id=1, source_target_pairs={{0,16},{16,0},{32,48},{48,32},{64,80},{80,64},{96,112},{112,96},{1... | collective-permute-start | bytes 319496 | tf_op jit(solution)/shard_map/ppermute | solution.py:476
  104.0 9.7 %collective-permute-start.6 = (f32[16,1664]{1,0:T(8,128)S(1)}, f32[16,1664]{1,0:T(8,128)S(1)}, u32[]{:S(2)}, u32[]{:S(2)}) collective-permute-start(f32[16,1664]{1,0:T(8,128)S(1)} %add_bitcast_fusion.1.after_ref), channel_id=1, source_target_pairs={{0,16},{16,0},{32,48},{48,32},{64,80},{80,64},{96,112},{112,96},{1... | collective-permute-start | bytes 319496 | tf_op jit(solution)/shard_map/ppermute | solution.py:476
  106.4 16.6 %all-to-all-start.4 = ((bf16[4,32,1024]{2,1,0:T(8,128)(2,1)}), bf16[4,32,1024]{2,1,0:T(8,128)(2,1)S(1)}, u32[]{:S(2)}, u32[]{:S(2)}) async-start(bf16[4,32,1024]{2,1,0:T(8,128)(2,1)} %add_along_x.1), calls=%async_computation.4 | async-start | bytes 524288 | tf_op jit(solution)/shard_map/all_to_all | solution.py:532

commit v4 on v3

--- a/solution.py
+++ b/solution.py
@@ -69,9 +69,10 @@
     return one_hot(token == token_of(row, core))
 
 
-def to_owners(core):
+def to_owners(core, hid):
     owned, row = iotas(TOKENS)
-    return one_hot(token_of(row, core) == (((owned >> 3) & 3) * 4 + (owned >> 5)) * 8 + (owned & 7))
+    away = ((owned >> 4) & 1) | ((owned >> 2) & 2)
+    return one_hot(token_of(row, core) == ((away ^ (hid >> 2)) * 4 + (owned >> 5)) * 8 + (owned & 7))
 
 
 SCALAR = pl.BlockSpec(memory_space=pltpu.SMEM)
@@ -146,18 +147,20 @@
     ordered_ref[...] = dot(to_rows(place_ref[0]), raw_ref[...]).astype(BF16)
     store = pltpu.make_async_copy(ordered_ref, ordered_hbm, sem)
     store.start()
-    merge = {rows: merge_matrix(2 * rows) for _, rows in blocks_of(words, LANES)}
     for i, (load, (at, rows)) in enumerate(zip(loads, blocks_of(words, LANES))):
         load.wait()
         if i == len(loads) // 2 - 1:
             start_all(later)
-        decode_rows(index_ref, table_ref, weight_ref, at, rows)
-        hidden = dot_nt(ordered_ref[...], weight_ref[: 2 * rows, :])
+        decode_rows(index_ref, table_ref, weight_ref.at[pl.ds(2 * at, 2 * rows)], at, rows)
+    merge = {rows: merge_matrix(2 * rows) for _, rows in blocks_of(words, LANES)}
+    for at, rows in blocks_of(words, LANES):
+        cols = slice(2 * at, 2 * (at + rows))
+        hidden = dot_nt(ordered_ref[...], weight_ref[cols, :])
         coarse = hidden.astype(BF16)
         fine = (hidden - coarse.astype(F32)).astype(BF16)
         hidden = dot(coarse, merge[rows]) + dot(fine, merge[rows])
-        near_ref[:, 2 * at : 2 * (at + rows)] = hidden[:HALF]
-        far_ref[:, 2 * at : 2 * (at + rows)] = hidden[HALF:]
+        near_ref[:, cols] = hidden[:HALF]
+        far_ref[:, cols] = hidden[HALF:]
     store.wait()
     wait_all(later)
 
@@ -184,7 +187,7 @@
             pltpu.VMEM(table.shape, F32),
             pltpu.VMEM(index.shape, I32),
             pltpu.VMEM((TOKENS, width), BF16),
-            pltpu.VMEM((WIDE, width), BF16),
+            pltpu.VMEM((2 * words, width), BF16),
             pltpu.SemaphoreType.DMA((pl.cdiv(words, LANES),)),
             pltpu.SemaphoreType.DMA((count + 2,)),
             pltpu.SemaphoreType.DMA,
@@ -418,14 +421,19 @@
     rows, width = wg_ref.shape
     gate = jnp.concatenate([near_ref[:, :width], far_ref[:, :width]], axis=0)
     up = jnp.concatenate([near_ref[:, width:], far_ref[:, width:]], axis=0)
-    order = to_owners(place_ref[0])
+    order = to_owners(place_ref[0], place_ref[1])
     merge = merge_matrix(WIDE)
     count = TOKENS // pieces
-    for at in range(0, rows, WIDE):
-        part = (dot_nt(gate, wg_ref[at : at + WIDE, :]) + dot_nt(up, wu_ref[at : at + WIDE, :])).astype(BF16)
+
+    def product(i, carry):
+        at = pl.ds(pl.multiple_of(i * WIDE, WIDE), WIDE)
+        part = (dot_nt(gate, wg_ref[at, :]) + dot_nt(up, wu_ref[at, :])).astype(BF16)
         part = dot(dot(order, part).astype(BF16), merge).astype(BF16)
         for piece in range(pieces):
-            sent_ref[piece, ENTRIES:, at : at + WIDE] = part[piece * count : (piece + 1) * count]
+            sent_ref[piece, ENTRIES:, at] = part[piece * count : (piece + 1) * count]
+        return carry
+
+    lax.fori_loop(0, rows // WIDE, product, 0)
     bins = bins_ref[...].astype(BF16)
     for piece in range(pieces):
         sent_ref[piece, :ENTRIES] = bins
@@ -444,29 +452,64 @@
     )(place, near, far, w_gate, w_up, bins)
 
 
-def add_along_x_kernel(back_ref, after_ref, sent_ref):
-    pieces = back_ref.shape[0]
+def put_bins(bins, sent_ref):
+    coarse = bins.astype(BF16)
+    sent_ref[:ENTRIES] = coarse
+    sent_ref[ENTRIES : 2 * ENTRIES] = (bins - coarse.astype(F32)).astype(BF16)
+
+
+def add_along_x_kernel(back_ref, after_ref, kept_ref, bins_ref, sent_ref):
     sums = back_ref[0].astype(F32)
-    for piece in range(1, pieces):
+    for piece in range(1, back_ref.shape[0]):
         sums = sums + back_ref[piece].astype(F32)
-    bins = sums[:ENTRIES].astype(BF16)
-    for piece in range(pieces):
-        own = sums[ENTRIES + 8 * piece : ENTRIES + 8 * piece + 8]
-        sent_ref[piece, :ENTRIES] = bins
-        sent_ref[piece, ENTRIES:] = jnp.concatenate([own, own], axis=0).astype(BF16)
+    half = kept_ref.shape[0]
+    kept_ref[...] = sums[ENTRIES : ENTRIES + half]
+    bins_ref[...] = sums[:ENTRIES]
+    put_bins(sums[:ENTRIES], sent_ref)
+    sent_ref[2 * ENTRIES :] = sums[ENTRIES + half :].astype(BF16)
 
 
 def add_along_x(back, after):
-    width = back.shape[2]
+    half, width = (back.shape[1] - ENTRIES) // 2, back.shape[2]
     return pl.pallas_call(
         add_along_x_kernel,
         in_specs=[IN_VMEM, ANYWHERE],
-        out_specs=IN_VMEM,
-        out_shape=shape((4, ENTRIES + 16, width), BF16),
+        out_specs=[IN_VMEM] * 3,
+        out_shape=[
+            pltpu.VMEM((half, width), F32),
+            pltpu.VMEM((ENTRIES, width), F32),
+            pltpu.VMEM((2 * ENTRIES + half, width), BF16),
+        ],
         compiler_params=params(),
         cost_estimate=cost(0.7),
         name="add_along_x",
     )(back, after)
+
+
+def add_along_z_kernel(kept_ref, bins_ref, back_ref, after_ref, rows_ref, sums_ref, sent_ref):
+    bins = bins_ref[...] + (back_ref[:ENTRIES].astype(F32) + back_ref[ENTRIES : 2 * ENTRIES].astype(F32))
+    rows = kept_ref[...] + back_ref[2 * ENTRIES :].astype(F32)
+    rows_ref[...] = rows
+    sums_ref[...] = bins
+    put_bins(bins, sent_ref)
+    sent_ref[2 * ENTRIES :] = rows.astype(BF16)
+
+
+def add_along_z(kept, bins, back, after):
+    rows, width = kept.shape
+    return pl.pallas_call(
+        add_along_z_kernel,
+        in_specs=[IN_VMEM] * 3 + [ANYWHERE],
+        out_specs=[IN_VMEM] * 3,
+        out_shape=[
+            pltpu.VMEM((rows, width), F32),
+            pltpu.VMEM(bins.shape, F32),
+            pltpu.VMEM((2 * ENTRIES + rows, width), BF16),
+        ],
+        compiler_params=params(),
+        cost_estimate=cost(0.7),
+        name="add_along_z",
+    )(kept, bins, back, after)
 
 
 ONE_CORE = [[2 * place + core for place in range(8)] for core in range(2)]
@@ -525,11 +568,14 @@
 
 
 SAME_Z = [[4 * z + x for x in range(4)] for z in range(4)]
-SAME_X = [[4 * z + x for z in range(4)] for x in range(4)]
-
-
-def exchange_hid(pieces, groups):
-    return lax.all_to_all(pieces, "hid", 0, 0, tiled=True, axis_index_groups=groups)
+
+
+def exchange_x(pieces):
+    return lax.all_to_all(pieces, "hid", 0, 0, tiled=True, axis_index_groups=SAME_Z)
+
+
+def other_hid(array, bit):
+    return lax.ppermute(array, "hid", [(i, i ^ bit) for i in range(16)])
 
 
 def local_hidden(pre_gate, pre_up, hidden_grad):
@@ -574,17 +620,18 @@
 
     down_sum, w_gate, w_up = down_bins(activ_near, activ_far, grad, down_index, (w_gate, w_up))
     sent = input_grads(place, grad_near, grad_far, w_gate, w_up, down_sum)
-    back_x = exchange_hid(sent, SAME_Z)
     gate_part = table_sums(grad_near, grad_far, 0, [gate_sums], [(0, width, 0)], sent)
+    kept, bins, sent = add_along_x(exchange_x(sent), gate_part)
     pieces = [(width, LANES, 0), (0, width - LANES, LANES)]
-    up_part = table_sums(grad_near, grad_far, 1, [gate_sums, up_sums], pieces, gate_part)
+    up_part = table_sums(grad_near, grad_far, 1, [gate_sums, up_sums], pieces, sent)
+    kept, bins, sent = add_along_z(kept, bins, other_hid(sent, 4), up_part)
     own, other = choose(place, gate_part, up_part, up_part)
-    own = total(exchange_inp(add_and_copy(own, other_core(other), back_x)))
+    own = total(exchange_inp(add_and_copy(own, other_core(other), sent)))
     other = other_core(own)
     gate_sum, up_sum = jnp.where(core == 0, own, other), jnp.where(core == 0, other, own)
-    back = exchange_hid(add_along_x(back_x, own), SAME_X)
-    input_grad = total(back[:, ENTRIES : ENTRIES + 8]).astype(BF16)
-    down_sum = total(back[:, :ENTRIES])
+    back = other_hid(sent, 8).astype(F32)
+    input_grad = (kept[:8] + back[2 * ENTRIES + 8 :]).astype(BF16)
+    down_sum = bins + (back[:ENTRIES] + back[ENTRIES : 2 * ENTRIES])
     scale = 1.0 / TOKENS
     return input_grad, gate_sum * scale, up_sum * scale, down_sum * scale
 

time: 126 us -> 124 us (0.984)
  blocking collectives: 13.3 us -> 0 us
  starting transfers between devices: 28.5 us -> 35.6 us
  waiting for transfers between devices: 12.3 us -> 18.4 us
  Pallas kernels: 65.2 us -> 63.6 us
    all_to_all x1 -> x0, blocking collectives: 13.3 us -> none  [exchange_inp(): lax.all_to_all(pieces, 'inp', 0, 0, tiled=True, axis_index_groups=ONE_CORE)]
    ppermute x0 -> x2, waiting for transfers between devices: none -> 11.6 us  [other_hid(): return lax.ppermute(array, 'hid', [(i, i ^ bit) for i in range(16)])]
    ppermute x0 -> x2, starting transfers between devices: none -> 7.85 us  [other_hid(): return lax.ppermute(array, 'hid', [(i, i ^ bit) for i in range(16)])]
    all_to_all x2 -> x1, starting transfers between devices: 11.3 us -> 4.18 us  [exchange_x(): lax.all_to_all(pieces, 'hid', 0, 0, tiled=True, axis_index_groups=SAME_Z)]
    all_to_all x2 -> x1, waiting for transfers between devices: 8.6 us -> 3.57 us  [exchange_x(): lax.all_to_all(pieces, 'hid', 0, 0, tiled=True, axis_index_groups=SAME_Z)]
    all_to_all x2 -> x3, starting transfers between devices: 8.94 us -> 13.4 us  [exchange_inp(): lax.all_to_all(pieces, 'inp', 0, 0, tiled=True, axis_index_groups=ONE_CORE)]
    ppermute x7, starting transfers between devices: 8.27 us -> 10.1 us  [other_core(): return lax.ppermute(array, 'inp', [(i, i ^ 1) for i in range(16)])]
  transfers between devices with their start and end apart: 11 -> 13, of which waited for: 4 -> 6; matrix products, arithmetic and copies ran while one was open for 1% -> 1% of each run, Pallas kernels for 40% -> 37%
where the time goes in v4:
time: 124 us; the launch traced here: 123 us
  Pallas kernels  63.6 us (51%)
  starting transfers between devices  35.6 us (29%)
  waiting for transfers between devices  18.4 us (15%)
  other arithmetic  3.32 us (3%)
    pallas_call x2, Pallas kernels, entry_sums(): pl.pallas_call(entry_sums_kernel, grid=(blocks,), in_specs=[pl.BlockSpec(...  22.7 us
    all_to_all x3, starting transfers between devices, exchange_inp(): lax.all_to_all(pieces, 'inp', 0, 0, tiled=True, axis_index_groups=ONE_CORE)  13.4 us
    ppermute x2, waiting for transfers between devices, other_hid(): return lax.ppermute(array, 'hid', [(i, i ^ bit) for i in range(16)])  11.6 us
    ppermute x7, starting transfers between devices, other_core(): return lax.ppermute(array, 'inp', [(i, i ^ 1) for i in range(16)])  10.1 us
    pallas_call x1, Pallas kernels, down_bins(): pl.pallas_call(kernel, in_specs=[IN_VMEM] * 2 + [IN_HBM] * (2 + count), o...  9.9 us
    pallas_call x1, Pallas kernels, forward_down(): pl.pallas_call(kernel, in_specs=[SCALAR] + [IN_HBM] * (3 + count), out_sp...  8.7 us
    pallas_call x2, Pallas kernels, forward_up(): pl.pallas_call(functools.partial(forward_up_kernel, first), in_specs=[SCA...  8.48 us
    ppermute x2, starting transfers between devices, other_hid(): return lax.ppermute(array, 'hid', [(i, i ^ bit) for i in range(16)])  7.85 us
  transfers between devices with their start and end apart: 13, of which 6 were waited for; matrix products, arithmetic and copies ran while one was open for 1% of the time, Pallas kernels for 37%

profile of v4, /device:TPU:1, one launch (start us, length us, event | category | flops | bytes accessed | tf_op | source)
XLA Modules:
  0.0 122.5 jit_solution(15142135339298617336)
XLA Ops:
  0.6 0.1 pad_add_fusion.refs_0_.place_ref
  0.7 8.7 %forward_down.1 = (f32[64,1664]{1,0:T(8,128)S(1)}, f32[64,1664]{1,0:T(8,128)S(1)}, bf16[128,1024]{1,0:T(8,128)(2,1)}, bf16[128,1024]{1,0:T(8,128)(2,1)S(1)}, s32...) custom-call(s32[2]{0:T(128)S(1)} %pad_add_fusion.refs_0_.place_ref, ...), custom_call_target="tpu_custom_call" | custom-call | bytes 15000000 | tf_op jit(solution)/shard_map/forward_down/pallas_call | solution.py:175
  9.4 3.3 %collective-permute-start.2 = (f32[64,1664]{1,0:T(8,128)S(1)}, f32[64,1664]{1,0:T(8,128)S(1)}, u32[]{:S(2)}, u32[]{:S(2)}) collective-permute-start(f32[64,1664]{1,0:T(8,128)S(1)} %get-tuple-element.46), channel_id=1, source_target_pairs={{0,16},{16,0},{32,48},{48,32},{64,80},{80,64},{96,112},{112,96},{1... | collective-permute-start | bytes 1277960 | tf_op jit(solution)/shard_map/ppermute | solution.py:519
  12.8 4.7 %forward_gate.1 = (f32[64,1664]{1,0:T(8,128)S(1)}, f32[64,1664]{1,0:T(8,128)S(1)}, bf16[1024,1664]{1,0:T(8,128)(2,1)}, bf16[128,1024]{1,0:T(8,128)(2,1)S(1)}, bf...) custom-call(s32[2]{0:T(128)S(1)} %pad_add_fusion.refs_0_.place_ref, bf16[128,1024]{1,0:T(8,128)(2,1)S(1)} %get-tuple-element.35.refs_1_, ...), custom_call_target="tpu_custom_call" | custom-call | bytes 15000000 | tf_op jit(solution)/shard_map/forward_gate/pallas_call | solution.py:230
  17.5 0.1 collective-permute-start
  17.6 3.8 %forward_up.1 = (f32[64,1664]{1,0:T(8,128)S(1)}, f32[64,1664]{1,0:T(8,128)S(1)}, bf16[1024,1664]{1,0:T(8,128)(2,1)}) custom-call(bf16[128,1024]{1,0:T(8,128)(2,1)S(1)} %get-tuple-element.40.refs_0_, s32[512,1664]{1,0:T(8,128)S(1)} %get-tuple-element.41.refs_1_, f32[16,1664]{1,0:T(8,128)S(1)} %get-tuple-element.42.refs_2_), custom_call_target="tpu_custom_call" | custom-call | bytes 15000000 | tf_op jit(solution)/shard_map/forward_up/pallas_call | solution.py:230
  21.4 0.6 collective-permute-start.1
  21.9 0.0 collective-permute-done.2
  22.0 0.0 collective-permute-done
  22.0 1.3 %collective-permute-done.1 = f32[64,1664]{1,0:T(8,128)S(1)} collective-permute-done((f32[64,1664]{1,0:T(8,128)S(1)}, f32[64,1664]{1,0:T(8,128)S(1)}, u32[]{:S(2)}, u32[]{:S(2)}) %collective-permute-start.1) | collective-permute-done | bytes 426016 | tf_op jit(solution)/shard_map/ppermute | solution.py:519
  23.4 0.9 maximum_bitcast_fusion.after_ref
  24.3 3.8 %all-to-all-start = ((bf16[8,8,4992]{2,1,0:T(8,128)(2,1)}), bf16[8,8,4992]{2,1,0:T(8,128)(2,1)S(1)}, u32[]{:S(2)}, u32[]{:S(2)}) async-start(bf16[8,8,4992]{2,1,0:T(8,128)(2,1)} %maximum_bitcast_fusion.after_ref), calls=%async_computation | async-start | bytes 1277952 | tf_op jit(solution)/shard_map/all_to_all | solution.py:523
  28.1 12.0 %entry_sums.2.refs_0_ = bf16[16,128,1792]{2,1,0:T(8,128)(2,1)} custom-call(bf16[128,1024]{1,0:T(8,128)(2,1)} %get-tuple-element.47.x_ref, s32[512,1664]{1,0:T(8,128)} %right_ref.2, s32[512,1664]{1,0:T(8,128)} %right_ref.2, s32[512,1664]{1,0:T(8,128)} %last_ref.3, bf16[8,8,4992]{2,1,0:T(8,128)(2,1)} %maximum_bitcast_fusion.after_ref), custom_call_target="tpu_custom_call" | custom-call | bytes 33000000 | tf_op jit(solution)/shard_map/entry_sums/pallas_call | solution.py:276
  40.1 0.0 all-to-all-done
  40.1 0.1 add_bitcast_fusion
  40.3 0.9 broadcast_in_dim.2.after_ref
  41.1 5.1 %all-to-all-start.1 = ((bf16[8,8,4992]{2,1,0:T(8,128)(2,1)}), bf16[8,8,4992]{2,1,0:T(8,128)(2,1)S(1)}, u32[]{:S(2)}, u32[]{:S(2)}) async-start(bf16[8,8,4992]{2,1,0:T(8,128)(2,1)} %broadcast_in_dim.2.after_ref), calls=%async_computation.1 | async-start | bytes 1277952 | tf_op jit(solution)/shard_map/all_to_all | solution.py:523
  46.3 10.7 %entry_sums.3.refs_1_ = bf16[16,128,1536]{2,1,0:T(8,128)(2,1)} custom-call(bf16[128,1024]{1,0:T(8,128)(2,1)} %get-tuple-element.47.x_ref, s32[512,1664]{1,0:T(8,128)} %last_ref.3, s32[512,1664]{1,0:T(8,128)} %last_ref.3, s32[512,1664]{1,0:T(8,128)} %last_ref.3, bf16[8,8,4992]{2,1,0:T(8,128)(2,1)} %broadcast_in_dim.2.after_ref), custom_call_target="tpu_custom_call" | custom-call | bytes 33000000 | tf_op jit(solution)/shard_map/entry_sums/pallas_call | solution.py:276
  56.9 0.0 all-to-all-done.1
  57.0 1.7 %collective-permute-start.3 = (bf16[64,3328]{1,0:T(8,128)(2,1)S(1)}, bf16[64,3328]{1,0:T(8,128)(2,1)S(1)}, u32[]{:S(2)}, u32[]{:S(2)}) collective-permute-start(bf16[64,3328]{1,0:T(8,128)(2,1)S(1)} %slice.39.near_ref), channel_id=1, source_target_pairs={{0,16},{16,0},{32,48},{48,32},{64,80},{80,64},{96,112},{112,96},{1... | collective-permute-start | bytes 1277960 | tf_op jit(solution)/shard_map/ppermute | solution.py:519
  58.7 0.1 collective-permute-start.4
  58.8 1.6 %collective-permute-done.4.refs_1_ = bf16[64,1664]{1,0:T(8,128)(2,1)S(1)} collective-permute-done((bf16[64,1664]{1,0:T(8,128)(2,1)S(1)}, bf16[64,1664]{1,0:T(8,128)(2,1)S(1)}, u32[]{:S(2)}, u32[]{:S(2)}) %collective-permute-start.4) | collective-permute-done | bytes 213024 | tf_op jit(solution)/shard_map/ppermute | solution.py:519
  60.3 9.9 %down_bins.1 = (f32[16,1024]{1,0:T(8,128)S(1)}, bf16[1024,1664]{1,0:T(8,128)(2,1)S(1)}, bf16[1024,1664]{1,0:T(8,128)(2,1)S(1)}) custom-call(bf16[64,1664]{1,0:T(8,128)(2,1)S(1)} %slice.40.refs_0_, bf16[64,1664]{1,0:T(8,128)(2,1)S(1)} %collective-permute-done.4.refs_1_, bf16[128,1024]{1,0:T(8,128)(2,1)} %get-tuple-element.50.refs_2_, s32[832,1024]{1,0:T(8,128)} %refs_3_.3, ...), custom_call_target="tpu_custom_call" | custom-call | bytes 30000000 | tf_op jit(solution)/shard_map/down_bins/pallas_call | solution.py:401
  70.2 0.0 collective-permute-done.3.far_ref
  70.3 5.0 %input_grad.1.refs_1_ = bf16[4,48,1024]{2,1,0:T(8,128)(2,1)} custom-call(s32[2]{0:T(128)S(1)} %pad_add_fusion.refs_0_.place_ref, bf16[64,3328]{1,0:T(8,128)(2,1)S(1)} %slice.39.near_ref, bf16[64,3328]{1,0:T(8,128)(2,1)S(1)} %collective-permute-done.3.far_ref, bf16[1024,1664]{1,0:T(8,128)(2,1)S(1)} %get-tuple-element.53.wg_ref, ...), custom_call_target="tpu_custom_call" | custom-call | bytes 10500000 | tf_op jit(solution)/shard_map/input_grad/pallas_call | solution.py:444
  75.3 4.2 %all-to-all-start.2 = ((bf16[4,48,1024]{2,1,0:T(8,128)(2,1)}), bf16[4,48,1024]{2,1,0:T(8,128)(2,1)S(1)}, u32[]{:S(2)}, u32[]{:S(2)}) async-start(bf16[4,48,1024]{2,1,0:T(8,128)(2,1)} %input_grad.1.refs_1_), calls=%async_computation.2 | async-start | bytes 786432 | tf_op jit(solution)/shard_map/all_to_all | solution.py:574
  79.4 3.6 %table_sums.2.after_ref.gate_ref = f32[16,1664]{1,0:T(8,128)S(1)} custom-call(bf16[64,3328]{1,0:T(8,128)(2,1)S(1)} %slice.39.near_ref, bf16[64,3328]{1,0:T(8,128)(2,1)S(1)} %collective-permute-done.3.far_ref, bf16[16,128,1792]{2,1,0:T(8,128)(2,1)} %entry_sums.2.refs_0_, bf16[4,48,1024]{2,1,0:T(8,128)(2,1)} %input_grad.1.refs_1_), custom_call_target="tpu_custom_call" | custom-call | bytes 13500000 | tf_op jit(solution)/shard_map/table_sums/pallas_call | solution.py:330
  83.1 3.6 %all-to-all-done.2.back_ref = bf16[4,48,1024]{2,1,0:T(8,128)(2,1)S(1)} async-done(((bf16[4,48,1024]{2,1,0:T(8,128)(2,1)}), bf16[4,48,1024]{2,1,0:T(8,128)(2,1)S(1)}, u32[]{:S(2)}, u32[]{:S(2)}) %all-to-all-start.2) | async-done | bytes 393248 | tf_op jit(solution)/shard_map/all_to_all | solution.py:574
  86.7 0.1 add_along_x.1
  86.7 3.7 %table_sums.3.after_ref.up_ref = f32[16,1664]{1,0:T(8,128)S(1)} custom-call(bf16[64,3328]{1,0:T(8,128)(2,1)S(1)} %slice.39.near_ref, bf16[64,3328]{1,0:T(8,128)(2,1)S(1)} %collective-permute-done.3.far_ref, bf16[16,128,1792]{2,1,0:T(8,128)(2,1)} %entry_sums.2.refs_0_, bf16[16,128,1536]{2,1,0:T(8,128)(2,1)} %entry_sums.3.refs_1_, ...), custom_call_target="tpu_custom_call" | custom-call | bytes 13500000 | tf_op jit(solution)/shard_map/table_sums/pallas_call | solution.py:330
  90.4 0.6 choose.1
  91.0 1.9 %collective-permute-start.7 = (f32[16,1664]{1,0:T(8,128)S(1)}, f32[16,1664]{1,0:T(8,128)S(1)}, u32[]{:S(2)}, u32[]{:S(2)}) collective-permute-start(f32[16,1664]{1,0:T(8,128)S(1)} %get-tuple-element.64), channel_id=1, source_target_pairs={{0,16},{16,0},{32,48},{48,32},{64,80},{80,64},{96,112},{112,96},{1... | collective-permute-start | bytes 319496 | tf_op jit(solution)/shard_map/ppermute | solution.py:519
  92.9 3.0 %collective-permute-start.5 = (bf16[48,1024]{1,0:T(8,128)(2,1)S(1)}, bf16[48,1024]{1,0:T(8,128)(2,1)S(1)}, u32[]{:S(2)}, u32[]{:S(2)}) collective-permute-start(bf16[48,1024]{1,0:T(8,128)(2,1)S(1)} %get-tuple-element.59.refs_2_), channel_id=1, source_target_pairs={{0,4},{1,5},{2,6},{3,7},{4,0},{5,1},{6,2},{7,3},{8,12},{9,13},{10,... | collective-permute-start | bytes 294920 | tf_op jit(solution)/shard_map/ppermute | solution.py:578
  95.9 5.2 %collective-permute-done.5.back_ref = bf16[48,1024]{1,0:T(8,128)(2,1)S(1)} collective-permute-done((bf16[48,1024]{1,0:T(8,128)(2,1)S(1)}, bf16[48,1024]{1,0:T(8,128)(2,1)S(1)}, u32[]{:S(2)}, u32[]{:S(2)}) %collective-permute-start.5) | collective-permute-done | bytes 98336 | tf_op jit(solution)/shard_map/ppermute | solution.py:578
  101.1 0.0 collective-permute-done.7.back_ref
  101.1 0.8 add_and_copy.1
  101.9 4.5 %all-to-all-start.3 = ((bf16[8,16,1664]{2,1,0:T(8,128)(2,1)}), bf16[8,16,1664]{2,1,0:T(8,128)(2,1)S(1)}, u32[]{:S(2)}, u32[]{:S(2)}) async-start(bf16[8,16,1664]{2,1,0:T(8,128)(2,1)} %add_and_copy.1), calls=%async_computation.3 | async-start | bytes 851968 | tf_op jit(solution)/shard_map/all_to_all | solution.py:523
  106.4 4.8 %collective-permute-start.6 = (bf16[48,1024]{1,0:T(8,128)(2,1)S(1)}, bf16[48,1024]{1,0:T(8,128)(2,1)S(1)}, u32[]{:S(2)}, u32[]{:S(2)}) collective-permute-start(bf16[48,1024]{1,0:T(8,128)(2,1)S(1)} %get-tuple-element.62.after_ref), channel_id=1, source_target_pairs={{0,8},{1,9},{2,10},{3,11},{4,12},{5,13},{6,14},{7,15},{8,0},{9,1},... | collective-permute-start | bytes 294920 | tf_op jit(solution)/shard_map/ppermute | solution.py:578
  111.3 6.4 %collective-permute-done.6 = bf16[48,1024]{1,0:T(8,128)(2,1)S(1)} collective-permute-done((bf16[48,1024]{1,0:T(8,128)(2,1)S(1)}, bf16[48,1024]{1,0:T(8,128)(2,1)S(1)}, u32[]{:S(2)}, u32[]{:S(2)}) %collective-permute-start.6) | collective-permute-done | bytes 98336 | tf_op jit(solution)/shard_map/ppermute | solution.py:578
  117.7 0.6 fusion.1
  118.4 0.0 all-to-all-done.3
  118.4 0.1 add_bitcast_fusion.1
  118.4 2.4 %collective-permute-start.8 = (f32[16,1664]{1,0:T(8,128)S(1)}, f32[16,1664]{1,0:T(8,128)S(1)}, u32[]{:S(2)}, u32[]{:S(2)}) collective-permute-start(f32[16,1664]{1,0:T(8,128)S(1)} %add_bitcast_fusion.1), channel_id=1, source_target_pairs={{0,16},{16,0},{32,48},{48,32},{64,80},{80,64},{96,112},{112,96},{1... | collective-permute-start | bytes 319496 | tf_op jit(solution)/shard_map/ppermute | solution.py:519
  120.8 0.6 fusion.3
  121.4 0.3 collective-permute-done.8
  121.8 0.8 select_multiply_fusion
  (9 shorter events, 0.3 us)
Async XLA Ops:
  9.4 12.5 %collective-permute-start.2 = (f32[64,1664]{1,0:T(8,128)S(1)}, f32[64,1664]{1,0:T(8,128)S(1)}, u32[]{:S(2)}, u32[]{:S(2)}) collective-permute-start(f32[64,1664]{1,0:T(8,128)S(1)} %get-tuple-element.46), channel_id=1, source_target_pairs={{0,16},{16,0},{32,48},{48,32},{64,80},{80,64},{96,112},{112,96},{1... | collective-permute-start | bytes 1277960 | tf_op jit(solution)/shard_map/ppermute | solution.py:519
  17.5 4.5 %collective-permute-start = (f32[64,1664]{1,0:T(8,128)S(1)}, f32[64,1664]{1,0:T(8,128)S(1)}, u32[]{:S(2)}, u32[]{:S(2)}) collective-permute-start(f32[64,1664]{1,0:T(8,128)S(1)} %get-tuple-element.39), channel_id=1, source_target_pairs={{0,16},{16,0},{32,48},{48,32},{64,80},{80,64},{96,112},{112,96},{1... | collective-permute-start | bytes 1277960 | tf_op jit(solution)/shard_map/ppermute | solution.py:519
  21.4 2.0 %collective-permute-start.1 = (f32[64,1664]{1,0:T(8,128)S(1)}, f32[64,1664]{1,0:T(8,128)S(1)}, u32[]{:S(2)}, u32[]{:S(2)}) collective-permute-start(f32[64,1664]{1,0:T(8,128)S(1)} %get-tuple-element.44), channel_id=1, source_target_pairs={{0,16},{16,0},{32,48},{48,32},{64,80},{80,64},{96,112},{112,96},{1... | collective-permute-start | bytes 1277960 | tf_op jit(solution)/shard_map/ppermute | solution.py:519
  24.3 15.8 %all-to-all-start = ((bf16[8,8,4992]{2,1,0:T(8,128)(2,1)}), bf16[8,8,4992]{2,1,0:T(8,128)(2,1)S(1)}, u32[]{:S(2)}, u32[]{:S(2)}) async-start(bf16[8,8,4992]{2,1,0:T(8,128)(2,1)} %maximum_bitcast_fusion.after_ref), calls=%async_computation | async-start | bytes 1277952 | tf_op jit(solution)/shard_map/all_to_all | solution.py:523
  41.1 15.8 %all-to-all-start.1 = ((bf16[8,8,4992]{2,1,0:T(8,128)(2,1)}), bf16[8,8,4992]{2,1,0:T(8,128)(2,1)S(1)}, u32[]{:S(2)}, u32[]{:S(2)}) async-start(bf16[8,8,4992]{2,1,0:T(8,128)(2,1)} %broadcast_in_dim.2.after_ref), calls=%async_computation.1 | async-start | bytes 1277952 | tf_op jit(solution)/shard_map/all_to_all | solution.py:523
  57.0 13.3 %collective-permute-start.3 = (bf16[64,3328]{1,0:T(8,128)(2,1)S(1)}, bf16[64,3328]{1,0:T(8,128)(2,1)S(1)}, u32[]{:S(2)}, u32[]{:S(2)}) collective-permute-start(bf16[64,3328]{1,0:T(8,128)(2,1)S(1)} %slice.39.near_ref), channel_id=1, source_target_pairs={{0,16},{16,0},{32,48},{48,32},{64,80},{80,64},{96,112},{112,96},{1... | collective-permute-start | bytes 1277960 | tf_op jit(solution)/shard_map/ppermute | solution.py:519
  58.7 1.7 %collective-permute-start.4 = (bf16[64,1664]{1,0:T(8,128)(2,1)S(1)}, bf16[64,1664]{1,0:T(8,128)(2,1)S(1)}, u32[]{:S(2)}, u32[]{:S(2)}) collective-permute-start(bf16[64,1664]{1,0:T(8,128)(2,1)S(1)} %slice.40.refs_0_), channel_id=1, source_target_pairs={{0,16},{16,0},{32,48},{48,32},{64,80},{80,64},{96,112},{112,96},{1... | collective-permute-start | bytes 638984 | tf_op jit(solution)/shard_map/ppermute | solution.py:519
  75.3 11.4 %all-to-all-start.2 = ((bf16[4,48,1024]{2,1,0:T(8,128)(2,1)}), bf16[4,48,1024]{2,1,0:T(8,128)(2,1)S(1)}, u32[]{:S(2)}, u32[]{:S(2)}) async-start(bf16[4,48,1024]{2,1,0:T(8,128)(2,1)} %input_grad.1.refs_1_), calls=%async_computation.2 | async-start | bytes 786432 | tf_op jit(solution)/shard_map/all_to_all | solution.py:574
  91.0 10.1 %collective-permute-start.7 = (f32[16,1664]{1,0:T(8,128)S(1)}, f32[16,1664]{1,0:T(8,128)S(1)}, u32[]{:S(2)}, u32[]{:S(2)}) collective-permute-start(f32[16,1664]{1,0:T(8,128)S(1)} %get-tuple-element.64), channel_id=1, source_target_pairs={{0,16},{16,0},{32,48},{48,32},{64,80},{80,64},{96,112},{112,96},{1... | collective-permute-start | bytes 319496 | tf_op jit(solution)/shard_map/ppermute | solution.py:519
  92.9 8.2 %collective-permute-start.5 = (bf16[48,1024]{1,0:T(8,128)(2,1)S(1)}, bf16[48,1024]{1,0:T(8,128)(2,1)S(1)}, u32[]{:S(2)}, u32[]{:S(2)}) collective-permute-start(bf16[48,1024]{1,0:T(8,128)(2,1)S(1)} %get-tuple-element.59.refs_2_), channel_id=1, source_target_pairs={{0,4},{1,5},{2,6},{3,7},{4,0},{5,1},{6,2},{7,3},{8,12},{9,13},{10,... | collective-permute-start | bytes 294920 | tf_op jit(solution)/shard_map/ppermute | solution.py:578
  101.9 16.5 %all-to-all-start.3 = ((bf16[8,16,1664]{2,1,0:T(8,128)(2,1)}), bf16[8,16,1664]{2,1,0:T(8,128)(2,1)S(1)}, u32[]{:S(2)}, u32[]{:S(2)}) async-start(bf16[8,16,1664]{2,1,0:T(8,128)(2,1)} %add_and_copy.1), calls=%async_computation.3 | async-start | bytes 851968 | tf_op jit(solution)/shard_map/all_to_all | solution.py:523
  106.4 11.3 %collective-permute-start.6 = (bf16[48,1024]{1,0:T(8,128)(2,1)S(1)}, bf16[48,1024]{1,0:T(8,128)(2,1)S(1)}, u32[]{:S(2)}, u32[]{:S(2)}) collective-permute-start(bf16[48,1024]{1,0:T(8,128)(2,1)S(1)} %get-tuple-element.62.after_ref), channel_id=1, source_target_pairs={{0,8},{1,9},{2,10},{3,11},{4,12},{5,13},{6,14},{7,15},{8,0},{9,1},... | collective-permute-start | bytes 294920 | tf_op jit(solution)/shard_map/ppermute | solution.py:578
  118.4 3.4 %collective-permute-start.8 = (f32[16,1664]{1,0:T(8,128)S(1)}, f32[16,1664]{1,0:T(8,128)S(1)}, u32[]{:S(2)}, u32[]{:S(2)}) collective-permute-start(f32[16,1664]{1,0:T(8,128)S(1)} %add_bitcast_fusion.1), channel_id=1, source_target_pairs={{0,16},{16,0},{32,48},{48,32},{64,80},{80,64},{96,112},{112,96},{1... | collective-permute-start | bytes 319496 | tf_op jit(solution)/shard_map/ppermute | solution.py:519

commit v5 on v2

--- a/solution.py
+++ b/solution.py
@@ -71,7 +71,7 @@
 
 def to_owners(core, hid):
     owned, row = iotas(TOKENS)
-    bits = ((owned >> 6) & 1) | ((owned >> 4) & 2) | ((owned >> 2) & 4) | (owned & 8)
+    bits = ((owned >> 4) & 4) | ((owned >> 2) & 8) | ((owned >> 4) & 1) | ((owned >> 2) & 2)
     return one_hot(token_of(row, core) == (bits ^ hid) * 8 + (owned & 7))
 
 
@@ -142,21 +142,25 @@
     small = [pltpu.make_async_copy(raw_hbm, raw_ref, next_sems.at[count])]
     small.append(pltpu.make_async_copy(table_hbm, table_ref, next_sems.at[count + 1]))
     later = [pltpu.make_async_copy(a, b, next_sems.at[i]) for i, (a, b) in enumerate(zip(next_hbm, next_refs))]
-    start_all(small + loads + later)
+    start_all(small + loads)
     wait_all(small)
     ordered_ref[...] = dot(to_rows(place_ref[0]), raw_ref[...]).astype(BF16)
     store = pltpu.make_async_copy(ordered_ref, ordered_hbm, sem)
     store.start()
+    for i, (load, (at, rows)) in enumerate(zip(loads, blocks_of(words, LANES))):
+        load.wait()
+        if i == len(loads) // 2 - 1:
+            start_all(later)
+        decode_rows(index_ref, table_ref, weight_ref.at[pl.ds(2 * at, 2 * rows)], at, rows)
     merge = {rows: merge_matrix(2 * rows) for _, rows in blocks_of(words, LANES)}
-    for load, (at, rows) in zip(loads, blocks_of(words, LANES)):
-        load.wait()
-        decode_rows(index_ref, table_ref, weight_ref, at, rows)
-        hidden = dot_nt(ordered_ref[...], weight_ref[: 2 * rows, :])
+    for at, rows in blocks_of(words, LANES):
+        cols = slice(2 * at, 2 * (at + rows))
+        hidden = dot_nt(ordered_ref[...], weight_ref[cols, :])
         coarse = hidden.astype(BF16)
         fine = (hidden - coarse.astype(F32)).astype(BF16)
         hidden = dot(coarse, merge[rows]) + dot(fine, merge[rows])
-        near_ref[:, 2 * at : 2 * (at + rows)] = hidden[:HALF]
-        far_ref[:, 2 * at : 2 * (at + rows)] = hidden[HALF:]
+        near_ref[:, cols] = hidden[:HALF]
+        far_ref[:, cols] = hidden[HALF:]
     store.wait()
     wait_all(later)
 
@@ -183,7 +187,7 @@
             pltpu.VMEM(table.shape, F32),
             pltpu.VMEM(index.shape, I32),
             pltpu.VMEM((TOKENS, width), BF16),
-            pltpu.VMEM((WIDE, width), BF16),
+            pltpu.VMEM((2 * words, width), BF16),
             pltpu.SemaphoreType.DMA((pl.cdiv(words, LANES),)),
             pltpu.SemaphoreType.DMA((count + 2,)),
             pltpu.SemaphoreType.DMA,
@@ -426,11 +430,16 @@
     up = jnp.concatenate([near_ref[:, width:], far_ref[:, width:]], axis=0)
     order = to_owners(place_ref[0], place_ref[1])
     merge = merge_matrix(WIDE)
-    for at in range(0, rows, WIDE):
-        part = (dot_nt(gate, wg_ref[at : at + WIDE, :]) + dot_nt(up, wu_ref[at : at + WIDE, :])).astype(BF16)
+
+    def product(i, carry):
+        at = pl.ds(pl.multiple_of(i * WIDE, WIDE), WIDE)
+        part = (dot_nt(gate, wg_ref[at, :]) + dot_nt(up, wu_ref[at, :])).astype(BF16)
         part = dot(dot(order, part).astype(BF16), merge)
-        kept_ref[:, at : at + WIDE] = part[:HALF]
-        sent_ref[2 * ENTRIES :, at : at + WIDE] = part[HALF:].astype(BF16)
+        kept_ref[:, at] = part[:HALF]
+        sent_ref[2 * ENTRIES :, at] = part[HALF:].astype(BF16)
+        return carry
+
+    lax.fori_loop(0, rows // WIDE, product, 0)
     put_bins(bins_ref[...], sent_ref)
 
 
@@ -576,17 +585,16 @@
     down_sum, w_gate, w_up = down_bins(activ_near, activ_far, grad, down_index, (w_gate, w_up))
     kept, sent = input_grads(place, grad_near, grad_far, w_gate, w_up, down_sum)
     gate_part = table_sums(grad_near, grad_far, 0, [gate_sums], [(0, width, 0)], sent)
-    kept, down_sum, sent = add_received(kept, down_sum, other_hid(sent, 1), gate_part)
+    kept, down_sum, sent = add_received(kept, down_sum, other_hid(sent, 4), gate_part)
     pieces = [(width, LANES, 0), (0, width - LANES, LANES)]
     up_part = table_sums(grad_near, grad_far, 1, [gate_sums, up_sums], pieces, sent)
-    kept, down_sum, sent = add_received(kept, down_sum, other_hid(sent, 2), up_part)
+    kept, down_sum, sent = add_received(kept, down_sum, other_hid(sent, 8), up_part)
     own, other = choose(place, gate_part, up_part, sent)
-    back = other_core(other)
-    kept, down_sum, sent = add_received(kept, down_sum, other_hid(sent, 4), back)
-    own = total(exchange_inp(add_and_copy(own, back, sent)))
+    own = total(exchange_inp(add_and_copy(own, other_core(other), up_part)))
     other = other_core(own)
     gate_sum, up_sum = jnp.where(core == 0, own, other), jnp.where(core == 0, other, own)
-    back = other_hid(sent, 8).astype(F32)
+    kept, down_sum, sent = add_received(kept, down_sum, other_hid(sent, 1), sent)
+    back = other_hid(sent, 2).astype(F32)
     input_grad = (kept[:8] + back[2 * ENTRIES + 8 :]).astype(BF16)
     down_sum = down_sum + (back[:ENTRIES] + back[ENTRIES : 2 * ENTRIES])
     scale = 1.0 / TOKENS

time: 122 us -> 121 us (level)
  starting transfers between devices: 35.3 us -> 38.2 us
  waiting for transfers between devices: 16 us -> 14.2 us
    ppermute x4, waiting for transfers between devices: 12.9 us -> 9.98 us  [other_hid(): return lax.ppermute(array, 'hid', [(i, i ^ bit) for i in range(16)])]
    ppermute x7, starting transfers between devices: 9.84 us -> 12.5 us  [other_core(): return lax.ppermute(array, 'inp', [(i, i ^ 1) for i in range(16)])]
  transfers between devices with their start and end apart: 14 -> 14, of which waited for: 6 -> 7; matrix products, arithmetic and copies ran while one was open for 1% -> 1% of each run, Pallas kernels for 40% -> 40%
where the time goes in v5:
time: 121 us; the launch traced here: 120 us
  Pallas kernels  62.8 us (52%)
  starting transfers between devices  38.2 us (32%)
  waiting for transfers between devices  14.2 us (12%)
  other arithmetic  3.32 us (3%)
    pallas_call x2, Pallas kernels, entry_sums(): pl.pallas_call(entry_sums_kernel, grid=(blocks,), in_specs=[pl.BlockSpec(...  22.7 us
    all_to_all x3, starting transfers between devices, exchange_inp(): lax.all_to_all(pieces, 'inp', 0, 0, tiled=True, axis_index_groups=ONE_CORE)  13.1 us
    ppermute x4, starting transfers between devices, other_hid(): return lax.ppermute(array, 'hid', [(i, i ^ bit) for i in range(16)])  12.7 us
    ppermute x7, starting transfers between devices, other_core(): return lax.ppermute(array, 'inp', [(i, i ^ 1) for i in range(16)])  12.5 us
    ppermute x4, waiting for transfers between devices, other_hid(): return lax.ppermute(array, 'hid', [(i, i ^ bit) for i in range(16)])  9.98 us
    pallas_call x1, Pallas kernels, down_bins(): pl.pallas_call(kernel, in_specs=[IN_VMEM] * 2 + [IN_HBM] * (2 + count), o...  9.9 us
    pallas_call x1, Pallas kernels, forward_down(): pl.pallas_call(kernel, in_specs=[SCALAR] + [IN_HBM] * (3 + count), out_sp...  8.7 us
    pallas_call x2, Pallas kernels, forward_up(): pl.pallas_call(functools.partial(forward_up_kernel, first), in_specs=[SCA...  8.48 us
  transfers between devices with their start and end apart: 14, of which 7 were waited for; matrix products, arithmetic and copies ran while one was open for 1% of the time, Pallas kernels for 40%

profile of v5, /device:TPU:1, one launch (start us, length us, event | category | flops | bytes accessed | tf_op | source)
XLA Modules:
  0.0 120.2 jit_solution(12782235533729492516)
XLA Ops:
  0.6 0.1 pad_add_fusion.refs_0_.place_ref
  0.7 8.7 %forward_down.1 = (f32[64,1664]{1,0:T(8,128)S(1)}, f32[64,1664]{1,0:T(8,128)S(1)}, bf16[128,1024]{1,0:T(8,128)(2,1)}, bf16[128,1024]{1,0:T(8,128)(2,1)S(1)}, s32...) custom-call(s32[2]{0:T(128)S(1)} %pad_add_fusion.refs_0_.place_ref, ...), custom_call_target="tpu_custom_call" | custom-call | bytes 15000000 | tf_op jit(solution)/shard_map/forward_down/pallas_call | solution.py:175
  9.4 3.3 %collective-permute-start.2 = (f32[64,1664]{1,0:T(8,128)S(1)}, f32[64,1664]{1,0:T(8,128)S(1)}, u32[]{:S(2)}, u32[]{:S(2)}) collective-permute-start(f32[64,1664]{1,0:T(8,128)S(1)} %get-tuple-element.51), channel_id=1, source_target_pairs={{0,16},{16,0},{32,48},{48,32},{64,80},{80,64},{96,112},{112,96},{1... | collective-permute-start | bytes 1277960 | tf_op jit(solution)/shard_map/ppermute | solution.py:490
  12.8 4.7 %forward_gate.1 = (f32[64,1664]{1,0:T(8,128)S(1)}, f32[64,1664]{1,0:T(8,128)S(1)}, bf16[1024,1664]{1,0:T(8,128)(2,1)}, bf16[128,1024]{1,0:T(8,128)(2,1)S(1)}, bf...) custom-call(s32[2]{0:T(128)S(1)} %pad_add_fusion.refs_0_.place_ref, bf16[128,1024]{1,0:T(8,128)(2,1)S(1)} %get-tuple-element.40.refs_1_, ...), custom_call_target="tpu_custom_call" | custom-call | bytes 15000000 | tf_op jit(solution)/shard_map/forward_gate/pallas_call | solution.py:230
  17.5 0.1 collective-permute-start
  17.6 3.8 %forward_up.1 = (f32[64,1664]{1,0:T(8,128)S(1)}, f32[64,1664]{1,0:T(8,128)S(1)}, bf16[1024,1664]{1,0:T(8,128)(2,1)}) custom-call(bf16[128,1024]{1,0:T(8,128)(2,1)S(1)} %get-tuple-element.45.refs_0_, s32[512,1664]{1,0:T(8,128)S(1)} %get-tuple-element.46.refs_1_, f32[16,1664]{1,0:T(8,128)S(1)} %get-tuple-element.47.refs_2_), custom_call_target="tpu_custom_call" | custom-call | bytes 15000000 | tf_op jit(solution)/shard_map/forward_up/pallas_call | solution.py:230
  21.4 0.6 collective-permute-start.1
  21.9 0.0 collective-permute-done.2
  22.0 0.0 collective-permute-done
  22.0 1.3 %collective-permute-done.1 = f32[64,1664]{1,0:T(8,128)S(1)} collective-permute-done((f32[64,1664]{1,0:T(8,128)S(1)}, f32[64,1664]{1,0:T(8,128)S(1)}, u32[]{:S(2)}, u32[]{:S(2)}) %collective-permute-start.1) | collective-permute-done | bytes 426016 | tf_op jit(solution)/shard_map/ppermute | solution.py:490
  23.4 0.9 maximum_bitcast_fusion.after_ref
  24.3 3.8 %all-to-all-start = ((bf16[8,8,4992]{2,1,0:T(8,128)(2,1)}), bf16[8,8,4992]{2,1,0:T(8,128)(2,1)S(1)}, u32[]{:S(2)}, u32[]{:S(2)}) async-start(bf16[8,8,4992]{2,1,0:T(8,128)(2,1)} %maximum_bitcast_fusion.after_ref), calls=%async_computation | async-start | bytes 1277952 | tf_op jit(solution)/shard_map/all_to_all | solution.py:494
  28.1 12.0 %entry_sums.2.refs_0_ = bf16[16,128,1792]{2,1,0:T(8,128)(2,1)} custom-call(bf16[128,1024]{1,0:T(8,128)(2,1)} %get-tuple-element.52.x_ref, s32[512,1664]{1,0:T(8,128)} %right_ref.2, s32[512,1664]{1,0:T(8,128)} %right_ref.2, s32[512,1664]{1,0:T(8,128)} %last_ref.3, bf16[8,8,4992]{2,1,0:T(8,128)(2,1)} %maximum_bitcast_fusion.after_ref), custom_call_target="tpu_custom_call" | custom-call | bytes 33000000 | tf_op jit(solution)/shard_map/entry_sums/pallas_call | solution.py:276
  40.1 0.0 all-to-all-done
  40.1 0.1 add_bitcast_fusion
  40.2 0.9 broadcast_in_dim.2.after_ref
  41.1 5.1 %all-to-all-start.1 = ((bf16[8,8,4992]{2,1,0:T(8,128)(2,1)}), bf16[8,8,4992]{2,1,0:T(8,128)(2,1)S(1)}, u32[]{:S(2)}, u32[]{:S(2)}) async-start(bf16[8,8,4992]{2,1,0:T(8,128)(2,1)} %broadcast_in_dim.2.after_ref), calls=%async_computation.1 | async-start | bytes 1277952 | tf_op jit(solution)/shard_map/all_to_all | solution.py:494
  46.2 10.7 %entry_sums.3.refs_1_ = bf16[16,128,1536]{2,1,0:T(8,128)(2,1)} custom-call(bf16[128,1024]{1,0:T(8,128)(2,1)} %get-tuple-element.52.x_ref, s32[512,1664]{1,0:T(8,128)} %last_ref.3, s32[512,1664]{1,0:T(8,128)} %last_ref.3, s32[512,1664]{1,0:T(8,128)} %last_ref.3, bf16[8,8,4992]{2,1,0:T(8,128)(2,1)} %broadcast_in_dim.2.after_ref), custom_call_target="tpu_custom_call" | custom-call | bytes 33000000 | tf_op jit(solution)/shard_map/entry_sums/pallas_call | solution.py:276
  56.9 0.0 all-to-all-done.1
  57.0 1.6 %collective-permute-start.3 = (bf16[64,3328]{1,0:T(8,128)(2,1)S(1)}, bf16[64,3328]{1,0:T(8,128)(2,1)S(1)}, u32[]{:S(2)}, u32[]{:S(2)}) collective-permute-start(bf16[64,3328]{1,0:T(8,128)(2,1)S(1)} %slice.39.near_ref), channel_id=1, source_target_pairs={{0,16},{16,0},{32,48},{48,32},{64,80},{80,64},{96,112},{112,96},{1... | collective-permute-start | bytes 1277960 | tf_op jit(solution)/shard_map/ppermute | solution.py:490
  58.6 0.1 collective-permute-start.4
  58.7 1.6 %collective-permute-done.4.refs_1_ = bf16[64,1664]{1,0:T(8,128)(2,1)S(1)} collective-permute-done((bf16[64,1664]{1,0:T(8,128)(2,1)S(1)}, bf16[64,1664]{1,0:T(8,128)(2,1)S(1)}, u32[]{:S(2)}, u32[]{:S(2)}) %collective-permute-start.4) | collective-permute-done | bytes 213024 | tf_op jit(solution)/shard_map/ppermute | solution.py:490
  60.3 9.9 %down_bins.1 = (f32[16,1024]{1,0:T(8,128)S(1)}, bf16[1024,1664]{1,0:T(8,128)(2,1)S(1)}, bf16[1024,1664]{1,0:T(8,128)(2,1)S(1)}) custom-call(bf16[64,1664]{1,0:T(8,128)(2,1)S(1)} %slice.40.refs_0_, bf16[64,1664]{1,0:T(8,128)(2,1)S(1)} %collective-permute-done.4.refs_1_, bf16[128,1024]{1,0:T(8,128)(2,1)} %get-tuple-element.55.refs_2_, s32[832,1024]{1,0:T(8,128)} %refs_3_.3, ...), custom_call_target="tpu_custom_call" | custom-call | bytes 30000000 | tf_op jit(solution)/shard_map/down_bins/pallas_call | solution.py:401
  70.2 0.0 collective-permute-done.3.far_ref
  70.2 4.2 %input_grad.1 = (f32[64,1024]{1,0:T(8,128)S(1)}, bf16[96,1024]{1,0:T(8,128)(2,1)S(1)}) custom-call(s32[2]{0:T(128)S(1)} %pad_add_fusion.refs_0_.place_ref, bf16[64,3328]{1,0:T(8,128)(2,1)S(1)} %slice.39.near_ref, bf16[64,3328]{1,0:T(8,128)(2,1)S(1)} %collective-permute-done.3.far_ref, bf16[1024,1664]{1,0:T(8,128)(2,1)S(1)} %get-tuple-element.58.wg_ref, ...), custom_call_target="tpu_custom_call" | custom-call | bytes 10500000 | tf_op jit(solution)/shard_map/input_grad/pallas_call | solution.py:448
  74.5 3.3 %collective-permute-start.5 = (bf16[96,1024]{1,0:T(8,128)(2,1)S(1)}, bf16[96,1024]{1,0:T(8,128)(2,1)S(1)}, u32[]{:S(2)}, u32[]{:S(2)}) collective-permute-start(bf16[96,1024]{1,0:T(8,128)(2,1)S(1)} %get-tuple-element.62.refs_1_), channel_id=1, source_target_pairs={{0,4},{1,5},{2,6},{3,7},{4,0},{5,1},{6,2},{7,3},{8,12},{9,13},{10,... | collective-permute-start | bytes 589832 | tf_op jit(solution)/shard_map/ppermute | solution.py:542
  77.7 3.6 %table_sums.2.after_ref.gate_ref = f32[16,1664]{1,0:T(8,128)S(1)} custom-call(bf16[64,3328]{1,0:T(8,128)(2,1)S(1)} %slice.39.near_ref, bf16[64,3328]{1,0:T(8,128)(2,1)S(1)} %collective-permute-done.3.far_ref, bf16[16,128,1792]{2,1,0:T(8,128)(2,1)} %entry_sums.2.refs_0_, bf16[96,1024]{1,0:T(8,128)(2,1)S(1)} %get-tuple-element.62.refs_1_), custom_call_target="tpu_custom_call" | custom-call | bytes 13500000 | tf_op jit(solution)/shard_map/table_sums/pallas_call | solution.py:330
  81.4 5.5 %collective-permute-done.5.back_ref = bf16[96,1024]{1,0:T(8,128)(2,1)S(1)} collective-permute-done((bf16[96,1024]{1,0:T(8,128)(2,1)S(1)}, bf16[96,1024]{1,0:T(8,128)(2,1)S(1)}, u32[]{:S(2)}, u32[]{:S(2)}) %collective-permute-start.5) | collective-permute-done | bytes 196640 | tf_op jit(solution)/shard_map/ppermute | solution.py:542
  87.0 5.2 %collective-permute-start.6 = (bf16[64,1024]{1,0:T(8,128)(2,1)S(1)}, bf16[64,1024]{1,0:T(8,128)(2,1)S(1)}, u32[]{:S(2)}, u32[]{:S(2)}) collective-permute-start(bf16[64,1024]{1,0:T(8,128)(2,1)S(1)} %get-tuple-element.66.refs_2_), channel_id=1, source_target_pairs={{0,8},{1,9},{2,10},{3,11},{4,12},{5,13},{6,14},{7,15},{8,0},{9,1},... | collective-permute-start | bytes 393224 | tf_op jit(solution)/shard_map/ppermute | solution.py:542
  92.1 3.7 %table_sums.3.after_ref.up_ref = f32[16,1664]{1,0:T(8,128)S(1)} custom-call(bf16[64,3328]{1,0:T(8,128)(2,1)S(1)} %slice.39.near_ref, bf16[64,3328]{1,0:T(8,128)(2,1)S(1)} %collective-permute-done.3.far_ref, bf16[16,128,1792]{2,1,0:T(8,128)(2,1)} %entry_sums.2.refs_0_, bf16[16,128,1536]{2,1,0:T(8,128)(2,1)} %entry_sums.3.refs_1_, ...), custom_call_target="tpu_custom_call" | custom-call | bytes 13500000 | tf_op jit(solution)/shard_map/table_sums/pallas_call | solution.py:330
  95.8 0.0 collective-permute-done.6.back_ref
  95.9 0.6 choose.1
  96.5 3.8 %collective-permute-start.9 = (f32[16,1664]{1,0:T(8,128)S(1)}, f32[16,1664]{1,0:T(8,128)S(1)}, u32[]{:S(2)}, u32[]{:S(2)}) collective-permute-start(f32[16,1664]{1,0:T(8,128)S(1)} %get-tuple-element.74), channel_id=1, source_target_pairs={{0,16},{16,0},{32,48},{48,32},{64,80},{80,64},{96,112},{112,96},{1... | collective-permute-start | bytes 319496 | tf_op jit(solution)/shard_map/ppermute | solution.py:490
  100.3 1.0 collective-permute-done.9.back_ref
  101.2 0.8 add_and_copy.1
  102.0 4.2 %all-to-all-start.2 = ((bf16[8,16,1664]{2,1,0:T(8,128)(2,1)}), bf16[8,16,1664]{2,1,0:T(8,128)(2,1)S(1)}, u32[]{:S(2)}, u32[]{:S(2)}) async-start(bf16[8,16,1664]{2,1,0:T(8,128)(2,1)} %add_and_copy.1), calls=%async_computation.2 | async-start | bytes 851968 | tf_op jit(solution)/shard_map/all_to_all | solution.py:494
  106.2 1.3 %collective-permute-start.7 = (bf16[48,1024]{1,0:T(8,128)(2,1)S(1)}, bf16[48,1024]{1,0:T(8,128)(2,1)S(1)}, u32[]{:S(2)}, u32[]{:S(2)}) collective-permute-start(bf16[48,1024]{1,0:T(8,128)(2,1)S(1)} %get-tuple-element.70.after_ref), channel_id=1, source_target_pairs={{0,1},{1,0},{2,3},{3,2},{4,5},{5,4},{6,7},{7,6},{8,9},{9,8},{10,11... | collective-permute-start | bytes 294920 | tf_op jit(solution)/shard_map/ppermute | solution.py:542
  107.5 2.2 %collective-permute-done.7.back_ref = bf16[48,1024]{1,0:T(8,128)(2,1)S(1)} collective-permute-done((bf16[48,1024]{1,0:T(8,128)(2,1)S(1)}, bf16[48,1024]{1,0:T(8,128)(2,1)S(1)}, u32[]{:S(2)}, u32[]{:S(2)}) %collective-permute-start.7) | collective-permute-done | bytes 98336 | tf_op jit(solution)/shard_map/ppermute | solution.py:542
  109.7 3.0 %collective-permute-start.8 = (bf16[48,1024]{1,0:T(8,128)(2,1)S(1)}, bf16[48,1024]{1,0:T(8,128)(2,1)S(1)}, u32[]{:S(2)}, u32[]{:S(2)}) collective-permute-start(bf16[48,1024]{1,0:T(8,128)(2,1)S(1)} %get-tuple-element.72), channel_id=1, source_target_pairs={{0,2},{1,3},{2,0},{3,1},{4,6},{5,7},{6,4},{7,5},{8,10},{9,11},{10,... | collective-permute-start | bytes 294920 | tf_op jit(solution)/shard_map/ppermute | solution.py:542
  112.7 2.2 %collective-permute-done.8 = bf16[48,1024]{1,0:T(8,128)(2,1)S(1)} collective-permute-done((bf16[48,1024]{1,0:T(8,128)(2,1)S(1)}, bf16[48,1024]{1,0:T(8,128)(2,1)S(1)}, u32[]{:S(2)}, u32[]{:S(2)}) %collective-permute-start.8) | collective-permute-done | bytes 98336 | tf_op jit(solution)/shard_map/ppermute | solution.py:542
  114.9 0.6 fusion.1
  115.6 0.0 all-to-all-done.2
  115.6 0.1 add_bitcast_fusion.1
  115.6 2.9 %collective-permute-start.10 = (f32[16,1664]{1,0:T(8,128)S(1)}, f32[16,1664]{1,0:T(8,128)S(1)}, u32[]{:S(2)}, u32[]{:S(2)}) collective-permute-start(f32[16,1664]{1,0:T(8,128)S(1)} %add_bitcast_fusion.1), channel_id=1, source_target_pairs={{0,16},{16,0},{32,48},{48,32},{64,80},{80,64},{96,112},{112,96},{1... | collective-permute-start | bytes 319496 | tf_op jit(solution)/shard_map/ppermute | solution.py:490
  118.5 0.6 fusion.3
  119.1 0.3 collective-permute-done.10
  119.5 0.8 select_multiply_fusion
  (11 shorter events, 0.3 us)
Async XLA Ops:
  9.4 12.5 %collective-permute-start.2 = (f32[64,1664]{1,0:T(8,128)S(1)}, f32[64,1664]{1,0:T(8,128)S(1)}, u32[]{:S(2)}, u32[]{:S(2)}) collective-permute-start(f32[64,1664]{1,0:T(8,128)S(1)} %get-tuple-element.51), channel_id=1, source_target_pairs={{0,16},{16,0},{32,48},{48,32},{64,80},{80,64},{96,112},{112,96},{1... | collective-permute-start | bytes 1277960 | tf_op jit(solution)/shard_map/ppermute | solution.py:490
  17.5 4.5 %collective-permute-start = (f32[64,1664]{1,0:T(8,128)S(1)}, f32[64,1664]{1,0:T(8,128)S(1)}, u32[]{:S(2)}, u32[]{:S(2)}) collective-permute-start(f32[64,1664]{1,0:T(8,128)S(1)} %get-tuple-element.44), channel_id=1, source_target_pairs={{0,16},{16,0},{32,48},{48,32},{64,80},{80,64},{96,112},{112,96},{1... | collective-permute-start | bytes 1277960 | tf_op jit(solution)/shard_map/ppermute | solution.py:490
  21.4 2.0 %collective-permute-start.1 = (f32[64,1664]{1,0:T(8,128)S(1)}, f32[64,1664]{1,0:T(8,128)S(1)}, u32[]{:S(2)}, u32[]{:S(2)}) collective-permute-start(f32[64,1664]{1,0:T(8,128)S(1)} %get-tuple-element.49), channel_id=1, source_target_pairs={{0,16},{16,0},{32,48},{48,32},{64,80},{80,64},{96,112},{112,96},{1... | collective-permute-start | bytes 1277960 | tf_op jit(solution)/shard_map/ppermute | solution.py:490
  24.3 15.8 %all-to-all-start = ((bf16[8,8,4992]{2,1,0:T(8,128)(2,1)}), bf16[8,8,4992]{2,1,0:T(8,128)(2,1)S(1)}, u32[]{:S(2)}, u32[]{:S(2)}) async-start(bf16[8,8,4992]{2,1,0:T(8,128)(2,1)} %maximum_bitcast_fusion.after_ref), calls=%async_computation | async-start | bytes 1277952 | tf_op jit(solution)/shard_map/all_to_all | solution.py:494
  41.1 15.8 %all-to-all-start.1 = ((bf16[8,8,4992]{2,1,0:T(8,128)(2,1)}), bf16[8,8,4992]{2,1,0:T(8,128)(2,1)S(1)}, u32[]{:S(2)}, u32[]{:S(2)}) async-start(bf16[8,8,4992]{2,1,0:T(8,128)(2,1)} %broadcast_in_dim.2.after_ref), calls=%async_computation.1 | async-start | bytes 1277952 | tf_op jit(solution)/shard_map/all_to_all | solution.py:494
  57.0 13.3 %collective-permute-start.3 = (bf16[64,3328]{1,0:T(8,128)(2,1)S(1)}, bf16[64,3328]{1,0:T(8,128)(2,1)S(1)}, u32[]{:S(2)}, u32[]{:S(2)}) collective-permute-start(bf16[64,3328]{1,0:T(8,128)(2,1)S(1)} %slice.39.near_ref), channel_id=1, source_target_pairs={{0,16},{16,0},{32,48},{48,32},{64,80},{80,64},{96,112},{112,96},{1... | collective-permute-start | bytes 1277960 | tf_op jit(solution)/shard_map/ppermute | solution.py:490
  58.6 1.7 %collective-permute-start.4 = (bf16[64,1664]{1,0:T(8,128)(2,1)S(1)}, bf16[64,1664]{1,0:T(8,128)(2,1)S(1)}, u32[]{:S(2)}, u32[]{:S(2)}) collective-permute-start(bf16[64,1664]{1,0:T(8,128)(2,1)S(1)} %slice.40.refs_0_), channel_id=1, source_target_pairs={{0,16},{16,0},{32,48},{48,32},{64,80},{80,64},{96,112},{112,96},{1... | collective-permute-start | bytes 638984 | tf_op jit(solution)/shard_map/ppermute | solution.py:490
  74.5 12.4 %collective-permute-start.5 = (bf16[96,1024]{1,0:T(8,128)(2,1)S(1)}, bf16[96,1024]{1,0:T(8,128)(2,1)S(1)}, u32[]{:S(2)}, u32[]{:S(2)}) collective-permute-start(bf16[96,1024]{1,0:T(8,128)(2,1)S(1)} %get-tuple-element.62.refs_1_), channel_id=1, source_target_pairs={{0,4},{1,5},{2,6},{3,7},{4,0},{5,1},{6,2},{7,3},{8,12},{9,13},{10,... | collective-permute-start | bytes 589832 | tf_op jit(solution)/shard_map/ppermute | solution.py:542
  87.0 8.9 %collective-permute-start.6 = (bf16[64,1024]{1,0:T(8,128)(2,1)S(1)}, bf16[64,1024]{1,0:T(8,128)(2,1)S(1)}, u32[]{:S(2)}, u32[]{:S(2)}) collective-permute-start(bf16[64,1024]{1,0:T(8,128)(2,1)S(1)} %get-tuple-element.66.refs_2_), channel_id=1, source_target_pairs={{0,8},{1,9},{2,10},{3,11},{4,12},{5,13},{6,14},{7,15},{8,0},{9,1},... | collective-permute-start | bytes 393224 | tf_op jit(solution)/shard_map/ppermute | solution.py:542
  96.5 4.8 %collective-permute-start.9 = (f32[16,1664]{1,0:T(8,128)S(1)}, f32[16,1664]{1,0:T(8,128)S(1)}, u32[]{:S(2)}, u32[]{:S(2)}) collective-permute-start(f32[16,1664]{1,0:T(8,128)S(1)} %get-tuple-element.74), channel_id=1, source_target_pairs={{0,16},{16,0},{32,48},{48,32},{64,80},{80,64},{96,112},{112,96},{1... | collective-permute-start | bytes 319496 | tf_op jit(solution)/shard_map/ppermute | solution.py:490
  102.0 13.5 %all-to-all-start.2 = ((bf16[8,16,1664]{2,1,0:T(8,128)(2,1)}), bf16[8,16,1664]{2,1,0:T(8,128)(2,1)S(1)}, u32[]{:S(2)}, u32[]{:S(2)}) async-start(bf16[8,16,1664]{2,1,0:T(8,128)(2,1)} %add_and_copy.1), calls=%async_computation.2 | async-start | bytes 851968 | tf_op jit(solution)/shard_map/all_to_all | solution.py:494
  106.2 3.5 %collective-permute-start.7 = (bf16[48,1024]{1,0:T(8,128)(2,1)S(1)}, bf16[48,1024]{1,0:T(8,128)(2,1)S(1)}, u32[]{:S(2)}, u32[]{:S(2)}) collective-permute-start(bf16[48,1024]{1,0:T(8,128)(2,1)S(1)} %get-tuple-element.70.after_ref), channel_id=1, source_target_pairs={{0,1},{1,0},{2,3},{3,2},{4,5},{5,4},{6,7},{7,6},{8,9},{9,8},{10,11... | collective-permute-start | bytes 294920 | tf_op jit(solution)/shard_map/ppermute | solution.py:542
  109.7 5.2 %collective-permute-start.8 = (bf16[48,1024]{1,0:T(8,128)(2,1)S(1)}, bf16[48,1024]{1,0:T(8,128)(2,1)S(1)}, u32[]{:S(2)}, u32[]{:S(2)}) collective-permute-start(bf16[48,1024]{1,0:T(8,128)(2,1)S(1)} %get-tuple-element.72), channel_id=1, source_target_pairs={{0,2},{1,3},{2,0},{3,1},{4,6},{5,7},{6,4},{7,5},{8,10},{9,11},{10,... | collective-permute-start | bytes 294920 | tf_op jit(solution)/shard_map/ppermute | solution.py:542
  115.6 3.8 %collective-permute-start.10 = (f32[16,1664]{1,0:T(8,128)S(1)}, f32[16,1664]{1,0:T(8,128)S(1)}, u32[]{:S(2)}, u32[]{:S(2)}) collective-permute-start(f32[16,1664]{1,0:T(8,128)S(1)} %add_bitcast_fusion.1), channel_id=1, source_target_pairs={{0,16},{16,0},{32,48},{48,32},{64,80},{80,64},{96,112},{112,96},{1... | collective-permute-start | bytes 319496 | tf_op jit(solution)/shard_map/ppermute | solution.py:490

commit v6 on v5

--- a/solution.py
+++ b/solution.py
@@ -71,7 +71,7 @@
 
 def to_owners(core, hid):
     owned, row = iotas(TOKENS)
-    bits = ((owned >> 4) & 4) | ((owned >> 2) & 8) | ((owned >> 4) & 1) | ((owned >> 2) & 2)
+    bits = ((owned >> 6) & 1) | ((owned >> 3) & 4) | ((owned >> 1) & 8) | ((owned >> 2) & 2)
     return one_hot(token_of(row, core) == (bits ^ hid) * 8 + (owned & 7))
 
 
@@ -416,12 +416,6 @@
     )(near, far, *in_hbm(grad, index, *brought))
 
 
-def put_bins(bins, sent_ref):
-    coarse = bins.astype(BF16)
-    sent_ref[:ENTRIES] = coarse
-    sent_ref[ENTRIES : 2 * ENTRIES] = (bins - coarse.astype(F32)).astype(BF16)
-
-
 def input_grad_kernel(
     place_ref, near_ref, far_ref, wg_ref, wu_ref, bins_ref, kept_ref, sent_ref
 ):
@@ -436,11 +430,11 @@
         part = (dot_nt(gate, wg_ref[at, :]) + dot_nt(up, wu_ref[at, :])).astype(BF16)
         part = dot(dot(order, part).astype(BF16), merge)
         kept_ref[:, at] = part[:HALF]
-        sent_ref[2 * ENTRIES :, at] = part[HALF:].astype(BF16)
+        sent_ref[ENTRIES:, at] = part[HALF:].astype(BF16)
         return carry
 
     lax.fori_loop(0, rows // WIDE, product, 0)
-    put_bins(bins_ref[...], sent_ref)
+    sent_ref[:ENTRIES] = bins_ref[...].astype(BF16)
 
 
 def input_grads(place, near, far, w_gate, w_up, bins):
@@ -449,7 +443,7 @@
         input_grad_kernel,
         in_specs=[SCALAR] + [IN_VMEM] * 5,
         out_specs=[IN_VMEM] * 2,
-        out_shape=[pltpu.VMEM((HALF, width), F32), pltpu.VMEM((2 * ENTRIES + HALF, width), BF16)],
+        out_shape=[pltpu.VMEM((HALF, width), F32), pltpu.VMEM((ENTRIES + HALF, width), BF16)],
         compiler_params=params(),
         cost_estimate=cost(3.5),
         name="input_grad",
@@ -457,12 +451,12 @@
 
 
 def add_received_kernel(kept_ref, bins_ref, back_ref, after_ref, rows_ref, sums_ref, sent_ref):
-    bins = bins_ref[...] + (back_ref[:ENTRIES].astype(F32) + back_ref[ENTRIES : 2 * ENTRIES].astype(F32))
-    rows = kept_ref[...] + back_ref[2 * ENTRIES :].astype(F32)
+    bins = bins_ref[...] + back_ref[:ENTRIES].astype(F32)
+    rows = kept_ref[...] + back_ref[ENTRIES:].astype(F32)
     rows_ref[...] = rows[: rows_ref.shape[0]]
     sums_ref[...] = bins
-    put_bins(bins, sent_ref)
-    sent_ref[2 * ENTRIES :] = rows[rows.shape[0] - sent_ref.shape[0] + 2 * ENTRIES :].astype(BF16)
+    sent_ref[:ENTRIES] = bins.astype(BF16)
+    sent_ref[ENTRIES:] = rows[rows.shape[0] - sent_ref.shape[0] + ENTRIES :].astype(BF16)
 
 
 def add_received(kept, bins, back, after):
@@ -475,12 +469,53 @@
         out_shape=[
             pltpu.VMEM((half, width), F32),
             pltpu.VMEM(bins.shape, F32),
-            pltpu.VMEM((2 * ENTRIES + half, width), BF16),
+            pltpu.VMEM((ENTRIES + half, width), BF16),
         ],
         compiler_params=params(),
         cost_estimate=cost(0.7),
         name="add_received",
     )(kept, bins, back, after)
+
+
+def add_places_kernel(pieces_ref, after_ref, out_ref):
+    sums = pieces_ref[0].astype(F32)
+    for place in range(1, pieces_ref.shape[0]):
+        sums = sums + pieces_ref[place].astype(F32)
+    out_ref[...] = sums
+
+
+def add_places(pieces, after):
+    return pl.pallas_call(
+        add_places_kernel,
+        in_specs=[IN_VMEM, ANYWHERE],
+        out_specs=IN_VMEM,
+        out_shape=pltpu.VMEM(pieces.shape[1:], F32),
+        compiler_params=params(),
+        cost_estimate=cost(0.7),
+        name="add_places",
+    )(pieces, after)
+
+
+def finish_kernel(place_ref, kept_ref, bins_ref, back_ref, own_ref, other_ref, grad_ref, gate_ref, up_ref, down_ref):
+    scale = 1.0 / TOKENS
+    back = back_ref[...].astype(F32)
+    grad_ref[...] = (kept_ref[:8] + back[ENTRIES + 8 :]).astype(BF16)
+    down_ref[...] = (bins_ref[...] + back[:ENTRIES]) * scale
+    gate_here = place_ref[0] == 0
+    gate_ref[...] = jnp.where(gate_here, own_ref[...], other_ref[...]) * scale
+    up_ref[...] = jnp.where(gate_here, other_ref[...], own_ref[...]) * scale
+
+
+def finish(place, kept, bins, back, own, other):
+    return pl.pallas_call(
+        finish_kernel,
+        in_specs=[SCALAR] + [IN_VMEM] * 5,
+        out_specs=[IN_VMEM] * 4,
+        out_shape=[shape((8, kept.shape[1]), BF16), shape(own.shape, F32), shape(own.shape, F32), shape(bins.shape, F32)],
+        compiler_params=params(),
+        cost_estimate=cost(0.7),
+        name="finish",
+    )(place, kept, bins, back, own, other)
 
 
 ONE_CORE = [[2 * place + core for place in range(8)] for core in range(2)]
@@ -585,20 +620,16 @@
     down_sum, w_gate, w_up = down_bins(activ_near, activ_far, grad, down_index, (w_gate, w_up))
     kept, sent = input_grads(place, grad_near, grad_far, w_gate, w_up, down_sum)
     gate_part = table_sums(grad_near, grad_far, 0, [gate_sums], [(0, width, 0)], sent)
-    kept, down_sum, sent = add_received(kept, down_sum, other_hid(sent, 4), gate_part)
+    kept, down_sum, sent = add_received(kept, down_sum, other_hid(sent, 1), gate_part)
     pieces = [(width, LANES, 0), (0, width - LANES, LANES)]
     up_part = table_sums(grad_near, grad_far, 1, [gate_sums, up_sums], pieces, sent)
-    kept, down_sum, sent = add_received(kept, down_sum, other_hid(sent, 8), up_part)
+    kept, down_sum, sent = add_received(kept, down_sum, other_hid(sent, 4), up_part)
     own, other = choose(place, gate_part, up_part, sent)
-    own = total(exchange_inp(add_and_copy(own, other_core(other), up_part)))
-    other = other_core(own)
-    gate_sum, up_sum = jnp.where(core == 0, own, other), jnp.where(core == 0, other, own)
-    kept, down_sum, sent = add_received(kept, down_sum, other_hid(sent, 1), sent)
-    back = other_hid(sent, 2).astype(F32)
-    input_grad = (kept[:8] + back[2 * ENTRIES + 8 :]).astype(BF16)
-    down_sum = down_sum + (back[:ENTRIES] + back[ENTRIES : 2 * ENTRIES])
-    scale = 1.0 / TOKENS
-    return input_grad, gate_sum * scale, up_sum * scale, down_sum * scale
+    back = other_core(other)
+    kept, down_sum, sent = add_received(kept, down_sum, other_hid(sent, 8), back)
+    last = other_hid(sent, 2)
+    own = add_places(exchange_inp(add_and_copy(own, back, sent)), last)
+    return tuple(finish(place, kept, down_sum, last, own, other_core(own)))
 
 
 def solution(mesh):

time: 121 us -> 116 us (0.959)
  waiting for transfers between devices: 14.2 us -> 11.7 us
  other arithmetic: 3.32 us -> 1.24 us
  starting transfers between devices: 38.2 us -> 36.2 us
  Pallas kernels: 62.8 us -> 64.1 us
    ppermute x4, waiting for transfers between devices: 9.98 us -> 4.62 us  [other_hid(): return lax.ppermute(array, 'hid', [(i, i ^ bit) for i in range(16)])]
    all_to_all x3, waiting for transfers between devices: 0.01 us -> 3.29 us  [exchange_inp(): lax.all_to_all(pieces, 'inp', 0, 0, tiled=True, axis_index_groups=ONE_CORE)]
    ppermute x7, starting transfers between devices: 12.5 us -> 10.2 us  [other_core(): return lax.ppermute(array, 'inp', [(i, i ^ 1) for i in range(16)])]
    mul x2 -> x0, other arithmetic: 1.39 us -> none  [shards(): return (input_grad, gate_sum * scale, up_sum * scale, down_sum * scale)]
    pallas_call x0 -> x2, Pallas kernels: none -> 1.32 us  [the longest x1 1.27 us: finish(): pl.pallas_call(finish_kernel, in_specs=[SCALAR] + [IN_VMEM] * 5, out_spec...]
  transfers between devices with their start and end apart: 14 -> 14, of which waited for: 7 -> 7; matrix products, arithmetic and copies ran while one was open for 1% -> 0% of each run, Pallas kernels for 40% -> 42%
where the time goes in v6:
time: 116 us; the launch traced here: 115 us
  Pallas kernels  64.1 us (55%)
  starting transfers between devices  36.2 us (31%)
  waiting for transfers between devices  11.7 us (10%)
  other arithmetic  1.24 us (1%)
    pallas_call x2, Pallas kernels, entry_sums(): pl.pallas_call(entry_sums_kernel, grid=(blocks,), in_specs=[pl.BlockSpec(...  22.7 us
    all_to_all x3, starting transfers between devices, exchange_inp(): lax.all_to_all(pieces, 'inp', 0, 0, tiled=True, axis_index_groups=ONE_CORE)  13.3 us
    ppermute x4, starting transfers between devices, other_hid(): return lax.ppermute(array, 'hid', [(i, i ^ bit) for i in range(16)])  12.7 us
    ppermute x7, starting transfers between devices, other_core(): return lax.ppermute(array, 'inp', [(i, i ^ 1) for i in range(16)])  10.2 us
    pallas_call x1, Pallas kernels, down_bins(): pl.pallas_call(kernel, in_specs=[IN_VMEM] * 2 + [IN_HBM] * (2 + count), o...  9.9 us
    pallas_call x1, Pallas kernels, forward_down(): pl.pallas_call(kernel, in_specs=[SCALAR] + [IN_HBM] * (3 + count), out_sp...  8.7 us
    pallas_call x2, Pallas kernels, forward_up(): pl.pallas_call(functools.partial(forward_up_kernel, first), in_specs=[SCA...  8.48 us
    pallas_call x2, Pallas kernels, table_sums(): pl.pallas_call(functools.partial(table_sums_kernel, part, pieces), in_spe...  7.33 us
  transfers between devices with their start and end apart: 14, of which 7 were waited for; matrix products, arithmetic and copies ran while one was open for 0% of the time, Pallas kernels for 42%

profile of v6, /device:TPU:1, one launch (start us, length us, event | category | flops | bytes accessed | tf_op | source)
XLA Modules:
  0.0 114.9 jit_solution(14888074644170142162)
XLA Ops:
  0.6 0.1 pad_add_fusion.refs_0_.place_ref
  0.7 8.7 %forward_down.1 = (f32[64,1664]{1,0:T(8,128)S(1)}, f32[64,1664]{1,0:T(8,128)S(1)}, bf16[128,1024]{1,0:T(8,128)(2,1)}, bf16[128,1024]{1,0:T(8,128)(2,1)S(1)}, s32...) custom-call(s32[2]{0:T(128)S(1)} %pad_add_fusion.refs_0_.place_ref, ...), custom_call_target="tpu_custom_call" | custom-call | bytes 15000000 | tf_op jit(solution)/shard_map/forward_down/pallas_call | solution.py:175
  9.4 3.3 %collective-permute-start.2 = (f32[64,1664]{1,0:T(8,128)S(1)}, f32[64,1664]{1,0:T(8,128)S(1)}, u32[]{:S(2)}, u32[]{:S(2)}) collective-permute-start(f32[64,1664]{1,0:T(8,128)S(1)} %get-tuple-element.51), channel_id=1, source_target_pairs={{0,16},{16,0},{32,48},{48,32},{64,80},{80,64},{96,112},{112,96},{1... | collective-permute-start | bytes 1277960 | tf_op jit(solution)/shard_map/ppermute | solution.py:525
  12.8 4.7 %forward_gate.1 = (f32[64,1664]{1,0:T(8,128)S(1)}, f32[64,1664]{1,0:T(8,128)S(1)}, bf16[1024,1664]{1,0:T(8,128)(2,1)}, bf16[128,1024]{1,0:T(8,128)(2,1)S(1)}, bf...) custom-call(s32[2]{0:T(128)S(1)} %pad_add_fusion.refs_0_.place_ref, bf16[128,1024]{1,0:T(8,128)(2,1)S(1)} %get-tuple-element.40.refs_1_, ...), custom_call_target="tpu_custom_call" | custom-call | bytes 15000000 | tf_op jit(solution)/shard_map/forward_gate/pallas_call | solution.py:230
  17.5 0.1 collective-permute-start
  17.6 3.8 %forward_up.1 = (f32[64,1664]{1,0:T(8,128)S(1)}, f32[64,1664]{1,0:T(8,128)S(1)}, bf16[1024,1664]{1,0:T(8,128)(2,1)}) custom-call(bf16[128,1024]{1,0:T(8,128)(2,1)S(1)} %get-tuple-element.45.refs_0_, s32[512,1664]{1,0:T(8,128)S(1)} %get-tuple-element.46.refs_1_, f32[16,1664]{1,0:T(8,128)S(1)} %get-tuple-element.47.refs_2_), custom_call_target="tpu_custom_call" | custom-call | bytes 15000000 | tf_op jit(solution)/shard_map/forward_up/pallas_call | solution.py:230
  21.4 0.6 collective-permute-start.1
  21.9 0.0 collective-permute-done.2
  22.0 0.0 collective-permute-done
  22.0 1.3 %collective-permute-done.1 = f32[64,1664]{1,0:T(8,128)S(1)} collective-permute-done((f32[64,1664]{1,0:T(8,128)S(1)}, f32[64,1664]{1,0:T(8,128)S(1)}, u32[]{:S(2)}, u32[]{:S(2)}) %collective-permute-start.1) | collective-permute-done | bytes 426016 | tf_op jit(solution)/shard_map/ppermute | solution.py:525
  23.4 0.9 maximum_bitcast_fusion.after_ref
  24.3 3.8 %all-to-all-start = ((bf16[8,8,4992]{2,1,0:T(8,128)(2,1)}), bf16[8,8,4992]{2,1,0:T(8,128)(2,1)S(1)}, u32[]{:S(2)}, u32[]{:S(2)}) async-start(bf16[8,8,4992]{2,1,0:T(8,128)(2,1)} %maximum_bitcast_fusion.after_ref), calls=%async_computation | async-start | bytes 1277952 | tf_op jit(solution)/shard_map/all_to_all | solution.py:529
  28.1 12.0 %entry_sums.2.refs_0_ = bf16[16,128,1792]{2,1,0:T(8,128)(2,1)} custom-call(bf16[128,1024]{1,0:T(8,128)(2,1)} %get-tuple-element.52.x_ref, s32[512,1664]{1,0:T(8,128)} %right_ref.2, s32[512,1664]{1,0:T(8,128)} %right_ref.2, s32[512,1664]{1,0:T(8,128)} %last_ref.3, bf16[8,8,4992]{2,1,0:T(8,128)(2,1)} %maximum_bitcast_fusion.after_ref), custom_call_target="tpu_custom_call" | custom-call | bytes 33000000 | tf_op jit(solution)/shard_map/entry_sums/pallas_call | solution.py:276
  40.1 0.0 all-to-all-done
  40.1 0.1 add_bitcast_fusion
  40.2 0.9 broadcast_in_dim.2.after_ref
  41.1 5.1 %all-to-all-start.1 = ((bf16[8,8,4992]{2,1,0:T(8,128)(2,1)}), bf16[8,8,4992]{2,1,0:T(8,128)(2,1)S(1)}, u32[]{:S(2)}, u32[]{:S(2)}) async-start(bf16[8,8,4992]{2,1,0:T(8,128)(2,1)} %broadcast_in_dim.2.after_ref), calls=%async_computation.1 | async-start | bytes 1277952 | tf_op jit(solution)/shard_map/all_to_all | solution.py:529
  46.2 10.7 %entry_sums.3.refs_1_ = bf16[16,128,1536]{2,1,0:T(8,128)(2,1)} custom-call(bf16[128,1024]{1,0:T(8,128)(2,1)} %get-tuple-element.52.x_ref, s32[512,1664]{1,0:T(8,128)} %last_ref.3, s32[512,1664]{1,0:T(8,128)} %last_ref.3, s32[512,1664]{1,0:T(8,128)} %last_ref.3, bf16[8,8,4992]{2,1,0:T(8,128)(2,1)} %broadcast_in_dim.2.after_ref), custom_call_target="tpu_custom_call" | custom-call | bytes 33000000 | tf_op jit(solution)/shard_map/entry_sums/pallas_call | solution.py:276
  56.9 0.0 all-to-all-done.1
  57.0 1.7 %collective-permute-start.3 = (bf16[64,3328]{1,0:T(8,128)(2,1)S(1)}, bf16[64,3328]{1,0:T(8,128)(2,1)S(1)}, u32[]{:S(2)}, u32[]{:S(2)}) collective-permute-start(bf16[64,3328]{1,0:T(8,128)(2,1)S(1)} %slice.23.near_ref), channel_id=1, source_target_pairs={{0,16},{16,0},{32,48},{48,32},{64,80},{80,64},{96,112},{112,96},{1... | collective-permute-start | bytes 1277960 | tf_op jit(solution)/shard_map/ppermute | solution.py:525
  58.6 0.1 collective-permute-start.4
  58.7 1.6 %collective-permute-done.4.refs_1_ = bf16[64,1664]{1,0:T(8,128)(2,1)S(1)} collective-permute-done((bf16[64,1664]{1,0:T(8,128)(2,1)S(1)}, bf16[64,1664]{1,0:T(8,128)(2,1)S(1)}, u32[]{:S(2)}, u32[]{:S(2)}) %collective-permute-start.4) | collective-permute-done | bytes 213024 | tf_op jit(solution)/shard_map/ppermute | solution.py:525
  60.3 9.9 %down_bins.1 = (f32[16,1024]{1,0:T(8,128)S(1)}, bf16[1024,1664]{1,0:T(8,128)(2,1)S(1)}, bf16[1024,1664]{1,0:T(8,128)(2,1)S(1)}) custom-call(bf16[64,1664]{1,0:T(8,128)(2,1)S(1)} %slice.24.refs_0_, bf16[64,1664]{1,0:T(8,128)(2,1)S(1)} %collective-permute-done.4.refs_1_, bf16[128,1024]{1,0:T(8,128)(2,1)} %get-tuple-element.55.refs_2_, s32[832,1024]{1,0:T(8,128)} %refs_3_.3, ...), custom_call_target="tpu_custom_call" | custom-call | bytes 30000000 | tf_op jit(solution)/shard_map/down_bins/pallas_call | solution.py:401
  70.2 0.0 collective-permute-done.3.far_ref
  70.2 4.2 %input_grad.1 = (f32[64,1024]{1,0:T(8,128)S(1)}, bf16[80,1024]{1,0:T(8,128)(2,1)S(1)}) custom-call(s32[2]{0:T(128)S(1)} %pad_add_fusion.refs_0_.place_ref, bf16[64,3328]{1,0:T(8,128)(2,1)S(1)} %slice.23.near_ref, bf16[64,3328]{1,0:T(8,128)(2,1)S(1)} %collective-permute-done.3.far_ref, bf16[1024,1664]{1,0:T(8,128)(2,1)S(1)} %get-tuple-element.58.wg_ref, ...), custom_call_target="tpu_custom_call" | custom-call | bytes 10500000 | tf_op jit(solution)/shard_map/input_grad/pallas_call | solution.py:442
  74.5 1.5 %collective-permute-start.5 = (bf16[80,1024]{1,0:T(8,128)(2,1)S(1)}, bf16[80,1024]{1,0:T(8,128)(2,1)S(1)}, u32[]{:S(2)}, u32[]{:S(2)}) collective-permute-start(bf16[80,1024]{1,0:T(8,128)(2,1)S(1)} %get-tuple-element.62.refs_1_), channel_id=1, source_target_pairs={{0,1},{1,0},{2,3},{3,2},{4,5},{5,4},{6,7},{7,6},{8,9},{9,8},{10,11... | collective-permute-start | bytes 491528 | tf_op jit(solution)/shard_map/ppermute | solution.py:577
  76.0 3.6 %table_sums.2.after_ref.gate_ref = f32[16,1664]{1,0:T(8,128)S(1)} custom-call(bf16[64,3328]{1,0:T(8,128)(2,1)S(1)} %slice.23.near_ref, bf16[64,3328]{1,0:T(8,128)(2,1)S(1)} %collective-permute-done.3.far_ref, bf16[16,128,1792]{2,1,0:T(8,128)(2,1)} %entry_sums.2.refs_0_, bf16[80,1024]{1,0:T(8,128)(2,1)S(1)} %get-tuple-element.62.refs_1_), custom_call_target="tpu_custom_call" | custom-call | bytes 13500000 | tf_op jit(solution)/shard_map/table_sums/pallas_call | solution.py:330
  79.6 0.6 collective-permute-done.5.back_ref
  80.2 3.1 %collective-permute-start.6 = (bf16[48,1024]{1,0:T(8,128)(2,1)S(1)}, bf16[48,1024]{1,0:T(8,128)(2,1)S(1)}, u32[]{:S(2)}, u32[]{:S(2)}) collective-permute-start(bf16[48,1024]{1,0:T(8,128)(2,1)S(1)} %get-tuple-element.66.refs_2_), channel_id=1, source_target_pairs={{0,4},{1,5},{2,6},{3,7},{4,0},{5,1},{6,2},{7,3},{8,12},{9,13},{10,... | collective-permute-start | bytes 294920 | tf_op jit(solution)/shard_map/ppermute | solution.py:577
  83.3 3.7 %table_sums.3.after_ref.up_ref = f32[16,1664]{1,0:T(8,128)S(1)} custom-call(bf16[64,3328]{1,0:T(8,128)(2,1)S(1)} %slice.23.near_ref, bf16[64,3328]{1,0:T(8,128)(2,1)S(1)} %collective-permute-done.3.far_ref, bf16[16,128,1792]{2,1,0:T(8,128)(2,1)} %entry_sums.2.refs_0_, bf16[16,128,1536]{2,1,0:T(8,128)(2,1)} %entry_sums.3.refs_1_, ...), custom_call_target="tpu_custom_call" | custom-call | bytes 13500000 | tf_op jit(solution)/shard_map/table_sums/pallas_call | solution.py:330
  87.0 0.0 collective-permute-done.6.back_ref
  87.0 0.6 choose.1
  87.6 2.2 %collective-permute-start.8 = (f32[16,1664]{1,0:T(8,128)S(1)}, f32[16,1664]{1,0:T(8,128)S(1)}, u32[]{:S(2)}, u32[]{:S(2)}) collective-permute-start(f32[16,1664]{1,0:T(8,128)S(1)} %get-tuple-element.71), channel_id=1, source_target_pairs={{0,16},{16,0},{32,48},{48,32},{64,80},{80,64},{96,112},{112,96},{1... | collective-permute-start | bytes 319496 | tf_op jit(solution)/shard_map/ppermute | solution.py:525
  89.8 5.4 %collective-permute-start.7 = (bf16[32,1024]{1,0:T(8,128)(2,1)S(1)}, bf16[32,1024]{1,0:T(8,128)(2,1)S(1)}, u32[]{:S(2)}, u32[]{:S(2)}) collective-permute-start(bf16[32,1024]{1,0:T(8,128)(2,1)S(1)} %get-tuple-element.70.after_ref), channel_id=1, source_target_pairs={{0,8},{1,9},{2,10},{3,11},{4,12},{5,13},{6,14},{7,15},{8,0},{9,1},... | collective-permute-start | bytes 196616 | tf_op jit(solution)/shard_map/ppermute | solution.py:577
  95.2 2.2 %collective-permute-done.7.back_ref = bf16[32,1024]{1,0:T(8,128)(2,1)S(1)} collective-permute-done((bf16[32,1024]{1,0:T(8,128)(2,1)S(1)}, bf16[32,1024]{1,0:T(8,128)(2,1)S(1)}, u32[]{:S(2)}, u32[]{:S(2)}) %collective-permute-start.7) | collective-permute-done | bytes 65568 | tf_op jit(solution)/shard_map/ppermute | solution.py:577
  97.4 0.0 collective-permute-done.8.after_ref.back_ref
  97.4 0.8 add_and_copy.1
  98.2 4.4 %all-to-all-start.2 = ((bf16[8,16,1664]{2,1,0:T(8,128)(2,1)}), bf16[8,16,1664]{2,1,0:T(8,128)(2,1)S(1)}, u32[]{:S(2)}, u32[]{:S(2)}) async-start(bf16[8,16,1664]{2,1,0:T(8,128)(2,1)} %add_and_copy.1), calls=%async_computation.2 | async-start | bytes 851968 | tf_op jit(solution)/shard_map/all_to_all | solution.py:529
  102.6 2.7 %collective-permute-start.9 = (bf16[32,1024]{1,0:T(8,128)(2,1)S(1)}, bf16[32,1024]{1,0:T(8,128)(2,1)S(1)}, u32[]{:S(2)}, u32[]{:S(2)}) collective-permute-start(bf16[32,1024]{1,0:T(8,128)(2,1)S(1)} %get-tuple-element.74.after_ref), channel_id=1, source_target_pairs={{0,2},{1,3},{2,0},{3,1},{4,6},{5,7},{6,4},{7,5},{8,10},{9,11},{10,... | collective-permute-start | bytes 196616 | tf_op jit(solution)/shard_map/ppermute | solution.py:577
  105.3 1.9 %collective-permute-done.9.after_ref.back_ref = bf16[32,1024]{1,0:T(8,128)(2,1)S(1)} collective-permute-done((bf16[32,1024]{1,0:T(8,128)(2,1)S(1)}, bf16[32,1024]{1,0:T(8,128)(2,1)S(1)}, u32[]{:S(2)}, u32[]{:S(2)}) %collective-permute-start.9) | collective-permute-done | bytes 65568 | tf_op jit(solution)/shard_map/ppermute | solution.py:577
  107.2 3.3 %all-to-all-done.2.pieces_ref = bf16[8,16,1664]{2,1,0:T(8,128)(2,1)S(1)} async-done(((bf16[8,16,1664]{2,1,0:T(8,128)(2,1)}), bf16[8,16,1664]{2,1,0:T(8,128)(2,1)S(1)}, u32[]{:S(2)}, u32[]{:S(2)}) %all-to-all-start.2) | async-done | bytes 426016 | tf_op jit(solution)/shard_map/all_to_all | solution.py:529
  110.5 0.1 add_places.1.own_ref
  110.6 2.2 %collective-permute-start.10 = (f32[16,1664]{1,0:T(8,128)S(1)}, f32[16,1664]{1,0:T(8,128)S(1)}, u32[]{:S(2)}, u32[]{:S(2)}) collective-permute-start(f32[16,1664]{1,0:T(8,128)S(1)} %add_places.1.own_ref), channel_id=1, source_target_pairs={{0,16},{16,0},{32,48},{48,32},{64,80},{80,64},{96,112},{112,96},{1... | collective-permute-start | bytes 319496 | tf_op jit(solution)/shard_map/ppermute | solution.py:525
  112.7 1.0 collective-permute-done.10.other_ref
  113.7 1.3 %finish.1 = (bf16[8,1024]{1,0:T(8,128)(2,1)}, f32[16,1664]{1,0:T(8,128)}, f32[16,1664]{1,0:T(8,128)}, f32[16,1024]{1,0:T(8,128)}) custom-call(s32[2]{0:T(128)S(1)} %pad_add_fusion.refs_0_.place_ref, f32[16,1024]{1,0:T(8,128)S(1)} %get-tuple-element.72.kept_ref, f32[16,1024]{1,0:T(8,128)S(1)} %get-tuple-element.73.bins_ref, ...), custom_call_target="tpu_custom_call" | custom-call | bytes 2100000 | tf_op jit(solution)/shard_map/finish/pallas_call | solution.py:510
  (10 shorter events, 0.3 us)
Async XLA Ops:
  9.4 12.5 %collective-permute-start.2 = (f32[64,1664]{1,0:T(8,128)S(1)}, f32[64,1664]{1,0:T(8,128)S(1)}, u32[]{:S(2)}, u32[]{:S(2)}) collective-permute-start(f32[64,1664]{1,0:T(8,128)S(1)} %get-tuple-element.51), channel_id=1, source_target_pairs={{0,16},{16,0},{32,48},{48,32},{64,80},{80,64},{96,112},{112,96},{1... | collective-permute-start | bytes 1277960 | tf_op jit(solution)/shard_map/ppermute | solution.py:525
  17.5 4.5 %collective-permute-start = (f32[64,1664]{1,0:T(8,128)S(1)}, f32[64,1664]{1,0:T(8,128)S(1)}, u32[]{:S(2)}, u32[]{:S(2)}) collective-permute-start(f32[64,1664]{1,0:T(8,128)S(1)} %get-tuple-element.44), channel_id=1, source_target_pairs={{0,16},{16,0},{32,48},{48,32},{64,80},{80,64},{96,112},{112,96},{1... | collective-permute-start | bytes 1277960 | tf_op jit(solution)/shard_map/ppermute | solution.py:525
  21.4 2.0 %collective-permute-start.1 = (f32[64,1664]{1,0:T(8,128)S(1)}, f32[64,1664]{1,0:T(8,128)S(1)}, u32[]{:S(2)}, u32[]{:S(2)}) collective-permute-start(f32[64,1664]{1,0:T(8,128)S(1)} %get-tuple-element.49), channel_id=1, source_target_pairs={{0,16},{16,0},{32,48},{48,32},{64,80},{80,64},{96,112},{112,96},{1... | collective-permute-start | bytes 1277960 | tf_op jit(solution)/shard_map/ppermute | solution.py:525
  24.3 15.8 %all-to-all-start = ((bf16[8,8,4992]{2,1,0:T(8,128)(2,1)}), bf16[8,8,4992]{2,1,0:T(8,128)(2,1)S(1)}, u32[]{:S(2)}, u32[]{:S(2)}) async-start(bf16[8,8,4992]{2,1,0:T(8,128)(2,1)} %maximum_bitcast_fusion.after_ref), calls=%async_computation | async-start | bytes 1277952 | tf_op jit(solution)/shard_map/all_to_all | solution.py:529
  41.1 15.8 %all-to-all-start.1 = ((bf16[8,8,4992]{2,1,0:T(8,128)(2,1)}), bf16[8,8,4992]{2,1,0:T(8,128)(2,1)S(1)}, u32[]{:S(2)}, u32[]{:S(2)}) async-start(bf16[8,8,4992]{2,1,0:T(8,128)(2,1)} %broadcast_in_dim.2.after_ref), calls=%async_computation.1 | async-start | bytes 1277952 | tf_op jit(solution)/shard_map/all_to_all | solution.py:529
  57.0 13.3 %collective-permute-start.3 = (bf16[64,3328]{1,0:T(8,128)(2,1)S(1)}, bf16[64,3328]{1,0:T(8,128)(2,1)S(1)}, u32[]{:S(2)}, u32[]{:S(2)}) collective-permute-start(bf16[64,3328]{1,0:T(8,128)(2,1)S(1)} %slice.23.near_ref), channel_id=1, source_target_pairs={{0,16},{16,0},{32,48},{48,32},{64,80},{80,64},{96,112},{112,96},{1... | collective-permute-start | bytes 1277960 | tf_op jit(solution)/shard_map/ppermute | solution.py:525
  58.6 1.7 %collective-permute-start.4 = (bf16[64,1664]{1,0:T(8,128)(2,1)S(1)}, bf16[64,1664]{1,0:T(8,128)(2,1)S(1)}, u32[]{:S(2)}, u32[]{:S(2)}) collective-permute-start(bf16[64,1664]{1,0:T(8,128)(2,1)S(1)} %slice.24.refs_0_), channel_id=1, source_target_pairs={{0,16},{16,0},{32,48},{48,32},{64,80},{80,64},{96,112},{112,96},{1... | collective-permute-start | bytes 638984 | tf_op jit(solution)/shard_map/ppermute | solution.py:525
  74.5 5.7 %collective-permute-start.5 = (bf16[80,1024]{1,0:T(8,128)(2,1)S(1)}, bf16[80,1024]{1,0:T(8,128)(2,1)S(1)}, u32[]{:S(2)}, u32[]{:S(2)}) collective-permute-start(bf16[80,1024]{1,0:T(8,128)(2,1)S(1)} %get-tuple-element.62.refs_1_), channel_id=1, source_target_pairs={{0,1},{1,0},{2,3},{3,2},{4,5},{5,4},{6,7},{7,6},{8,9},{9,8},{10,11... | collective-permute-start | bytes 491528 | tf_op jit(solution)/shard_map/ppermute | solution.py:577
  80.2 6.8 %collective-permute-start.6 = (bf16[48,1024]{1,0:T(8,128)(2,1)S(1)}, bf16[48,1024]{1,0:T(8,128)(2,1)S(1)}, u32[]{:S(2)}, u32[]{:S(2)}) collective-permute-start(bf16[48,1024]{1,0:T(8,128)(2,1)S(1)} %get-tuple-element.66.refs_2_), channel_id=1, source_target_pairs={{0,4},{1,5},{2,6},{3,7},{4,0},{5,1},{6,2},{7,3},{8,12},{9,13},{10,... | collective-permute-start | bytes 294920 | tf_op jit(solution)/shard_map/ppermute | solution.py:577
  87.6 9.8 %collective-permute-start.8 = (f32[16,1664]{1,0:T(8,128)S(1)}, f32[16,1664]{1,0:T(8,128)S(1)}, u32[]{:S(2)}, u32[]{:S(2)}) collective-permute-start(f32[16,1664]{1,0:T(8,128)S(1)} %get-tuple-element.71), channel_id=1, source_target_pairs={{0,16},{16,0},{32,48},{48,32},{64,80},{80,64},{96,112},{112,96},{1... | collective-permute-start | bytes 319496 | tf_op jit(solution)/shard_map/ppermute | solution.py:525
  89.8 7.6 %collective-permute-start.7 = (bf16[32,1024]{1,0:T(8,128)(2,1)S(1)}, bf16[32,1024]{1,0:T(8,128)(2,1)S(1)}, u32[]{:S(2)}, u32[]{:S(2)}) collective-permute-start(bf16[32,1024]{1,0:T(8,128)(2,1)S(1)} %get-tuple-element.70.after_ref), channel_id=1, source_target_pairs={{0,8},{1,9},{2,10},{3,11},{4,12},{5,13},{6,14},{7,15},{8,0},{9,1},... | collective-permute-start | bytes 196616 | tf_op jit(solution)/shard_map/ppermute | solution.py:577
  98.2 12.3 %all-to-all-start.2 = ((bf16[8,16,1664]{2,1,0:T(8,128)(2,1)}), bf16[8,16,1664]{2,1,0:T(8,128)(2,1)S(1)}, u32[]{:S(2)}, u32[]{:S(2)}) async-start(bf16[8,16,1664]{2,1,0:T(8,128)(2,1)} %add_and_copy.1), calls=%async_computation.2 | async-start | bytes 851968 | tf_op jit(solution)/shard_map/all_to_all | solution.py:529
  102.6 4.6 %collective-permute-start.9 = (bf16[32,1024]{1,0:T(8,128)(2,1)S(1)}, bf16[32,1024]{1,0:T(8,128)(2,1)S(1)}, u32[]{:S(2)}, u32[]{:S(2)}) collective-permute-start(bf16[32,1024]{1,0:T(8,128)(2,1)S(1)} %get-tuple-element.74.after_ref), channel_id=1, source_target_pairs={{0,2},{1,3},{2,0},{3,1},{4,6},{5,7},{6,4},{7,5},{8,10},{9,11},{10,... | collective-permute-start | bytes 196616 | tf_op jit(solution)/shard_map/ppermute | solution.py:577
  110.6 3.1 %collective-permute-start.10 = (f32[16,1664]{1,0:T(8,128)S(1)}, f32[16,1664]{1,0:T(8,128)S(1)}, u32[]{:S(2)}, u32[]{:S(2)}) collective-permute-start(f32[16,1664]{1,0:T(8,128)S(1)} %add_places.1.own_ref), channel_id=1, source_target_pairs={{0,16},{16,0},{32,48},{48,32},{64,80},{80,64},{96,112},{112,96},{1... | collective-permute-start | bytes 319496 | tf_op jit(solution)/shard_map/ppermute | solution.py:525
